TPU v7x, 256 devices: a whole 4x4x8 slice. The times are simulated.
256 devices in a mesh: angle: 8 (over y, x_hi), gz: 32 (over x_lo, z, core).
Axes of the slice: x: 4 (x_hi: 2, x_lo: 2; x = x_hi * 2 + x_lo), y: 4, z: 8, core: 2. Of those that a mesh axis runs over, the one named last changes fastest.
Arguments:
- volume: bfloat16 [32, 512, 512], P('gz'), may hold values from -0.3984375 to 0.3984375
- probe: float32 [8, 2, 128, 128], replicated, may hold values from -0.046875 to 0.046875
- measured: float32 [8, 32, 128, 128], P('angle', 'gz'), may hold values from 2 to 40
- angle_index: int32 [8], P('angle'), may hold values from 0 to 7, each once
- row_offset: int32 [8, 32], P('angle', 'gz'), may hold values from -64 to -32, as said below
- col_offset: int32 [8, 32], P('angle', 'gz'), may hold values from 0 to 384, as said below
Outputs:
- volume_update: float32 [32, 512, 512], P('gz', 'angle')
- probe_update: float32 [8, 2, 128, 128], replicated
Inputs may be any that keep to these rules, and one draw needn't show every extreme that they name: `row_offset`: windows may reach 64 rows past either end of the projection; both ends are used. `col_offset`: both ends are used. `angle_index`: each angle number once.
All inputs are finite; a program needn't handle non-finite values.
Results may differ from a plain program's by a relative error of at most 0.0005.
Values sent between devices are 32-bit elements; how exact they have to be, the bound alone decides.
No kernel may reach another device: no remote copies, remote signals or barrier semaphores. Data moves between devices by JAX's collectives and lax.ppermute only.
A program may use at most 64 MiB of HBM per device.

v0:
```python
import math

import jax
import jax.numpy as jnp
from jax import lax
from jax.sharding import PartitionSpec as P

precise = lax.Precision.HIGH


def twiddle_table(row_count, col_count, modulus, sign):
    rows_iota = jnp.arange(row_count, dtype=jnp.int32)[:, None]
    cols_iota = jnp.arange(col_count, dtype=jnp.int32)[None, :]
    product = rows_iota * cols_iota % modulus
    angles = sign * 2.0 * math.pi / modulus * product.astype(jnp.float32)
    return (jnp.cos(angles), jnp.sin(angles))


def signed_freq(count):
    index = jnp.arange(count, dtype=jnp.int32)
    return jnp.where(index < count // 2, index, index - count).astype(jnp.float32)


def axis_transform(real_in, imag_in, sign, real_only):
    depth, length, lanes = real_in.shape
    broad = min(length, 128)
    narrow = length // broad
    first_cos, first_sin = twiddle_table(broad, broad, broad, sign)
    turn_cos, turn_sin = twiddle_table(broad, narrow, length, sign)
    last_cos, last_sin = twiddle_table(narrow, narrow, narrow, sign)
    shaped_real = real_in.reshape(depth, broad, narrow, lanes)
    section_real = jnp.einsum("kn,znal->zkal", first_cos, shaped_real, precision=precise)
    section_imag = jnp.einsum("kn,znal->zkal", first_sin, shaped_real, precision=precise)
    if imag_in is not None:
        shaped_imag = imag_in.reshape(depth, broad, narrow, lanes)
        section_real = section_real - jnp.einsum(
            "kn,znal->zkal", first_sin, shaped_imag, precision=precise
        )
        section_imag = section_imag + jnp.einsum(
            "kn,znal->zkal", first_cos, shaped_imag, precision=precise
        )
    turn_c = turn_cos[None, :, :, None]
    turn_s = turn_sin[None, :, :, None]
    twist_real = section_real * turn_c - section_imag * turn_s
    twist_imag = section_real * turn_s + section_imag * turn_c
    out_real = jnp.einsum("ja,zkal->zjkl", last_cos, twist_real, precision=precise)
    out_real = out_real - jnp.einsum("ja,zkal->zjkl", last_sin, twist_imag, precision=precise)
    out_real = out_real.reshape(depth, length, lanes)
    if real_only:
        return (out_real, None)
    out_imag = jnp.einsum("ja,zkal->zjkl", last_sin, twist_real, precision=precise)
    out_imag = out_imag + jnp.einsum("ja,zkal->zjkl", last_cos, twist_imag, precision=precise)
    return (out_real, out_imag.reshape(depth, length, lanes))


def window_transform(real_in, imag_in, sign):
    window = real_in.shape[-1]
    table_cos, table_sin = twiddle_table(window, window, window, sign)
    rows_real = jnp.einsum("ij,pmjk->pmik", table_cos, real_in, precision=precise) - jnp.einsum(
        "ij,pmjk->pmik", table_sin, imag_in, precision=precise
    )
    rows_imag = jnp.einsum("ij,pmjk->pmik", table_sin, real_in, precision=precise) + jnp.einsum(
        "ij,pmjk->pmik", table_cos, imag_in, precision=precise
    )
    out_real = jnp.einsum("pmij,jk->pmik", rows_real, table_cos, precision=precise) - jnp.einsum(
        "pmij,jk->pmik", rows_imag, table_sin, precision=precise
    )
    out_imag = jnp.einsum("pmij,jk->pmik", rows_real, table_sin, precision=precise) + jnp.einsum(
        "pmij,jk->pmik", rows_imag, table_cos, precision=precise
    )
    return (out_real, out_imag)


def shear_tables(angle_value, width_x, width_y, angle_count):
    theta = math.pi * (angle_value + 0.5) / angle_count - math.pi / 2
    shear_x = -jnp.tan(theta / 2)
    shear_y = jnp.sin(theta)
    cells_y = jnp.arange(width_y, dtype=jnp.int32).astype(jnp.float32) - width_y / 2
    cells_x = jnp.arange(width_x, dtype=jnp.int32).astype(jnp.float32) - width_x / 2
    phase_one = (
        -2.0 * math.pi * signed_freq(width_x)[:, None] * shear_x * cells_y[None, :] / width_x
    )
    phase_two = (
        -2.0 * math.pi * signed_freq(width_y)[:, None] * shear_y * cells_x[None, :] / width_y
    )
    return (
        jnp.cos(phase_one)[None],
        jnp.sin(phase_one)[None],
        jnp.cos(phase_two)[None],
        jnp.sin(phase_two)[None],
    )


def adjoint_spectrum(slab_grad, tables, back_cos, back_sin):
    cos_one, sin_one, cos_two, sin_two = tables
    width_x = cos_one.shape[1]
    width_y = slab_grad.shape[-1]
    cbar_real = jnp.dot(slab_grad, back_cos, precision=precise) / width_y
    cbar_imag = -jnp.dot(slab_grad, back_sin, precision=precise) / width_y
    spread_real = cbar_real[:, :, None] * cos_two + cbar_imag[:, :, None] * sin_two
    spread_imag = cbar_imag[:, :, None] * cos_two - cbar_real[:, :, None] * sin_two
    columns_grad, unused = axis_transform(spread_real, spread_imag, 1.0, True)
    sheared_grad = jnp.swapaxes(columns_grad, 1, 2)
    grad_spec_real, grad_spec_imag = axis_transform(sheared_grad, None, -1.0, False)
    grad_spec_real = grad_spec_real / width_x
    grad_spec_imag = grad_spec_imag / width_x
    unturn_real = grad_spec_real * cos_one + grad_spec_imag * sin_one
    unturn_imag = grad_spec_imag * cos_one - grad_spec_real * sin_one
    return (unturn_real, unturn_imag)


def local(volume, probe, measured, angle_index, row_offset, col_offset):
    depth, width_x, width_y = volume.shape
    window = probe.shape[-1]
    rows_total = depth * lax.axis_size("gz")
    angle_count = lax.axis_size("angle")
    angle_value = angle_index.astype(jnp.float32)
    tables = shear_tables(angle_value[0], width_x, width_y, angle_count)
    cos_one, sin_one, cos_two, sin_two = tables
    field = volume.astype(jnp.float32)
    spec_real, spec_imag = axis_transform(field, None, -1.0, False)
    turned_real = spec_real * cos_one - spec_imag * sin_one
    turned_imag = spec_real * sin_one + spec_imag * cos_one
    sheared, unused = axis_transform(turned_real, turned_imag, 1.0, True)
    columns = jnp.swapaxes(sheared / width_x, 1, 2)
    beam_real, beam_imag = axis_transform(columns, None, -1.0, False)
    summed_real = jnp.sum(beam_real * cos_two - beam_imag * sin_two, axis=2)
    summed_imag = jnp.sum(beam_real * sin_two + beam_imag * cos_two, axis=2)
    back_cos, back_sin = twiddle_table(width_y, width_y, width_y, 1.0)
    projection = (
        jnp.dot(summed_real, back_cos, precision=precise)
        - jnp.dot(summed_imag, back_sin, precision=precise)
    ) / width_y
    whole = lax.all_gather(projection, "gz", axis=0, tiled=True)
    half = window // 2
    padded = jnp.pad(whole, ((half, half), (0, 0)))
    rows_here = row_offset[0]
    cols_here = col_offset[0]

    def cut_patch(row_start, col_start):
        return lax.dynamic_slice(padded, (row_start + half, col_start), (window, window))

    patches = jax.vmap(cut_patch)(rows_here, cols_here)
    measure = measured[0]
    object_real = jnp.cos(patches)[:, None]
    object_imag = jnp.sin(patches)[:, None]
    probe_real = probe[:, 0][None]
    probe_imag = probe[:, 1][None]
    exit_real = probe_real * object_real - probe_imag * object_imag
    exit_imag = probe_real * object_imag + probe_imag * object_real
    far_real, far_imag = window_transform(exit_real, exit_imag, -1.0)
    intensity = jnp.sum(far_real * far_real + far_imag * far_imag, axis=1)
    factor = ((1.0 - jnp.sqrt(measure + 1.0) / jnp.sqrt(intensity + 1.0)) / window)[:, None]
    back_real, back_imag = window_transform(factor * far_real, factor * far_imag, 1.0)
    probe_grad_real = jnp.sum(object_real * back_real + object_imag * back_imag, axis=0)
    probe_grad_imag = jnp.sum(object_real * back_imag - object_imag * back_real, axis=0)
    probe_grad = jnp.stack([probe_grad_real, probe_grad_imag], axis=1)
    object_grad_real = jnp.sum(probe_real * back_real + probe_imag * back_imag, axis=1)
    object_grad_imag = jnp.sum(probe_real * back_imag - probe_imag * back_real, axis=1)
    patch_grad = object_grad_imag * object_real[:, 0] - object_grad_real * object_imag[:, 0]
    buffer = jnp.zeros(padded.shape, jnp.float32)
    start_row = rows_here[0] + half
    start_col = cols_here[0]
    buffer = lax.dynamic_update_slice(buffer, patch_grad[0], (start_row, start_col))
    local_grad = buffer[half : half + rows_total]
    slab_grad = lax.psum_scatter(local_grad, "gz", scatter_dimension=0, tiled=True)
    probe_total = lax.psum(probe_grad, ("angle", "gz"))
    unturn_real, unturn_imag = adjoint_spectrum(slab_grad, tables, back_cos, back_sin)
    field_grad, unused = axis_transform(unturn_real, unturn_imag, 1.0, True)
    volume_part = lax.psum_scatter(field_grad, "angle", scatter_dimension=1, tiled=True)
    return (4.0 * volume_part, probe_total / 16.0)


def solution(mesh):
    return jax.shard_map(
        local,
        mesh=mesh,
        in_specs=(
            P("gz", None, None),
            P(),
            P("angle", "gz", None, None),
            P("angle"),
            P("angle", "gz"),
            P("angle", "gz"),
        ),
        out_specs=(P("gz", "angle", None), P()),
        check_vma=False,
    )
```

profile of v0, /device:TPU:1, one launch (start us, length us, event | category | flops | bytes accessed | tf_op | source)
XLA Modules:
  0.0 664.3 jit_solution(1285419459540519402)
XLA Ops:
  8.1 1.2 reshape.799
  10.0 0.9 add_bitcast_fusion.5
  10.9 1.5 fusion.50
  12.4 1.5 fusion.52
  14.0 1.6 fusion.17
  15.6 1.6 fusion.16
  18.6 5.4 fusion.119
  24.0 5.2 fusion.133
  29.2 5.7 fusion.14
  34.9 6.3 add_bitcast_fusion.4
  41.2 1.7 copy.275
  43.4 1.0 fusion.174
  44.4 1.2 fusion.13
  47.1 1.0 convolution_bitcast_fusion.4
  48.1 1.0 add_bitcast_fusion.3
  49.1 1.5 fusion.44
  50.6 1.5 fusion.46
  53.5 1.6 fusion.11
  55.1 11.3 %add_reduce_fusion = (f32[4,128]{0,1:T(8,128)S(1)}, f32[4,128]{0,1:T(8,128)S(1)}) fusion(f32[1,4,128,512]{3,1,2,0:T(4,128)S(1)} %fusion.11, f32[512]{0:T(512)S(1)} %convert_add_fusion, f32[4,128]{0,1:T(8,128)S(1)} %fusion.105, f32[128,512,4]{1,2,0:T(4,128)S(1)} %fusion.44, f32[128,4,512]{2,0,1:T(8,128)S(1)} %get-tuple-element.33), kind=kOutput, calls=%fused_computation.71 | convolution fusion | flops 9174240 | bytes 3153920 | tf_op jit(solution)/shard_map/ja,zkal->zjkl/dot_general | solution.py:52
  66.4 4.3 fusion.80
  70.9 4.3 fusion.76
  75.2 39.0 %all-gather.1 = f32[32,1,512]{2,1,0:T(1,128)S(1)} all-gather(f32[1,1,512]{2,1,0:T(1,128)S(1)} %bitcast.410), channel_id=2, replica_groups=mesh['angle'=8,'gz'=32] {'gz'}, dimensions={0}, use_global_device_ids=true | all-gather | bytes 67584 | tf_op jit(solution)/shard_map/all_gather | solution.py:134
  114.6 0.8 fusion.139
  115.4 0.8 fusion.149
  116.2 0.8 fusion.21
  118.5 0.8 fusion.20
  120.0 0.8 add_reduce_fusion.1
  120.9 0.8 fusion.92
  121.6 0.8 fusion.94
  122.4 0.8 fusion.19
  123.9 1.5 fusion.116
  125.4 0.8 fusion.18
  126.2 0.9 convolution_subtract_fusion.9
  127.2 0.9 add_bitcast_fusion.6
  128.2 1.7 dynamic_update_slice.3
  130.6 1.1 pad_maximum_fusion
  133.0 182.6 %all-reduce.7.cloned.1.call-done = f32[32,512]{1,0:T(8,128)} async-done(((f32[32,512]{1,0:T(8,128)}), f32[32,512]{1,0:T(8,128)}) %all-reduce.7.cloned.1.call-update) | async-done | bytes 65552
  315.6 5.6 fusion.74
  321.3 5.7 fusion.78
  327.4 5.2 fusion.34
  332.6 5.2 fusion.35
  337.8 5.5 fusion.8
  343.4 5.2 add_bitcast_fusion.2
  349.5 1.0 fusion.172
  350.6 1.3 fusion.7
  353.3 0.8 convolution_bitcast_fusion.2
  354.2 1.0 add_bitcast_fusion.1
  355.2 1.5 fusion.38
  356.7 1.5 fusion.40
  358.3 1.6 fusion.6
  359.9 1.7 fusion.4
  363.0 5.6 fusion.109
  368.6 5.2 fusion.123
  373.8 5.4 fusion.1
  379.3 6.3 add_bitcast_fusion
  385.5 1.7 copy.334
  387.8 1.0 fusion.170
  388.8 1.1 fusion
  389.9 1.3 copy.335
  391.2 185.8 %all-reduce.5.cloned.1.call-done = f32[8,2,128,128]{3,2,0,1:T(8,128)} async-done(((f32[8,2,128,128]{3,2,0,1:T(8,128)}), f32[8,2,128,128]{3,2,0,1:T(8,128)}) %all-reduce.5.cloned.1.call-update) | async-done | bytes 1048592 | tf_op jit(solution)/shard_map/psum | solution.py:167
  577.0 1.3 broadcast_multiply_fusion
  578.3 1.1 copy.336
  579.4 76.6 %reduce-scatter.2.cloned.1.call-done = f32[1,64,512]{2,1,0:T(8,128)} async-done(((f32[1,512,512]{2,1,0:T(8,128)}), f32[1,64,512]{2,1,0:T(8,128)}) %reduce-scatter.2.cloned.1.call-update) | async-done | bytes 131088 | tf_op jit(solution)/shard_map/reduce_scatter | solution.py:170
  656.0 1.6 broadcast_multiply_fusion.1
  (61 shorter events, 14.5 us)
Async XLA Ops:
  7.2 308.5 %all-reduce.7.cloned.1.call-start = ((), (), s32[]{:S(2)}) async-start(), calls=%async_computation.3 | async-start | bytes 131072
  70.8 43.8 %copy-start = (f32[8,2,128,128]{3,2,1,0:T(8,128)S(1)}, f32[8,2,128,128]{3,2,1,0:T(8,128)}, u32[]{:S(2)}) copy-start(f32[8,2,128,128]{3,2,1,0:T(8,128)} %param.7) | copy-start | bytes 3145732
  120.0 0.8 copy-start.2
  126.2 1.0 copy-start.1
  130.5 446.5 %all-reduce.5.cloned.1.call-start = ((), (), s32[]{:S(2)}) async-start(), calls=%async_computation.2 | async-start | bytes 2097152 | tf_op jit(solution)/shard_map/psum | solution.py:167
  131.7 524.3 %reduce-scatter.2.cloned.1.call-start = ((), (), s32[]{:S(2)}) async-start(), calls=%async_computation.1 | async-start | bytes 1179648 | tf_op jit(solution)/shard_map/reduce_scatter | solution.py:170
  131.8 0.7 copy-start.3
Sparse Core Ops, SparseCore 0:
  130.7 184.9 all-reduce.6
  322.0 254.9 all-reduce.4
  580.9 75.0 reduce-scatter.1
where the time goes:
time: 674 us; the launch traced here: 664 us
  waiting for transfers between devices  445 us (66%)
  matrix products  140 us (21%)
  blocking collectives  39 us (6%)
  local copies, waits for them, and re-layouts  19.1 us (3%)
  between operations  16.7 us (2%)
    psum x1, waiting for transfers between devices, local(): probe_total = lax.psum(probe_grad, ('angle', 'gz'))  186 us
    unnamed x4, waiting for transfers between devices  183 us
    reduce_scatter x1, waiting for transfers between devices, local(): lax.psum_scatter(field_grad, 'angle', scatter_dimension=1, tiled=True)  76.6 us
    all_gather x1, blocking collectives, local(): whole = lax.all_gather(projection, 'gz', axis=0, tiled=True)  39 us
    dot_general x6, matrix products, axis_transform(): jnp.einsum('kn,znal->zkal', first_sin, shaped_real, precision=precise)  18.8 us
    dot_general x6, matrix products, axis_transform(): jnp.einsum('kn,znal->zkal', first_cos, shaped_real, precision=precise)  18.7 us
    dot_general x3, matrix products, axis_transform(): jnp.einsum('kn,znal->zkal', first_sin, shaped_imag, precision=precise)  17.7 us
    dot_general x3, matrix products, axis_transform(): jnp.einsum('kn,znal->zkal', first_cos, shaped_imag, precision=precise)  16.6 us
  transfers between devices with their start and end apart: 3, of which 3 were waited for; matrix products, arithmetic and copies ran while one was open for 12% of the time, Pallas kernels for 0%

commit v1 on v0

v1 whole, which is shorter than its diff:
```python
import math

import jax
import jax.numpy as jnp
import numpy as np
from jax import lax
from jax.experimental import pallas as pl
from jax.experimental.pallas import tpu as pltpu
from jax.sharding import Mesh, PartitionSpec as P

N = 512
H = N // 2
W = 128
MODES = 8
ANGLES = 8
ROWS = 32
HALF = MODES * 2 * W // 2
CHUNK = HALF // 16
F32 = jnp.float32
BF16 = jnp.bfloat16


def split_const(table):
    high = table.astype(BF16)
    low = (table - high.astype(np.float64)).astype(BF16)
    return np.stack([high, low])


def dft_tables():
    k, n = np.arange(H)[:, None], np.arange(N)[None, :]
    turns = 2.0 * np.pi / N * (k * n % N)
    table = np.concatenate([np.cos(turns), -np.sin(turns)], 0)
    table[H] = 1.0 - 2.0 * (np.arange(N) % 2)
    return split_const(table), split_const(np.ascontiguousarray(table.T))


def window_tables():
    j = np.arange(W)
    turns = 2.0 * np.pi / W * (j[:, None] * j[None, :] % W)
    c, s = np.cos(turns), np.sin(turns)
    return split_const(np.block([[c, s], [-s, c]])), split_const(np.block([[c, -s], [s, c]]))


def shears():
    theta = np.pi * (np.arange(ANGLES) + 0.5) / ANGLES - np.pi / 2
    return -np.tan(theta / 2), np.sin(theta)


def cos_sin(phase):
    return np.stack([np.cos(phase), np.sin(phase)], 1)


def phase_tables():
    shear_x, shear_y = shears()
    cells = np.arange(N) - N / 2
    unit_one = -2.0 * np.pi / N * shear_x
    unit_two = -2.0 * np.pi / N * shear_y
    by_y = unit_one[:, None, None] * cells[None, None, :]
    coarse = cos_sin(by_y * (8 * np.arange(H // 8))[None, :, None]).astype(np.float32)
    fine = cos_sin(by_y * np.arange(8)[None, :, None]).astype(np.float32)
    nyquist = np.ones((ANGLES, 8, N))
    nyquist[:, 0] = 0.5 * np.cos(by_y[:, 0] * H)
    freq = np.arange(H, dtype=np.float64)
    freq[0] = H
    by_k = unit_one[:, None, None] * freq[None, None, :]
    rows_coarse = cos_sin(by_k * cells[::8][None, :, None]).astype(np.float32)
    rows_fine = cos_sin(by_k * np.arange(8)[None, :, None]).astype(np.float32)
    two = unit_two[:, None, None] * np.arange(H)[None, :, None] * cells[None, None, :]
    table = np.concatenate([np.cos(two), np.sin(two)], 1)
    table[:, H] = np.cos(unit_two[:, None] * H * cells[None, :])
    beams = np.moveaxis(split_const(table), 0, 1)
    return coarse, fine, nyquist.astype(np.float32), rows_coarse, rows_fine, np.ascontiguousarray(beams)


def mm(a, b):
    return lax.dot_general(a, b, (((1,), (0,)), ((), ())), preferred_element_type=F32)


def mm_t(a, b):
    return lax.dot_general(a, b, (((1,), (1,)), ((), ())), preferred_element_type=F32)


def split(value):
    high = value.astype(BF16)
    return high, (value - high.astype(F32)).astype(BF16)


def three(dot, a, b):
    return dot(a[0], b[0]) + (dot(a[0], b[1]) + dot(a[1], b[0]))


def forward_kernel(
    sc, volume, dft, dft_t, coarse, fine, nyquist, beams, out, spec, turned_hi, turned_lo, field_hi, field_lo
):
    block = volume[0]
    for part in range(2):
        lanes = pl.ds(part * H, H)
        spec[:, lanes] = mm(dft[0], block[:, part * H : (part + 1) * H]) + mm(
            dft[1], block[:, part * H : (part + 1) * H]
        )
    first = lax.broadcasted_iota(jnp.int32, (8, N), 0) == 0
    half_row = jnp.where(first, 0.5, 1.0)
    for pair in range(H // 16):
        reals, imags = [], []
        for u in (2 * pair, 2 * pair + 1):
            ca, sa = coarse[0, 0, u : u + 1, :], coarse[0, 1, u : u + 1, :]
            cb, sb = fine[0, 0], fine[0, 1]
            c, s = ca * cb - sa * sb, sa * cb + ca * sb
            a, b = spec[8 * u : 8 * u + 8, :], spec[H + 8 * u : H + 8 * u + 8, :]
            real, imag = a * c - b * s, a * s + b * c
            if u == 0:
                real, imag = real * half_row, imag * nyquist[0]
            reals.append(real)
            imags.append(imag)
        for base, parts in ((0, reals), (H, imags)):
            high, low = split(jnp.concatenate(parts, 0))
            turned_hi[base + 16 * pair : base + 16 * pair + 16, :] = high
            turned_lo[base + 16 * pair : base + 16 * pair + 16, :] = low
    for part in range(2):
        lanes = slice(part * H, (part + 1) * H)
        field = three(mm, (dft_t[0], dft_t[1]), (turned_hi[:, lanes], turned_lo[:, lanes]))
        high, low = split(field)
        field_hi[:, lanes] = high
        field_lo[:, lanes] = low
    spec[...] = three(mm_t, (dft[0], dft[1]), (field_hi[...], field_lo[...]))
    total = jnp.zeros((8, N), F32)
    for r in range(0, H, 32):
        a, b = spec[r : r + 32, :], spec[H + r : H + r + 32, :]
        c = beams[0, 0, r : r + 32, :].astype(F32) + beams[0, 1, r : r + 32, :].astype(F32)
        s = beams[0, 0, H + r : H + r + 32, :].astype(F32) + beams[0, 1, H + r : H + r + 32, :].astype(F32)
        c_low = c
        if r == 0:
            top = lax.broadcasted_iota(jnp.int32, (32, N), 0) == 0
            c_low, s = jnp.where(top, s, c), jnp.where(top, 0.0, s)
        real = jnp.sum(a * c - b * s, axis=1, keepdims=True)
        imag = jnp.sum(a * s + b * c_low, axis=1, keepdims=True)
        if r == 0:
            weight = jnp.where(lax.broadcasted_iota(jnp.int32, (32, 1), 0) == 0, 0.5, 1.0)
            real, imag = real * weight, imag * weight
        f_real = dft[0, r : r + 32, :].astype(F32) + dft[1, r : r + 32, :].astype(F32)
        f_imag = dft[0, H + r : H + r + 32, :].astype(F32) + dft[1, H + r : H + r + 32, :].astype(F32)
        terms = real * f_real + imag * f_imag
        total = total + jnp.sum(terms.reshape(4, 8, N), axis=0)
    row = jnp.sum(total, axis=0, keepdims=True) * (4.0 / (N * N))
    for t in range(4):
        out[pl.ds(t, ROWS, stride=4), :] = jnp.broadcast_to(row[:, t * W : (t + 1) * W], (ROWS, W))


def window_kernel(sc, whole, probe, measured, left, right, keep, send, exits, far, pieces):
    row, col, core = sc[0], sc[1], sc[2]
    rows = jnp.concatenate([whole[pl.ds(t, ROWS, stride=4), :] for t in range(4)], axis=1)
    band = pltpu.roll(rows, lax.rem(N - col, N), 1)[:, :W]
    pad = jnp.zeros((W - ROWS, W), F32)
    obj_real = pltpu.roll(jnp.concatenate([jnp.cos(band) - 1.0, pad], 0), -row, 0) + 1.0
    obj_imag = pltpu.roll(jnp.concatenate([jnp.sin(band), pad], 0), -row, 0)
    lefts, rights = (left[0], left[1]), (right[0], right[1])
    intensity = jnp.zeros((W, W), F32)
    for pair in range(MODES // 2):
        for m in (2 * pair, 2 * pair + 1):
            lanes = slice((m % 2) * W, (m % 2 + 1) * W)
            p_real, p_imag = probe[m, 0], probe[m, 1]
            exits[:W, lanes] = p_real * obj_real - p_imag * obj_imag
            exits[W:, lanes] = p_real * obj_imag + p_imag * obj_real
        first = three(mm, lefts, split(exits[...]))
        turned = jnp.concatenate(
            [
                jnp.concatenate([first[:W, :W], first[W:, :W]], 1),
                jnp.concatenate([first[:W, W:], first[W:, W:]], 1),
            ],
            0,
        )
        waves = three(mm, split(turned), rights)
        far[2 * W * pair : 2 * W * (pair + 1), :] = waves
        power = waves * waves
        power = power[:W] + power[W:]
        intensity = intensity + (power[:, :W] + power[:, W:])
    factor = (1.0 - jnp.sqrt(measured[0, 0] + 1.0) / jnp.sqrt(intensity + 1.0)) * (1.0 / W)
    factors = jnp.concatenate([jnp.concatenate([factor, factor], 1)] * 2, 0)
    grad_real, grad_imag = jnp.zeros((W, W), F32), jnp.zeros((W, W), F32)
    for pair in range(MODES // 2):
        scaled = far[2 * W * pair : 2 * W * (pair + 1), :] * factors
        first = three(mm, split(scaled), lefts)
        turned = jnp.concatenate(
            [
                jnp.concatenate([first[:W, :W], first[W:, :W]], 1),
                jnp.concatenate([first[:W, W:], first[W:, W:]], 1),
            ],
            0,
        )
        back = three(mm, rights, split(turned))
        for m in (2 * pair, 2 * pair + 1):
            lanes = slice((m % 2) * W, (m % 2 + 1) * W)
            b_real, b_imag = back[:W, lanes], back[W:, lanes]
            p_real, p_imag = probe[m, 0], probe[m, 1]
            grad_real = grad_real + (p_real * b_real + p_imag * b_imag)
            grad_imag = grad_imag + (p_real * b_imag - p_imag * b_real)
            exits[:W, lanes] = obj_real * b_real + obj_imag * b_imag
            exits[W:, lanes] = obj_real * b_imag - obj_imag * b_real

        def store(target, pair=pair):
            for m in (2 * pair, 2 * pair + 1):
                lanes = slice((m % 2) * W, (m % 2 + 1) * W)
                base = (m % 4) * 2 * W
                target[base : base + 2 * W, :] = exits[:, lanes]

        owner = 2 * pair // 4
        pl.when(core == owner)(lambda: store(keep))
        pl.when(core != owner)(lambda: store(send))
    patch = grad_imag * obj_real - grad_real * obj_imag
    shown = pltpu.roll(patch, W + row, 0)[:ROWS]
    wide = pltpu.roll(jnp.concatenate([shown, jnp.zeros((ROWS, N - W), F32)], 1), col, 1)
    for t in range(4):
        pieces[t] = wide[:, t * W : (t + 1) * W]
    for parity in range(2):

        def place(target, parity=parity):
            for t in range(4):
                target[HALF + 16 * t : HALF + 16 * (t + 1), :] = pieces[t, pl.ds(parity, 16, stride=2), :]

        pl.when(core == parity)(lambda: place(keep))
        pl.when(core != parity)(lambda: place(send))


def pack_kernel(sc, keep, other, out):
    angle = jnp.broadcast_to(sc[0].astype(F32), (8, W))
    for peer in range(16):
        rows = slice(CHUNK * peer, CHUNK * (peer + 1))
        out[peer, :CHUNK, :] = keep[rows, :] + other[rows, :]
        for t in range(4):
            base = HALF + 16 * t + 8 * (peer % 2)
            out[peer, CHUNK + 8 * t : CHUNK + 8 * t + 8, :] = keep[base : base + 8, :] + other[base : base + 8, :]
        out[peer, CHUNK + 32 :, :] = angle


def relay_kernel(received, out, pieces):
    total = received[0, :CHUNK, :]
    for peer in range(1, 16):
        total = total + received[peer, :CHUNK, :]
    for a in range(ANGLES):
        pieces[32 * a : 32 * a + 32, :] = (
            received[2 * a, CHUNK : CHUNK + 32, :] + received[2 * a + 1, CHUNK : CHUNK + 32, :]
        )
    for z in range(8):
        out[z, :CHUNK, :] = total
        out[z, CHUNK:, :] = pieces[pl.ds(z, 32, stride=8), :]


def adjoint_kernel(
    sc, received, dft_t, rows_coarse, rows_fine, beams, out, pieces, cbar, rows_dft, sheared_hi, sheared_lo, chunk
):
    step = pl.program_id(0)
    block = sc[ANGLES]
    lane_first = lax.broadcasted_iota(jnp.int32, (8, H), 1) == 0

    @pl.when(step == 0)
    def start():
        total = received[0]
        for z in range(1, 8):
            total = total + received[z]
        chunk[...] = total[:CHUNK] * (1.0 / 16.0)
        pieces[...] = total[CHUNK:]
        rows = jnp.concatenate([pieces[pl.ds(t, 8, stride=4), :] for t in range(4)], axis=1)
        spectrum = three(mm, split(rows), (dft_t[0], dft_t[1])) * (1.0 / N)
        weight = jnp.where(lax.broadcasted_iota(jnp.int32, (8, N), 1) % H == 0, 0.5, 1.0)
        cbar[...] = spectrum * weight
        at = pl.ds(pl.multiple_of(64 * block, 64), 64)
        rows_dft[...] = dft_t[0, at, :].astype(F32) + dft_t[1, at, :].astype(F32)

    mine = cbar[pl.ds(step, 1), :]
    c_real, c_imag = mine[:, :H], mine[:, H:]
    lane_zero = lax.broadcasted_iota(jnp.int32, (64, H), 1) == 0
    r_cos, r_sin = rows_dft[:, :H], rows_dft[:, H:]
    r_sin_real = jnp.where(lane_zero, 0.0, r_sin)
    r_cos_imag = jnp.where(lane_zero, r_sin, r_cos)
    shifted = jnp.concatenate([c_real * r_cos + c_imag * r_sin_real, c_imag * r_cos_imag - c_real * r_sin_real], 1)
    here = three(mm, split(shifted), (beams[0, 0], beams[0, 1]))
    high, low = split(here)
    at_rows = pl.ds(pl.multiple_of(64 * step, 64), 64)
    sheared_hi[at_rows, :] = high
    sheared_lo[at_rows, :] = low

    @pl.when(step == ANGLES - 1)
    def finish():
        spectrum = three(mm, (sheared_hi[...], sheared_lo[...]), (dft_t[0], dft_t[1]))
        sums = [None] * 8
        for a in range(ANGLES):
            number = sc[a]
            cb, sb = rows_fine[number, 0], rows_fine[number, 1]
            for u in range(8):
                ca, sa = rows_coarse[number, 0, u : u + 1, :], rows_coarse[number, 1, u : u + 1, :]
                c, s = ca * cb - sa * sb, sa * cb + ca * sb
                c_first, s_first = jnp.where(lane_first, 1.0, c), jnp.where(lane_first, 0.0, s)
                base = 64 * a + 8 * u
                real, imag = spectrum[base : base + 8, :H], spectrum[base : base + 8, H:]
                unturned = jnp.concatenate([real * c_first + imag * s_first, imag * c - real * s_first], 1)
                sums[u] = unturned if a == 0 else sums[u] + unturned
        weight = jnp.where(lax.broadcasted_iota(jnp.int32, (64, N), 1) % H == 0, 0.5 / 32.0, 1.0 / 32.0)
        whole = jnp.concatenate(sums, 0) * weight
        zeros = jnp.zeros((64, N), BF16)
        high, low = split(whole)
        result = None
        for side in range(2):
            dft_rows = [
                jnp.concatenate([dft_t[p, 64 * a + 32 * side : 64 * a + 32 * side + 32, :] for a in range(ANGLES)], 0)
                for p in range(2)
            ]
            order = (lambda v: [v, zeros]) if side == 0 else (lambda v: [zeros, v])
            columns = (jnp.concatenate(order(high), 0), jnp.concatenate(order(low), 0))
            part = three(mm_t, dft_rows, columns)
            result = part if result is None else result + part
        for peer in range(16):
            a = peer // 2
            out[peer, :CHUNK, :] = chunk[...]
            out[peer, CHUNK:, :] = result[32 * a : 32 * a + 32, :]


def assemble_kernel(sc, received, out):
    lower = lax.broadcasted_iota(jnp.int32, (32, W), 1) < 64
    for b in range(4):
        even = received[4 * b + sc[0], CHUNK:, :]
        odd = received[4 * b + 2 + sc[0], CHUNK:, :]
        lanes = slice(b * W, (b + 1) * W)
        out[0, :32, lanes] = jnp.where(lower, even, pltpu.roll(odd, 64, 1))
        out[0, 32:, lanes] = jnp.where(lower, pltpu.roll(even, 64, 1), odd)


params = dict(vmem_limit_bytes=48 * 1024 * 1024)


def full(shape):
    zeros = (0,) * len(shape)
    return pl.BlockSpec(shape, lambda *unused: zeros)


def by_angle(shape):
    return pl.BlockSpec((1,) + shape, lambda i, sc: (sc[0],) + (0,) * len(shape))


def forward_call(sc, volume, tables):
    dft, dft_t, coarse, fine, nyquist, beams = tables
    return pl.pallas_call(
        forward_kernel,
        grid_spec=pltpu.PrefetchScalarGridSpec(
            num_scalar_prefetch=1,
            grid=(1,),
            in_specs=[
                full((1, N, N)),
                full((2, N, N)),
                full((2, N, N)),
                by_angle((2, H // 8, N)),
                by_angle((2, 8, N)),
                by_angle((8, N)),
                by_angle((2, N, N)),
            ],
            out_specs=full((W, W)),
            scratch_shapes=[pltpu.VMEM((N, N), F32)] + [pltpu.VMEM((N, N), BF16)] * 4,
        ),
        out_shape=jax.ShapeDtypeStruct((4 * ROWS, W), F32),
        compiler_params=pltpu.CompilerParams(**params),
        name="forward",
    )(sc, volume, dft, dft_t, coarse, fine, nyquist, beams)


def vmem_call(kernel, out_shapes, scratch, name, *args):
    specs = [
        pl.BlockSpec(memory_space=pltpu.SMEM if a.dtype == jnp.int32 else pltpu.VMEM) for a in args
    ]
    single = not isinstance(out_shapes, list)
    shapes = [out_shapes] if single else out_shapes
    outs = pl.pallas_call(
        kernel,
        in_specs=specs,
        out_specs=[pl.BlockSpec(memory_space=pltpu.VMEM)] * len(shapes),
        out_shape=[jax.ShapeDtypeStruct(s, F32) for s in shapes],
        scratch_shapes=scratch,
        compiler_params=pltpu.CompilerParams(**params),
        name=name,
    )(*args)
    return outs[0] if single else outs


def adjoint_call(sc, received, dft_t, rows_coarse, rows_fine, beams):
    return pl.pallas_call(
        adjoint_kernel,
        grid_spec=pltpu.PrefetchScalarGridSpec(
            num_scalar_prefetch=1,
            grid=(ANGLES,),
            in_specs=[
                full((8, CHUNK + 32, W)),
                full((2, N, N)),
                pl.BlockSpec((ANGLES, 2, 8, H), lambda i, sc: (0, 0, sc[ANGLES], 0)),
                full((ANGLES, 2, 8, H)),
                pl.BlockSpec((1, 2, N, N), lambda i, sc: (sc[i], 0, 0, 0)),
            ],
            out_specs=full((16, CHUNK + 32, W)),
            scratch_shapes=[
                pltpu.VMEM((32, W), F32),
                pltpu.VMEM((8, N), F32),
                pltpu.VMEM((64, N), F32),
                pltpu.VMEM((N, N), BF16),
                pltpu.VMEM((N, N), BF16),
                pltpu.VMEM((CHUNK, W), F32),
            ],
        ),
        out_shape=jax.ShapeDtypeStruct((16, CHUNK + 32, W), F32),
        compiler_params=pltpu.CompilerParams(**params),
        name="adjoint",
    )(sc, received, dft_t, rows_coarse, rows_fine, beams)


GZ = ("xl", "z", "core")
PLANE = ("y", "xh", "xl")


def exchange(blocks, axes):
    return lax.all_to_all(blocks, axes, split_axis=0, concat_axis=0, tiled=True)


def swap(rows):
    return lax.ppermute(rows, "core", [(0, 1), (1, 0)])


def local(volume, probe, measured, angle_index, row_offset, col_offset):
    dft, dft_t = (jnp.asarray(t) for t in dft_tables())
    left, right = (jnp.asarray(t) for t in window_tables())
    coarse, fine, nyquist, rows_coarse, rows_fine, beams = (jnp.asarray(t) for t in phase_tables())
    core = lax.axis_index("core")
    block = 2 * lax.axis_index("y") + lax.axis_index("xh")
    row = forward_call(angle_index, volume, (dft, dft_t, coarse, fine, nyquist, beams))
    whole = exchange(row.reshape(ROWS, 4, W), GZ).reshape(4 * ROWS, W)
    places = jnp.stack([row_offset[0, 0], col_offset[0, 0], core.astype(jnp.int32)])
    keep, send = vmem_call(
        window_kernel,
        [(HALF + 64, W)] * 2,
        [pltpu.VMEM((2 * W, 2 * W), F32), pltpu.VMEM((MODES * W, 2 * W), F32), pltpu.VMEM((4, ROWS, W), F32)],
        "window",
        places,
        whole,
        probe,
        measured,
        left,
        right,
    )
    packed = vmem_call(pack_kernel, (16, CHUNK + 40, W), [], "pack", angle_index, keep, swap(send))
    shared = exchange(packed, PLANE)
    angles = shared.reshape(ANGLES, 2, CHUNK + 40, W)[:, 0, CHUNK + 32, 0].astype(jnp.int32)
    relay = vmem_call(relay_kernel, (8, CHUNK + 32, W), [pltpu.VMEM((256, W), F32)], "relay", shared)
    rows = exchange(relay, "z")
    numbers = jnp.concatenate([angles, jnp.stack([block.astype(jnp.int32)])])
    blocks = adjoint_call(numbers, rows, dft_t, rows_coarse, rows_fine, beams)
    final = exchange(blocks, PLANE)
    mine = final[:, :CHUNK, :].reshape(HALF, W)
    other = swap(mine)
    here = jnp.stack([lax.axis_index("xl").astype(jnp.int32)])
    volume_update = vmem_call(assemble_kernel, (1, 64, N), [], "assemble", here, final)
    probe_update = jnp.where(core == 0, jnp.stack([mine, other]), jnp.stack([other, mine]))
    return volume_update, probe_update.reshape(MODES, 2, W, W)


def solution(mesh):
    split_mesh = Mesh(mesh.devices.reshape(4, 2, 2, 8, 2), ("y", "xh", "xl", "z", "core"))
    angle, gz = ("y", "xh"), GZ
    return jax.shard_map(
        local,
        mesh=split_mesh,
        in_specs=(
            P(gz, None, None),
            P(),
            P(angle, gz, None, None),
            P(angle),
            P(angle, gz),
            P(angle, gz),
        ),
        out_specs=(P(gz, angle, None), P()),
        check_vma=False,
    )
```

time: 674 us -> 113 us (0.17); the launches traced: 664 us -> 113 us
  waiting for transfers between devices: 445 us -> 21.5 us
  matrix products: 140 us -> 0 us
  Pallas kernels: 0 us -> 22 us
  starting transfers between devices: 0.12 us -> 18.6 us
  between operations: 16.7 us -> 2.67 us
  local copies, waits for them, and re-layouts: 19.1 us -> 8.61 us
    psum x1 -> x0, waiting for transfers between devices: 186 us -> none  [local(): probe_total = lax.psum(probe_grad, ('angle', 'gz'))]
    unnamed x4 -> x0, waiting for transfers between devices: 183 us -> none
    dot_general x56 -> x0, matrix products: 140 us -> none  [the longest x6 18.8 us: axis_transform(): jnp.einsum('kn,znal->zkal', first_sin, shaped_real, precision=precise)]
    reduce_scatter x1 -> x0, waiting for transfers between devices: 76.6 us -> none  [local(): lax.psum_scatter(field_grad, 'angle', scatter_dimension=1, tiled=True)]
    all_gather x1 -> x0, blocking collectives: 39 us -> none  [local(): whole = lax.all_gather(projection, 'gz', axis=0, tiled=True)]
    all_to_all x0 -> x2, blocking collectives: none -> 38.1 us  [exchange(): return lax.all_to_all(blocks, axes, split_axis=0, concat_axis=0, tiled=True)]
    pallas_call x0 -> x6, Pallas kernels: none -> 22 us  [the longest x1 10.4 us: adjoint_call(): pl.pallas_call(adjoint_kernel, grid_spec=pltpu.PrefetchScalarGridSpec(num...]
    all_to_all x0 -> x2, waiting for transfers between devices: none -> 19.2 us  [exchange(): return lax.all_to_all(blocks, axes, split_axis=0, concat_axis=0, tiled=True)]
  transfers between devices with their start and end apart: 3 -> 4, of which waited for: 3 -> 4; matrix products, arithmetic and copies ran while one was open for 12% -> 0% of each run, Pallas kernels for 0% -> 1%
where the time goes in v1:
time: 113 us
  blocking collectives  38.1 us (34%)
  Pallas kernels  22 us (19%)
  waiting for transfers between devices  21.5 us (19%)
  starting transfers between devices  18.6 us (16%)
  local copies, waits for them, and re-layouts  8.61 us (8%)
  between operations  2.67 us (2%)
  other arithmetic  1.2 us (1%)
    all_to_all x2, blocking collectives, exchange(): return lax.all_to_all(blocks, axes, split_axis=0, concat_axis=0, tiled=True)  38.1 us
    all_to_all x2, waiting for transfers between devices, exchange(): return lax.all_to_all(blocks, axes, split_axis=0, concat_axis=0, tiled=True)  19.2 us
    all_to_all x2, starting transfers between devices, exchange(): return lax.all_to_all(blocks, axes, split_axis=0, concat_axis=0, tiled=True)  14.5 us
    pallas_call x1, Pallas kernels, adjoint_call(): pl.pallas_call(adjoint_kernel, grid_spec=pltpu.PrefetchScalarGridSpec(num...  10.4 us
    unnamed x27, local copies, waits for them, and re-layouts  8.57 us
    pallas_call x4, Pallas kernels, vmem_call(): pl.pallas_call(kernel, in_specs=specs, out_specs=[pl.BlockSpec(memory_spa...  6.8 us
    pallas_call x1, Pallas kernels, forward_call(): pl.pallas_call(forward_kernel, grid_spec=pltpu.PrefetchScalarGridSpec(num...  4.89 us
    ppermute x2, starting transfers between devices, swap(): return lax.ppermute(rows, 'core', [(0, 1), (1, 0)])  4.11 us
  transfers between devices with their start and end apart: 4, of which 4 were waited for; matrix products, arithmetic and copies ran while one was open for 0% of the time, Pallas kernels for 1%

profile of v1, /device:TPU:1, one launch (start us, length us, event | category | flops | bytes accessed | tf_op | source)
XLA Modules:
  0.0 112.8 jit_solution(17291439974742494494)
XLA Ops:
  1.3 0.0 copy-start
  1.3 1.2 %copy-done = bf16[2,512,512]{2,1,0:T(8,128)(2,1)S(1)} copy-done((bf16[2,512,512]{2,1,0:T(8,128)(2,1)S(1)}, bf16[2,512,512]{2,1,0:T(8,128)(2,1)}, u32[]{:S(2)}) %copy-start) | copy-done | bytes 1048600
  2.5 0.0 copy-start.3
  2.5 1.2 %copy-done.3 = f32[8,2,32,512]{3,2,1,0:T(8,128)S(1)} copy-done((f32[8,2,32,512]{3,2,1,0:T(8,128)S(1)}, f32[8,2,32,512]{3,2,1,0:T(8,128)}, u32[]{:S(2)}) %copy-start.3) | copy-done | bytes 1048600
  3.7 0.0 copy-start.4
  3.7 1.2 %copy-done.4 = bf16[2,512,512]{2,1,0:T(8,128)(2,1)S(1)} copy-done((bf16[2,512,512]{2,1,0:T(8,128)(2,1)S(1)}, bf16[2,512,512]{2,1,0:T(8,128)(2,1)}, u32[]{:S(2)}) %copy-start.4) | copy-done | bytes 1048600
  5.0 0.0 copy-start.6
  5.0 1.0 copy-done.6
  6.0 0.0 copy-start.9
  6.0 0.9 copy-done.9
  6.9 0.0 copy-start.11
  7.0 0.9 copy-done.11
  7.9 0.0 copy-start.5
  7.9 0.0 copy-start.12
  7.9 0.0 copy-start.1
  7.9 0.0 copy-start.2
  7.9 0.0 copy-start.10
  7.9 4.9 %forward.1 = f32[128,128]{1,0:T(8,128)} custom-call(s32[1]{0:T(128)S(6)} %copy.20.sc, bf16[1,512,512]{2,1,0:T(8,128)(2,1)S(1)} %copy-done.6, bf16[2,512,512]{2,1,0:T(8,128)(2,1)S(1)} %copy-done.4, bf16[2,512,512]{2,1,0:T(8,128)(2,1)S(1)} %copy-done, f32[8,2,32,512]{3,2,1,0:T(8,128)S(1)} %copy-done.3, f32[8,2,8,512]{3,2,1,0:T(8,128)S(1)} %copy-done.9, ...), custom_call_target="tpu_custom_call" | custom-call | tf_op jit(solution)/shard_map/forward/pallas_call | solution.py:341
  12.8 11.0 %all-to-all-start = ((f32[32,4,128]{2,1,0:T(4,128)}), f32[32,4,128]{2,1,0:T(4,128)S(1)}, u32[]{:S(2)}, u32[]{:S(2)}) async-start(f32[32,4,128]{2,1,0:T(4,128)} %bitcast.4), calls=%async_computation | async-start | bytes 131072 | tf_op jit(solution)/shard_map/all_to_all | solution.py:416
  25.1 0.1 pad_add_fusion.sc
  25.2 6.7 %all-to-all-done = f32[32,4,128]{2,1,0:T(4,128)S(1)} async-done(((f32[32,4,128]{2,1,0:T(4,128)}), f32[32,4,128]{2,1,0:T(4,128)S(1)}, u32[]{:S(2)}, u32[]{:S(2)}) %all-to-all-start) | async-done | bytes 65568 | tf_op jit(solution)/shard_map/all_to_all | solution.py:416
  31.9 0.0 copy-done.5
  31.9 0.0 copy-done.12
  31.9 0.0 copy-start.7
  31.9 0.9 copy-done.7
  32.9 0.0 copy-start.8
  32.9 0.9 copy-done.8
  33.8 5.2 %window.1 = (f32[1088,128]{1,0:T(8,128)S(1)}, f32[1088,128]{1,0:T(8,128)S(1)}) custom-call(s32[3]{0:T(128)S(1)} %pad_add_fusion.sc, f32[128,128]{1,0:T(8,128)S(1)} %bitcast.17, f32[8,2,128,128]{3,2,1,0:T(8,128)S(1)} %copy-done.5, f32[1,1,128,128]{3,2,1,0:T(8,128)S(1)} %copy-done.12, bf16[2,256,256]{2,1,0:T(8,128)(2,1)S(1)} %copy-done.8, ...), custom_call_target="tpu_custom_call" | custom-call | tf_op jit(solution)/shard_map/window/pallas_call | solution.py:370
  39.0 1.3 %collective-permute-start = (f32[1088,128]{1,0:T(8,128)S(1)}, f32[1088,128]{1,0:T(8,128)S(1)}, u32[]{:S(2)}, u32[]{:S(2)}) collective-permute-start(f32[1088,128]{1,0:T(8,128)S(1)} %get-tuple-element.5), channel_id=1, source_target_pairs={{0,1},{1,0},{2,3},{3,2},{4,5},{5,4},{6,7},{7,6},{8,9},{9,8},{10,11... | collective-permute-start | bytes 1671176 | tf_op jit(solution)/shard_map/ppermute | solution.py:420
  40.3 1.6 %collective-permute-done.other = f32[1088,128]{1,0:T(8,128)S(1)} collective-permute-done((f32[1088,128]{1,0:T(8,128)S(1)}, f32[1088,128]{1,0:T(8,128)S(1)}, u32[]{:S(2)}, u32[]{:S(2)}) %collective-permute-start) | collective-permute-done | bytes 557088 | tf_op jit(solution)/shard_map/ppermute | solution.py:420
  41.9 0.1 pack.1
  42.0 20.8 %all_to_all.20.received = f32[16,104,128]{2,1,0:T(8,128)S(1)} all-to-all(f32[16,104,128]{2,1,0:T(8,128)S(1)} %pack.1), channel_id=1, replica_groups=mesh['y'=4,'xh'=2,'xl'=2,'z'=8,'core'=2] {'y','xh','xl'}, dimensions={0} | all-to-all | bytes 1703936 | tf_op jit(solution)/shard_map/all_to_all | solution.py:416
  62.7 0.8 relay.1
  63.6 3.5 %all-to-all-start.2 = ((f32[8,96,128]{2,1,0:T(8,128)}), f32[8,96,128]{2,1,0:T(8,128)S(1)}, u32[]{:S(2)}, u32[]{:S(2)}) async-start(f32[8,96,128]{2,1,0:T(8,128)} %relay.1), calls=%async_computation.2 | async-start | bytes 786432 | tf_op jit(solution)/shard_map/all_to_all | solution.py:416
  67.0 0.1 copy.19
  67.1 0.1 pad_add_fusion.1.sc
  67.2 12.5 %all-to-all-done.2.received = f32[8,96,128]{2,1,0:T(8,128)S(1)} async-done(((f32[8,96,128]{2,1,0:T(8,128)}), f32[8,96,128]{2,1,0:T(8,128)S(1)}, u32[]{:S(2)}, u32[]{:S(2)}) %all-to-all-start.2) | async-done | bytes 393248 | tf_op jit(solution)/shard_map/all_to_all | solution.py:416
  79.7 0.0 copy-done.1
  79.7 0.0 copy-done.2
  79.7 0.0 copy-done.10
  79.7 10.4 %adjoint.1 = f32[16,96,128]{2,1,0:T(8,128)S(1)} custom-call(s32[9]{0:T(128)S(1)} %pad_add_fusion.1.sc, f32[8,96,128]{2,1,0:T(8,128)S(1)} %all-to-all-done.2.received, bf16[2,512,512]{2,1,0:T(8,128)(2,1)S(1)} %copy-done.1, f32[8,2,64,256]{3,2,1,0:T(8,128)S(1)} %copy-done.2, f32[8,2,8,256]{3,2,1,0:T(8,128)S(1)} %copy-done.10, ...), custom_call_target="tpu_custom_call" | custom-call | tf_op jit(solution)/shard_map/adjoint/pallas_call | solution.py:383
  90.1 17.3 %all_to_all.21.received = f32[16,96,128]{2,1,0:T(8,128)S(1)} all-to-all(f32[16,96,128]{2,1,0:T(8,128)S(1)} %adjoint.1), channel_id=1, replica_groups=mesh['y'=4,'xh'=2,'xl'=2,'z'=8,'core'=2] {'y','xh','xl'}, dimensions={0} | all-to-all | bytes 1572864 | tf_op jit(solution)/shard_map/all_to_all | solution.py:416
  107.4 2.8 %collective-permute-start.1 = (f32[1024,128]{1,0:T(8,128)S(1)}, f32[1024,128]{1,0:T(8,128)S(1)}, u32[]{:S(2)}, u32[]{:S(2)}) collective-permute-start(f32[1024,128]{1,0:T(8,128)S(1)} %bitcast.18), channel_id=1, source_target_pairs={{0,1},{1,0},{2,3},{3,2},{4,5},{5,4},{6,7},{7,6},{8,9},{9,8},{10,11... | collective-permute-start | bytes 1572872 | tf_op jit(solution)/shard_map/ppermute | solution.py:420
  110.2 0.8 assemble.1
  110.9 0.8 collective-permute-done.1
  111.7 1.0 maximum_select_fusion
  (3 shorter events, 0.0 us)
Async XLA Ops:
  1.3 1.2 %copy-start = (bf16[2,512,512]{2,1,0:T(8,128)(2,1)S(1)}, bf16[2,512,512]{2,1,0:T(8,128)(2,1)}, u32[]{:S(2)}) copy-start(bf16[2,512,512]{2,1,0:T(8,128)(2,1)} %constant.43.clone.dft_t) | copy-start | bytes 3145732
  2.5 1.2 %copy-start.3 = (f32[8,2,32,512]{3,2,1,0:T(8,128)S(1)}, f32[8,2,32,512]{3,2,1,0:T(8,128)}, u32[]{:S(2)}) copy-start(f32[8,2,32,512]{3,2,1,0:T(8,128)} %constant.46.clone.coarse) | copy-start | bytes 3145732
  3.7 1.2 %copy-start.4 = (bf16[2,512,512]{2,1,0:T(8,128)(2,1)S(1)}, bf16[2,512,512]{2,1,0:T(8,128)(2,1)}, u32[]{:S(2)}) copy-start(bf16[2,512,512]{2,1,0:T(8,128)(2,1)} %constant.42.clone.dft) | copy-start | bytes 3145732
  5.0 1.0 copy-start.6
  6.0 0.9 copy-start.9
  6.9 0.9 copy-start.11
  7.9 24.0 %copy-start.5 = (f32[8,2,128,128]{3,2,1,0:T(8,128)S(1)}, f32[8,2,128,128]{3,2,1,0:T(8,128)}, u32[]{:S(2)}) copy-start(f32[8,2,128,128]{3,2,1,0:T(8,128)} %probe.1) | copy-start | bytes 3145732
  7.9 24.0 %copy-start.12 = (f32[1,1,128,128]{3,2,1,0:T(8,128)S(1)}, f32[1,1,128,128]{3,2,1,0:T(8,128)}, u32[]{:S(2)}) copy-start(f32[1,1,128,128]{3,2,1,0:T(8,128)} %measured.1) | copy-start | bytes 196612
  7.9 71.8 %copy-start.1 = (bf16[2,512,512]{2,1,0:T(8,128)(2,1)S(1)}, bf16[2,512,512]{2,1,0:T(8,128)(2,1)}, u32[]{:S(2)}) copy-start(bf16[2,512,512]{2,1,0:T(8,128)(2,1)} %constant.43.clone.dft_t) | copy-start | bytes 3145732
  7.9 71.8 %copy-start.2 = (f32[8,2,64,256]{3,2,1,0:T(8,128)S(1)}, f32[8,2,64,256]{3,2,1,0:T(8,128)}, u32[]{:S(2)}) copy-start(f32[8,2,64,256]{3,2,1,0:T(8,128)} %constant.49.clone.rows_coarse) | copy-start | bytes 3145732
  7.9 71.8 %copy-start.10 = (f32[8,2,8,256]{3,2,1,0:T(8,128)S(1)}, f32[8,2,8,256]{3,2,1,0:T(8,128)}, u32[]{:S(2)}) copy-start(f32[8,2,8,256]{3,2,1,0:T(8,128)} %constant.50.clone.rows_fine) | copy-start | bytes 393220
  12.8 19.1 %all-to-all-start = ((f32[32,4,128]{2,1,0:T(4,128)}), f32[32,4,128]{2,1,0:T(4,128)S(1)}, u32[]{:S(2)}, u32[]{:S(2)}) async-start(f32[32,4,128]{2,1,0:T(4,128)} %bitcast.4), calls=%async_computation | async-start | bytes 131072 | tf_op jit(solution)/shard_map/all_to_all | solution.py:416
  31.9 1.0 copy-start.7
  32.9 0.9 copy-start.8
  39.0 2.9 %collective-permute-start = (f32[1088,128]{1,0:T(8,128)S(1)}, f32[1088,128]{1,0:T(8,128)S(1)}, u32[]{:S(2)}, u32[]{:S(2)}) collective-permute-start(f32[1088,128]{1,0:T(8,128)S(1)} %get-tuple-element.5), channel_id=1, source_target_pairs={{0,1},{1,0},{2,3},{3,2},{4,5},{5,4},{6,7},{7,6},{8,9},{9,8},{10,11... | collective-permute-start | bytes 1671176 | tf_op jit(solution)/shard_map/ppermute | solution.py:420
  63.6 16.1 %all-to-all-start.2 = ((f32[8,96,128]{2,1,0:T(8,128)}), f32[8,96,128]{2,1,0:T(8,128)S(1)}, u32[]{:S(2)}, u32[]{:S(2)}) async-start(f32[8,96,128]{2,1,0:T(8,128)} %relay.1), calls=%async_computation.2 | async-start | bytes 786432 | tf_op jit(solution)/shard_map/all_to_all | solution.py:416
  107.4 4.3 %collective-permute-start.1 = (f32[1024,128]{1,0:T(8,128)S(1)}, f32[1024,128]{1,0:T(8,128)S(1)}, u32[]{:S(2)}, u32[]{:S(2)}) collective-permute-start(f32[1024,128]{1,0:T(8,128)S(1)} %bitcast.18), channel_id=1, source_target_pairs={{0,1},{1,0},{2,3},{3,2},{4,5},{5,4},{6,7},{7,6},{8,9},{9,8},{10,11... | collective-permute-start | bytes 1572872 | tf_op jit(solution)/shard_map/ppermute | solution.py:420

commit v2 on v1

v2 whole, which is shorter than its diff:
```python
import math

import jax
import jax.numpy as jnp
import numpy as np
from jax import lax
from jax.experimental import pallas as pl
from jax.experimental.pallas import tpu as pltpu
from jax.sharding import Mesh, PartitionSpec as P

N = 512
H = N // 2
W = 128
MODES = 8
ANGLES = 8
PAIRS = ANGLES // 2
ROWS = 32
HALF = MODES * 2 * W // 2
CHUNK = HALF // 16
F32 = jnp.float32
BF16 = jnp.bfloat16


def split_const(table):
    high = table.astype(BF16)
    low = (table - high.astype(np.float64)).astype(BF16)
    return np.stack([high, low])


def dft_tables():
    k, n = np.arange(H)[:, None], np.arange(N)[None, :]
    turns = 2.0 * np.pi / N * (k * n % N)
    table = np.concatenate([np.cos(turns), -np.sin(turns)], 0)
    table[H] = 1.0 - 2.0 * (np.arange(N) % 2)
    return split_const(table), split_const(np.ascontiguousarray(table.T))


def window_tables():
    j = np.arange(W)
    turns = 2.0 * np.pi / W * (j[:, None] * j[None, :] % W)
    c, s = np.cos(turns), np.sin(turns)
    return np.stack([split_const(np.block([[c, s], [-s, c]])), split_const(np.block([[c, -s], [s, c]]))])


def shears():
    theta = np.pi * (np.arange(ANGLES) + 0.5) / ANGLES - np.pi / 2
    return -np.tan(theta / 2), np.sin(theta)


def cos_sin(phase):
    return np.stack([np.cos(phase), np.sin(phase)], 1)


def phase_tables():
    shear_x, shear_y = shears()
    cells = np.arange(N) - N / 2
    unit_one = -2.0 * np.pi / N * shear_x
    unit_two = -2.0 * np.pi / N * shear_y[:PAIRS]
    by_y = unit_one[:, None, None] * cells[None, None, :]
    nyquist = np.ones((ANGLES, 1, 8, N))
    nyquist[:, 0, 0] = 0.5 * np.cos(by_y[:, 0] * H)
    factors = np.concatenate(
        [
            cos_sin(by_y * (8 * np.arange(H // 8))[None, :, None]).reshape(ANGLES, H // 4, N),
            cos_sin(by_y * np.arange(8)[None, :, None]).reshape(ANGLES, 16, N),
            nyquist[:, 0],
        ],
        1,
    )
    freq = np.arange(H, dtype=np.float64)
    freq[0] = H
    by_k = unit_one[:PAIRS, None, None] * freq[None, None, :]
    rows_coarse = cos_sin(by_k * cells[::8][None, :, None])
    rows_fine = cos_sin(by_k * np.arange(8)[None, :, None])
    two = unit_two[:, None, None] * np.arange(H)[None, :, None] * cells[None, None, :]
    table = np.concatenate([np.cos(two), np.sin(two)], 1)
    table[:, H] = np.cos(unit_two[:, None] * H * cells[None, :])
    beams = np.ascontiguousarray(np.moveaxis(split_const(table), 0, 1))
    rows_tables = np.concatenate([rows_coarse, rows_fine], 2)
    return factors.astype(np.float32), rows_tables.astype(np.float32), beams


def mm(a, b):
    return lax.dot_general(a, b, (((1,), (0,)), ((), ())), preferred_element_type=F32)


def mm_t(a, b):
    return lax.dot_general(a, b, (((1,), (1,)), ((), ())), preferred_element_type=F32)


def split(value):
    high = value.astype(BF16)
    return high, (value - high.astype(F32)).astype(BF16)


def three(dot, a, b):
    return dot(a[0], b[0]) + (dot(a[0], b[1]) + dot(a[1], b[0]))


def forward_kernel(
    sc, volume, dft_hbm, dft_t_hbm, factors_hbm, beams_hbm, out,
    slab, dft, dft_t, factors, beams, spec, turned_hi, turned_lo, field_hi, field_lo, sems,
):
    number = sc[0]
    mirrored = number >= PAIRS
    sign = jnp.where(mirrored, -1.0, 1.0)
    moves = [
        pltpu.make_async_copy(volume.at[0], slab, sems.at[0]),
        pltpu.make_async_copy(dft_hbm, dft, sems.at[1]),
        pltpu.make_async_copy(factors_hbm.at[number], factors, sems.at[2]),
        pltpu.make_async_copy(dft_t_hbm, dft_t, sems.at[3]),
        pltpu.make_async_copy(
            beams_hbm.at[jnp.where(mirrored, ANGLES - 1 - number, number)], beams, sems.at[4]
        ),
    ]
    for move in moves:
        move.start()
    moves[0].wait()
    moves[1].wait()
    for part in range(2):
        lanes = slice(part * H, (part + 1) * H)
        spec[:, lanes] = mm(dft[0], slab[:, lanes]) + mm(dft[1], slab[:, lanes])
    moves[2].wait()
    first = lax.broadcasted_iota(jnp.int32, (8, N), 0) == 0
    half_row = jnp.where(first, 0.5, 1.0)
    for pair in range(H // 16):
        reals, imags = [], []
        for u in (2 * pair, 2 * pair + 1):
            ca, sa = factors[u : u + 1, :], factors[32 + u : 33 + u, :]
            cb, sb = factors[64:72, :], factors[72:80, :]
            c, s = ca * cb - sa * sb, sa * cb + ca * sb
            a, b = spec[8 * u : 8 * u + 8, :], spec[H + 8 * u : H + 8 * u + 8, :]
            real, imag = a * c - b * s, a * s + b * c
            if u == 0:
                real, imag = real * half_row, imag * factors[80:88, :]
            reals.append(real)
            imags.append(imag)
        for base, parts in ((0, reals), (H, imags)):
            high, low = split(jnp.concatenate(parts, 0))
            turned_hi[base + 16 * pair : base + 16 * pair + 16, :] = high
            turned_lo[base + 16 * pair : base + 16 * pair + 16, :] = low
    moves[3].wait()
    for part in range(2):
        lanes = slice(part * H, (part + 1) * H)
        field = three(mm, (dft_t[0], dft_t[1]), (turned_hi[:, lanes], turned_lo[:, lanes]))
        high, low = split(field)
        field_hi[:, lanes] = high
        field_lo[:, lanes] = low
    spec[...] = three(mm_t, (dft[0], dft[1]), (field_hi[...], field_lo[...]))
    moves[4].wait()
    total = jnp.zeros((8, N), F32)
    for r in range(0, H, 32):
        a, b = spec[r : r + 32, :], spec[H + r : H + r + 32, :]
        c = beams[0, r : r + 32, :].astype(F32) + beams[1, r : r + 32, :].astype(F32)
        s = beams[0, H + r : H + r + 32, :].astype(F32) + beams[1, H + r : H + r + 32, :].astype(F32)
        c_low = c
        if r == 0:
            top = lax.broadcasted_iota(jnp.int32, (32, N), 0) == 0
            c_low, s = jnp.where(top, s, c), jnp.where(top, 0.0, s)
        s = s * sign
        real = jnp.sum(a * c - b * s, axis=1, keepdims=True)
        imag = jnp.sum(a * s + b * c_low, axis=1, keepdims=True)
        if r == 0:
            weight = jnp.where(lax.broadcasted_iota(jnp.int32, (32, 1), 0) == 0, 0.5, 1.0)
            real, imag = real * weight, imag * weight
        f_real = dft[0, r : r + 32, :].astype(F32) + dft[1, r : r + 32, :].astype(F32)
        f_imag = dft[0, H + r : H + r + 32, :].astype(F32) + dft[1, H + r : H + r + 32, :].astype(F32)
        terms = real * f_real + imag * f_imag
        total = total + jnp.sum(terms.reshape(4, 8, N), axis=0)
    row = jnp.sum(total, axis=0, keepdims=True) * (4.0 / (N * N))
    for t in range(4):
        out[pl.ds(t, ROWS, stride=4), :] = jnp.broadcast_to(row[:, t * W : (t + 1) * W], (ROWS, W))


def window_kernel(row_ref, col_ref, whole, probe, measured, dfts, keep, send, exits, far, pieces):
    row, col, core = row_ref[0, 0], col_ref[0, 0], lax.axis_index("core")
    rows = jnp.concatenate([whole[pl.ds(t, ROWS, stride=4), :] for t in range(4)], axis=1)
    band = pltpu.roll(rows, lax.rem(N - col, N), 1)[:, :W]
    pad = jnp.zeros((W - ROWS, W), F32)
    obj_real = pltpu.roll(jnp.concatenate([jnp.cos(band) - 1.0, pad], 0), -row, 0) + 1.0
    obj_imag = pltpu.roll(jnp.concatenate([jnp.sin(band), pad], 0), -row, 0)
    lefts, rights = (dfts[0, 0], dfts[0, 1]), (dfts[1, 0], dfts[1, 1])
    intensity = jnp.zeros((W, W), F32)
    for pair in range(MODES // 2):
        for m in (2 * pair, 2 * pair + 1):
            lanes = slice((m % 2) * W, (m % 2 + 1) * W)
            p_real, p_imag = probe[m, 0], probe[m, 1]
            exits[pair, :W, lanes] = p_real * obj_real - p_imag * obj_imag
            exits[pair, W:, lanes] = p_real * obj_imag + p_imag * obj_real
        first = three(mm, lefts, split(exits[pair]))
        turned = jnp.concatenate(
            [
                jnp.concatenate([first[:W, :W], first[W:, :W]], 1),
                jnp.concatenate([first[:W, W:], first[W:, W:]], 1),
            ],
            0,
        )
        waves = three(mm, split(turned), rights)
        far[2 * W * pair : 2 * W * (pair + 1), :] = waves
        power = waves * waves
        power = power[:W] + power[W:]
        intensity = intensity + (power[:, :W] + power[:, W:])
    factor = (1.0 - jnp.sqrt(measured[0, 0] + 1.0) / jnp.sqrt(intensity + 1.0)) * (1.0 / W)
    factors = jnp.concatenate([jnp.concatenate([factor, factor], 1)] * 2, 0)
    grad_real, grad_imag = jnp.zeros((W, W), F32), jnp.zeros((W, W), F32)
    for pair in range(MODES // 2):
        scaled = far[2 * W * pair : 2 * W * (pair + 1), :] * factors
        first = three(mm, split(scaled), lefts)
        turned = jnp.concatenate(
            [
                jnp.concatenate([first[:W, :W], first[W:, :W]], 1),
                jnp.concatenate([first[:W, W:], first[W:, W:]], 1),
            ],
            0,
        )
        back = three(mm, rights, split(turned))
        for m in (2 * pair, 2 * pair + 1):
            lanes = slice((m % 2) * W, (m % 2 + 1) * W)
            b_real, b_imag = back[:W, lanes], back[W:, lanes]
            p_real, p_imag = probe[m, 0], probe[m, 1]
            grad_real = grad_real + (p_real * b_real + p_imag * b_imag)
            grad_imag = grad_imag + (p_real * b_imag - p_imag * b_real)
            exits[pair, :W, lanes] = obj_real * b_real + obj_imag * b_imag
            exits[pair, W:, lanes] = obj_real * b_imag - obj_imag * b_real

        def store(target, pair=pair):
            for m in (2 * pair, 2 * pair + 1):
                lanes = slice((m % 2) * W, (m % 2 + 1) * W)
                base = (m % 4) * 2 * W
                target[base : base + 2 * W, :] = exits[pair, :, lanes]

        owner = 2 * pair // 4
        pl.when(core == owner)(lambda: store(keep))
        pl.when(core != owner)(lambda: store(send))
    patch = grad_imag * obj_real - grad_real * obj_imag
    shown = pltpu.roll(patch, W + row, 0)[:ROWS]
    wide = pltpu.roll(jnp.concatenate([shown, jnp.zeros((ROWS, N - W), F32)], 1), col, 1)
    for t in range(4):
        pieces[t] = wide[:, t * W : (t + 1) * W]
    for parity in range(2):

        def place(target, parity=parity):
            for t in range(4):
                target[HALF + 16 * t : HALF + 16 * (t + 1), :] = pieces[t, pl.ds(parity, 16, stride=2), :]

        pl.when(core == parity)(lambda: place(keep))
        pl.when(core != parity)(lambda: place(send))


def pack_kernel(sc, keep, other, out):
    angle = jnp.broadcast_to(sc[0].astype(F32), (8, W))
    for peer in range(16):
        rows = slice(CHUNK * peer, CHUNK * (peer + 1))
        out[peer, :CHUNK, :] = keep[rows, :] + other[rows, :]
        for t in range(4):
            base = HALF + 16 * t + 8 * (peer % 2)
            out[peer, CHUNK + 8 * t : CHUNK + 8 * t + 8, :] = keep[base : base + 8, :] + other[base : base + 8, :]
        out[peer, CHUNK + 32 :, :] = angle


def relay_kernel(received, out, pieces):
    total = received[0, :CHUNK, :]
    for peer in range(1, 16):
        total = total + received[peer, :CHUNK, :]
    for a in range(ANGLES):
        number = jnp.max(received[2 * a, CHUNK + 32 :, :]).astype(jnp.int32)
        slot = jnp.where(number >= PAIRS, 2 * (ANGLES - 1 - number) + 1, 2 * number)
        pieces[pl.ds(pl.multiple_of(32 * slot, 32), 32), :] = (
            received[2 * a, CHUNK : CHUNK + 32, :] + received[2 * a + 1, CHUNK : CHUNK + 32, :]
        )
    for z in range(8):
        out[z, :CHUNK, :] = total
        out[z, CHUNK:, :] = pieces[pl.ds(z, 32, stride=8), :]


def adjoint_kernel(received, dft_t, rows_tables, *refs):
    beams, (out, pieces, shifted, sheared) = refs[:PAIRS], refs[PAIRS:]
    block = 2 * lax.axis_index("y") + lax.axis_index("xh")
    total = received[0]
    for z in range(1, 8):
        total = total + received[z]
    chunk = total[:CHUNK] * (1.0 / 16.0)
    pieces[...] = total[CHUNK:]
    rows = jnp.concatenate([pieces[pl.ds(t, 8, stride=4), :] for t in range(4)], axis=1)
    spectrum = three(mm, split(rows), (dft_t[0], dft_t[1]))
    weight = jnp.where(lax.broadcasted_iota(jnp.int32, (8, N), 1) % H == 0, 0.5 / N, 1.0 / N)
    cbar = spectrum * weight
    at = pl.ds(pl.multiple_of(64 * block, 64), 64)
    rows_dft = dft_t[0, at, :].astype(F32) + dft_t[1, at, :].astype(F32)
    lane_zero = lax.broadcasted_iota(jnp.int32, (64, H), 1) == 0
    r_cos, r_sin = rows_dft[:, :H], rows_dft[:, H:]
    r_sin_real = jnp.where(lane_zero, 0.0, r_sin)
    r_cos_imag = jnp.where(lane_zero, r_sin, r_cos)
    mirror = jnp.where(lane_zero, 1.0, -1.0)
    for slot in range(ANGLES):
        c_real, c_imag = cbar[slot : slot + 1, :H], cbar[slot : slot + 1, H:]
        cosines = c_real * r_cos + c_imag * r_sin_real
        sines = c_imag * r_cos_imag - c_real * r_sin_real
        if slot % 2:
            sines = sines * mirror
        high, low = split(jnp.concatenate([cosines, sines], 1))
        shifted[0, 64 * slot : 64 * slot + 64, :] = high
        shifted[1, 64 * slot : 64 * slot + 64, :] = low
    for q in range(PAIRS):
        at = slice(2 * 64 * q, 2 * 64 * (q + 1))
        here = three(mm, (shifted[0, at, :], shifted[1, at, :]), (beams[q][0], beams[q][1]))
        high, low = split(here)
        sheared[0, at, :] = high
        sheared[1, at, :] = low
    spectrum = three(mm, (sheared[0], sheared[1]), (dft_t[0], dft_t[1]))
    lane_first = lax.broadcasted_iota(jnp.int32, (8, H), 1) == 0
    sums = [None] * 8
    for q in range(PAIRS):
        cb, sb = rows_tables[q, 0, 64:72, :], rows_tables[q, 1, 64:72, :]
        near = rows_tables[q, :, pl.ds(pl.multiple_of(8 * block, 8), 8), :]
        for u in range(8):
            ca, sa = near[0, u : u + 1, :], near[1, u : u + 1, :]
            c, s = ca * cb - sa * sb, sa * cb + ca * sb
            c_first, s_first = jnp.where(lane_first, 1.0, c), jnp.where(lane_first, 0.0, s)
            base = 2 * 64 * q + 8 * u
            one, two = spectrum[base : base + 8, :], spectrum[base + 64 : base + 72, :]
            both, apart = one + two, one - two
            unturned = jnp.concatenate(
                [both[:, :H] * c_first + apart[:, H:] * s_first, both[:, H:] * c - apart[:, :H] * s_first], 1
            )
            sums[u] = unturned if q == 0 else sums[u] + unturned
    weight = jnp.where(lax.broadcasted_iota(jnp.int32, (64, N), 1) % H == 0, 0.5 / 32.0, 1.0 / 32.0)
    whole = jnp.concatenate(sums, 0) * weight
    zeros = jnp.zeros((64, N), BF16)
    high, low = split(whole)
    result = None
    for side in range(2):
        dft_rows = [
            jnp.concatenate([dft_t[p, 64 * a + 32 * side : 64 * a + 32 * side + 32, :] for a in range(ANGLES)], 0)
            for p in range(2)
        ]
        order = (lambda v: [v, zeros]) if side == 0 else (lambda v: [zeros, v])
        columns = (jnp.concatenate(order(high), 0), jnp.concatenate(order(low), 0))
        part = three(mm_t, dft_rows, columns)
        result = part if result is None else result + part
    for peer in range(16):
        a = peer // 2
        out[peer, :CHUNK, :] = chunk
        out[peer, CHUNK:, :] = result[32 * a : 32 * a + 32, :]


def assemble_kernel(received, out):
    xl = lax.axis_index("xl")
    lower = lax.broadcasted_iota(jnp.int32, (32, W), 1) < 64
    for b in range(4):
        even = received[4 * b + xl, CHUNK:, :]
        odd = received[4 * b + 2 + xl, CHUNK:, :]
        lanes = slice(b * W, (b + 1) * W)
        out[0, :32, lanes] = jnp.where(lower, even, pltpu.roll(odd, 64, 1))
        out[0, 32:, lanes] = jnp.where(lower, pltpu.roll(even, 64, 1), odd)


def forward_call(*args):
    return pl.pallas_call(
        forward_kernel,
        in_specs=[pl.BlockSpec(memory_space=pltpu.SMEM)] + [pl.BlockSpec(memory_space=pl.ANY)] * 5,
        out_specs=pl.BlockSpec(memory_space=pltpu.VMEM),
        out_shape=jax.ShapeDtypeStruct((4 * ROWS, W), F32),
        scratch_shapes=[
            pltpu.VMEM((N, N), BF16),
            pltpu.VMEM((2, N, N), BF16),
            pltpu.VMEM((2, N, N), BF16),
            pltpu.VMEM((H // 4 + 24, N), F32),
            pltpu.VMEM((2, N, N), BF16),
            pltpu.VMEM((N, N), F32),
        ]
        + [pltpu.VMEM((N, N), BF16)] * 4
        + [pltpu.SemaphoreType.DMA((5,))],
        compiler_params=pltpu.CompilerParams(vmem_limit_bytes=60 * 1024 * 1024),
        cost_estimate=pl.CostEstimate(flops=4 * 10**9, bytes_accessed=4 * 10**6, transcendentals=0),
        name="forward",
    )(*args)


def vmem_call(kernel, outs, scratch, name, *args):
    result = pl.pallas_call(
        kernel,
        in_specs=[
            pl.BlockSpec(memory_space=pltpu.SMEM if a.dtype == jnp.int32 else pltpu.VMEM) for a in args
        ],
        out_specs=[pl.BlockSpec(memory_space=pltpu.VMEM)] * len(outs),
        out_shape=[jax.ShapeDtypeStruct(o, F32) for o in outs],
        scratch_shapes=scratch,
        compiler_params=pltpu.CompilerParams(vmem_limit_bytes=32 * 1024 * 1024),
        cost_estimate=pl.CostEstimate(flops=3 * 10**9, bytes_accessed=4 * 10**6, transcendentals=0),
        name=name,
    )(*args)
    return result if len(outs) > 1 else result[0]


GZ = ("xl", "z", "core")
PLANE = ("y", "xh", "xl")


def exchange(blocks, axes):
    return lax.all_to_all(blocks, axes, split_axis=0, concat_axis=0, tiled=True)


def swap(rows):
    return lax.ppermute(rows, "core", [(0, 1), (1, 0)])


def local(volume, probe, measured, angle_index, row_offset, col_offset):
    dft, dft_t = (jnp.asarray(t) for t in dft_tables())
    dfts = jnp.asarray(window_tables())
    factors, rows_tables, all_beams = phase_tables()
    factors, rows_tables, all_beams = jnp.asarray(factors), jnp.asarray(rows_tables), jnp.asarray(all_beams)
    beams = [jnp.asarray(b) for b in np.asarray(phase_tables()[2])]
    row = forward_call(angle_index, volume, dft, dft_t, factors, all_beams)
    whole = exchange(row.reshape(ROWS, 4, W), GZ).reshape(4 * ROWS, W)
    keep, send = vmem_call(
        window_kernel,
        [(HALF + 64, W)] * 2,
        [
            pltpu.VMEM((MODES // 2, 2 * W, 2 * W), F32),
            pltpu.VMEM((MODES * W, 2 * W), F32),
            pltpu.VMEM((4, ROWS, W), F32),
        ],
        "window",
        row_offset,
        col_offset,
        whole,
        probe,
        measured,
        dfts,
    )
    packed = vmem_call(pack_kernel, [(16, CHUNK + 40, W)], [], "pack", angle_index, keep, swap(send))
    shared = exchange(packed, PLANE)
    relay = vmem_call(relay_kernel, [(8, CHUNK + 32, W)], [pltpu.VMEM((256, W), F32)], "relay", shared)
    rows = exchange(relay, "z")
    blocks = vmem_call(
        adjoint_kernel,
        [(16, CHUNK + 32, W)],
        [pltpu.VMEM((32, W), F32), pltpu.VMEM((2, N, N), BF16), pltpu.VMEM((2, N, N), BF16)],
        "adjoint",
        rows,
        dft_t,
        rows_tables,
        *beams,
    )
    final = exchange(blocks, PLANE)
    mine = final[:, :CHUNK, :].reshape(HALF, W)
    other = swap(mine)
    volume_update = vmem_call(assemble_kernel, [(1, 64, N)], [], "assemble", final)
    core = lax.axis_index("core")
    probe_update = jnp.where(core == 0, jnp.stack([mine, other]), jnp.stack([other, mine]))
    return volume_update, probe_update.reshape(MODES, 2, W, W)


def solution(mesh):
    split_mesh = Mesh(mesh.devices.reshape(4, 2, 2, 8, 2), ("y", "xh", "xl", "z", "core"))
    angle, gz = ("y", "xh"), GZ
    return jax.shard_map(
        local,
        mesh=split_mesh,
        in_specs=(
            P(gz, None, None),
            P(),
            P(angle, gz, None, None),
            P(angle),
            P(angle, gz),
            P(angle, gz),
        ),
        out_specs=(P(gz, angle, None), P()),
        check_vma=False,
    )
```

time: 113 us -> 95.8 us (0.85)
  blocking collectives: 38.1 us -> 52.3 us
  waiting for transfers between devices: 21.5 us -> 9.14 us
  local copies, waits for them, and re-layouts: 8.61 us -> 0.08 us
  Pallas kernels: 22 us -> 14.6 us
  starting transfers between devices: 18.6 us -> 15.7 us
    all_to_all x2 -> x3, blocking collectives: 38.1 us -> 52.3 us  [exchange(): return lax.all_to_all(blocks, axes, split_axis=0, concat_axis=0, tiled=True)]
    all_to_all x2 -> x1, waiting for transfers between devices: 19.2 us -> 6.78 us  [exchange(): return lax.all_to_all(blocks, axes, split_axis=0, concat_axis=0, tiled=True)]
    unnamed x27 -> x18, local copies, waits for them, and re-layouts: 8.57 us -> 0.04 us
    pallas_call x6, Pallas kernels: 22 us -> 14.6 us  [the longest x5 9.04 us: vmem_call(): pl.pallas_call(kernel, in_specs=[pl.BlockSpec(memory_space=pltpu.SMEM if...]
    all_to_all x2 -> x1, starting transfers between devices: 14.5 us -> 11.1 us  [exchange(): return lax.all_to_all(blocks, axes, split_axis=0, concat_axis=0, tiled=True)]
  transfers between devices with their start and end apart: 4 -> 3, of which waited for: 4 -> 3; matrix products, arithmetic and copies ran while one was open for 0% -> 0% of each run, Pallas kernels for 1% -> 1%
where the time goes in v2:
time: 95.8 us; the launch traced here: 95.5 us
  blocking collectives  52.3 us (55%)
  starting transfers between devices  15.7 us (16%)
  Pallas kernels  14.6 us (15%)
  waiting for transfers between devices  9.14 us (10%)
  between operations  2.69 us (3%)
  other arithmetic  1.04 us (1%)
    all_to_all x3, blocking collectives, exchange(): return lax.all_to_all(blocks, axes, split_axis=0, concat_axis=0, tiled=True)  52.3 us
    all_to_all x1, starting transfers between devices, exchange(): return lax.all_to_all(blocks, axes, split_axis=0, concat_axis=0, tiled=True)  11.1 us
    pallas_call x5, Pallas kernels, vmem_call(): pl.pallas_call(kernel, in_specs=[pl.BlockSpec(memory_space=pltpu.SMEM if...  9.04 us
    all_to_all x1, waiting for transfers between devices, exchange(): return lax.all_to_all(blocks, axes, split_axis=0, concat_axis=0, tiled=True)  6.78 us
    pallas_call x1, Pallas kernels, forward_call(): pl.pallas_call(forward_kernel, in_specs=[pl.BlockSpec(memory_space=pltpu....  5.54 us
    ppermute x2, starting transfers between devices, swap(): return lax.ppermute(rows, 'core', [(0, 1), (1, 0)])  4.63 us
    ppermute x2, waiting for transfers between devices, swap(): return lax.ppermute(rows, 'core', [(0, 1), (1, 0)])  2.36 us
  transfers between devices with their start and end apart: 3, of which 3 were waited for; matrix products, arithmetic and copies ran while one was open for 0% of the time, Pallas kernels for 1%

profile of v2, /device:TPU:1, one launch (start us, length us, event | category | flops | bytes accessed | tf_op | source)
XLA Modules:
  0.0 95.5 jit_solution(2129974349617564471)
XLA Ops:
  1.3 0.0 copy-start
  1.3 0.0 copy-start.1
  1.3 0.0 copy-start.8
  1.3 5.5 %forward.1 = f32[128,128]{1,0:T(8,128)} custom-call(s32[1]{0:T(128)S(6)} %copy.18.sc, bf16[1,512,512]{2,1,0:T(8,128)(2,1)} %volume.1, bf16[2,512,512]{2,1,0:T(8,128)(2,1)} %constant.26.clone.dft_hbm, bf16[2,512,512]{2,1,0:T(8,128)(2,1)} %constant.27.clone.dft_t_hbm.dft_t, f32[8,88,512]{2,1,0:T(8,128)} %constant.29.clone.factors_hbm, ...), custom_call_target="tpu_custom_call" | custom-call | flops 4000000000 | bytes 4000000 | tf_op jit(solution)/shard_map/forward/pallas_call | solution.py:359
  6.9 11.1 %all-to-all-start = ((f32[32,4,128]{2,1,0:T(4,128)}), f32[32,4,128]{2,1,0:T(4,128)S(1)}, u32[]{:S(2)}, u32[]{:S(2)}) async-start(f32[32,4,128]{2,1,0:T(4,128)} %bitcast.11), calls=%async_computation | async-start | bytes 131072 | tf_op jit(solution)/shard_map/all_to_all | solution.py:401
  19.2 6.8 %all-to-all-done = f32[32,4,128]{2,1,0:T(4,128)S(1)} async-done(((f32[32,4,128]{2,1,0:T(4,128)}), f32[32,4,128]{2,1,0:T(4,128)S(1)}, u32[]{:S(2)}, u32[]{:S(2)}) %all-to-all-start) | async-done | bytes 65568 | tf_op jit(solution)/shard_map/all_to_all | solution.py:401
  26.0 0.0 copy-done
  26.0 0.0 copy-done.1
  26.0 0.0 copy-done.8
  26.0 4.6 %window.1 = (f32[1088,128]{1,0:T(8,128)S(1)}, f32[1088,128]{1,0:T(8,128)S(1)}) custom-call(s32[1,1]{1,0:T(1,128)S(6)} %copy.19.row_ref, s32[1,1]{1,0:T(1,128)S(6)} %copy.20.col_ref, f32[128,128]{1,0:T(8,128)S(1)} %bitcast.6, f32[8,2,128,128]{3,2,1,0:T(8,128)S(1)} %copy-done, f32[1,1,128,128]{3,2,1,0:T(8,128)S(1)} %copy-done.1, ...), custom_call_target="tpu_custom_call" | custom-call | flops 3000000000 | bytes 4000000 | tf_op jit(solution)/shard_map/window/pallas_call | solution.py:381
  30.6 1.3 %collective-permute-start = (f32[1088,128]{1,0:T(8,128)S(1)}, f32[1088,128]{1,0:T(8,128)S(1)}, u32[]{:S(2)}, u32[]{:S(2)}) collective-permute-start(f32[1088,128]{1,0:T(8,128)S(1)} %get-tuple-element.5), channel_id=1, source_target_pairs={{0,1},{1,0},{2,3},{3,2},{4,5},{5,4},{6,7},{7,6},{8,9},{9,8},{10,11... | collective-permute-start | bytes 1671176 | tf_op jit(solution)/shard_map/ppermute | solution.py:405
  31.9 1.6 %collective-permute-done.other = f32[1088,128]{1,0:T(8,128)S(1)} collective-permute-done((f32[1088,128]{1,0:T(8,128)S(1)}, f32[1088,128]{1,0:T(8,128)S(1)}, u32[]{:S(2)}, u32[]{:S(2)}) %collective-permute-start) | collective-permute-done | bytes 557088 | tf_op jit(solution)/shard_map/ppermute | solution.py:405
  33.5 0.1 pack.1
  33.6 20.8 %all_to_all.20.received = f32[16,104,128]{2,1,0:T(8,128)S(1)} all-to-all(f32[16,104,128]{2,1,0:T(8,128)S(1)} %pack.1), channel_id=1, replica_groups=mesh['y'=4,'xh'=2,'xl'=2,'z'=8,'core'=2] {'y','xh','xl'}, dimensions={0} | all-to-all | bytes 1703936 | tf_op jit(solution)/shard_map/all_to_all | solution.py:401
  54.3 0.0 copy-start.2
  54.4 0.0 copy-start.3
  54.4 0.0 copy-start.4
  54.4 0.0 copy-start.5
  54.4 0.0 copy-start.6
  54.4 0.0 copy-start.7
  54.4 0.2 relay.1
  54.6 15.7 %all_to_all.21.received = f32[8,96,128]{2,1,0:T(8,128)S(1)} all-to-all(f32[8,96,128]{2,1,0:T(8,128)S(1)} %relay.1), channel_id=1, replica_groups=mesh['y'=4,'xh'=2,'xl'=2,'z'=8,'core'=2] {'z'}, dimensions={0} | all-to-all | bytes 786432 | tf_op jit(solution)/shard_map/all_to_all | solution.py:401
  70.3 0.0 copy-done.2
  70.3 0.0 copy-done.3
  70.3 0.0 copy-done.4
  70.3 0.0 copy-done.5
  70.3 0.0 copy-done.6
  70.3 0.0 copy-done.7
  70.3 3.5 %adjoint.1 = f32[16,96,128]{2,1,0:T(8,128)S(1)} custom-call(f32[8,96,128]{2,1,0:T(8,128)S(1)} %all_to_all.21.received, bf16[2,512,512]{2,1,0:T(8,128)(2,1)S(1)} %copy-done.2, f32[4,2,72,256]{3,2,1,0:T(8,128)S(1)} %copy-done.7, bf16[2,512,512]{2,1,0:T(8,128)(2,1)S(1)} %copy-done.6, bf16[2,512,512]{2,1,0:T(8,128)(2,1)S(1)} %copy-done.5, ...), custom_call_target="tpu_custom_call" | custom-call | flops 3000000000 | bytes 4000000 | tf_op jit(solution)/shard_map/adjoint/pallas_call | solution.py:381
  73.8 15.7 %all_to_all.22.received = f32[16,96,128]{2,1,0:T(8,128)S(1)} all-to-all(f32[16,96,128]{2,1,0:T(8,128)S(1)} %adjoint.1), channel_id=1, replica_groups=mesh['y'=4,'xh'=2,'xl'=2,'z'=8,'core'=2] {'y','xh','xl'}, dimensions={0} | all-to-all | bytes 1572864 | tf_op jit(solution)/shard_map/all_to_all | solution.py:401
  89.6 3.3 %collective-permute-start.1 = (f32[1024,128]{1,0:T(8,128)S(1)}, f32[1024,128]{1,0:T(8,128)S(1)}, u32[]{:S(2)}, u32[]{:S(2)}) collective-permute-start(f32[1024,128]{1,0:T(8,128)S(1)} %bitcast.7), channel_id=1, source_target_pairs={{0,1},{1,0},{2,3},{3,2},{4,5},{5,4},{6,7},{7,6},{8,9},{9,8},{10,11... | collective-permute-start | bytes 1572872 | tf_op jit(solution)/shard_map/ppermute | solution.py:405
  92.9 0.8 assemble.1
  93.7 0.8 collective-permute-done.1
  94.4 1.0 %maximum_select_fusion = f32[2,1024,128]{2,1,0:T(8,128)} fusion(f32[1,1024,128]{2,1,0:T(8,128)S(1)} %bitcast.10, f32[1,1024,128]{2,1,0:T(8,128)S(1)} %bitcast.8, pred[]{:T(512)S(6)} %eq.3), kind=kLoop, calls=%fused_computation | loop fusion | flops 786432 | bytes 2097153 | tf_op jit(solution)/shard_map/jit(_where)/select_n | solution.py:451
  (1 shorter events, 0.0 us)
Async XLA Ops:
  1.3 24.7 %copy-start = (f32[8,2,128,128]{3,2,1,0:T(8,128)S(1)}, f32[8,2,128,128]{3,2,1,0:T(8,128)}, u32[]{:S(2)}) copy-start(f32[8,2,128,128]{3,2,1,0:T(8,128)} %probe.1) | copy-start | bytes 3145732
  1.3 24.7 %copy-start.1 = (f32[1,1,128,128]{3,2,1,0:T(8,128)S(1)}, f32[1,1,128,128]{3,2,1,0:T(8,128)}, u32[]{:S(2)}) copy-start(f32[1,1,128,128]{3,2,1,0:T(8,128)} %measured.1) | copy-start | bytes 196612
  1.3 24.7 %copy-start.8 = (bf16[2,2,256,256]{3,2,1,0:T(8,128)(2,1)S(1)}, bf16[2,2,256,256]{3,2,1,0:T(8,128)(2,1)}, u32[]{:S(2)}) copy-start(bf16[2,2,256,256]{3,2,1,0:T(8,128)(2,1)} %constant.28.clone.dfts) | copy-start | bytes 1572868
  6.9 19.1 %all-to-all-start = ((f32[32,4,128]{2,1,0:T(4,128)}), f32[32,4,128]{2,1,0:T(4,128)S(1)}, u32[]{:S(2)}, u32[]{:S(2)}) async-start(f32[32,4,128]{2,1,0:T(4,128)} %bitcast.11), calls=%async_computation | async-start | bytes 131072 | tf_op jit(solution)/shard_map/all_to_all | solution.py:401
  30.6 2.9 %collective-permute-start = (f32[1088,128]{1,0:T(8,128)S(1)}, f32[1088,128]{1,0:T(8,128)S(1)}, u32[]{:S(2)}, u32[]{:S(2)}) collective-permute-start(f32[1088,128]{1,0:T(8,128)S(1)} %get-tuple-element.5), channel_id=1, source_target_pairs={{0,1},{1,0},{2,3},{3,2},{4,5},{5,4},{6,7},{7,6},{8,9},{9,8},{10,11... | collective-permute-start | bytes 1671176 | tf_op jit(solution)/shard_map/ppermute | solution.py:405
  54.3 16.0 %copy-start.2 = (bf16[2,512,512]{2,1,0:T(8,128)(2,1)S(1)}, bf16[2,512,512]{2,1,0:T(8,128)(2,1)}, u32[]{:S(2)}) copy-start(bf16[2,512,512]{2,1,0:T(8,128)(2,1)} %constant.27.clone.dft_t_hbm.dft_t) | copy-start | bytes 3145732
  54.4 16.0 %copy-start.3 = (bf16[2,512,512]{2,1,0:T(8,128)(2,1)S(1)}, bf16[2,512,512]{2,1,0:T(8,128)(2,1)}, u32[]{:S(2)}) copy-start(bf16[2,512,512]{2,1,0:T(8,128)(2,1)} %constant.35.clone.refs_3_) | copy-start | bytes 3145732
  54.4 16.0 %copy-start.4 = (bf16[2,512,512]{2,1,0:T(8,128)(2,1)S(1)}, bf16[2,512,512]{2,1,0:T(8,128)(2,1)}, u32[]{:S(2)}) copy-start(bf16[2,512,512]{2,1,0:T(8,128)(2,1)} %constant.34.clone.refs_2_) | copy-start | bytes 3145732
  54.4 16.0 %copy-start.5 = (bf16[2,512,512]{2,1,0:T(8,128)(2,1)S(1)}, bf16[2,512,512]{2,1,0:T(8,128)(2,1)}, u32[]{:S(2)}) copy-start(bf16[2,512,512]{2,1,0:T(8,128)(2,1)} %constant.33.clone.refs_1_) | copy-start | bytes 3145732
  54.4 16.0 %copy-start.6 = (bf16[2,512,512]{2,1,0:T(8,128)(2,1)S(1)}, bf16[2,512,512]{2,1,0:T(8,128)(2,1)}, u32[]{:S(2)}) copy-start(bf16[2,512,512]{2,1,0:T(8,128)(2,1)} %constant.32.clone.refs_0_) | copy-start | bytes 3145732
  54.4 16.0 %copy-start.7 = (f32[4,2,72,256]{3,2,1,0:T(8,128)S(1)}, f32[4,2,72,256]{3,2,1,0:T(8,128)}, u32[]{:S(2)}) copy-start(f32[4,2,72,256]{3,2,1,0:T(8,128)} %constant.30.clone.rows_tables) | copy-start | bytes 1769476
  89.6 4.8 %collective-permute-start.1 = (f32[1024,128]{1,0:T(8,128)S(1)}, f32[1024,128]{1,0:T(8,128)S(1)}, u32[]{:S(2)}, u32[]{:S(2)}) collective-permute-start(f32[1024,128]{1,0:T(8,128)S(1)} %bitcast.7), channel_id=1, source_target_pairs={{0,1},{1,0},{2,3},{3,2},{4,5},{5,4},{6,7},{7,6},{8,9},{9,8},{10,11... | collective-permute-start | bytes 1572872 | tf_op jit(solution)/shard_map/ppermute | solution.py:405

commit v3 on v2

v3 whole, which is shorter than its diff:
```python
import math

import jax
import jax.numpy as jnp
import numpy as np
from jax import lax
from jax.experimental import pallas as pl
from jax.experimental.pallas import tpu as pltpu
from jax.sharding import Mesh, PartitionSpec as P

N = 512
H = N // 2
W = 128
MODES = 8
ANGLES = 8
PAIRS = ANGLES // 2
ROWS = 32
HALF = MODES * 2 * W // 2
CHUNK = HALF // 16
F32 = jnp.float32
BF16 = jnp.bfloat16


def split_const(table):
    high = table.astype(BF16)
    low = (table - high.astype(np.float64)).astype(BF16)
    return np.stack([high, low])


def dft_tables():
    k, n = np.arange(H)[:, None], np.arange(N)[None, :]
    turns = np.pi / N * (k * (2 * n + 1) % (2 * N))
    table = np.concatenate([np.cos(turns), -np.sin(turns)], 0)
    table[H] = 2.0 * (np.arange(N) % 2) - 1.0
    return split_const(table), split_const(np.ascontiguousarray(table.T))


def window_tables():
    j = np.arange(W)
    turns = 2.0 * np.pi / W * (j[:, None] * j[None, :] % W)
    c, s = np.cos(turns), np.sin(turns)
    return np.stack([split_const(np.block([[c, s], [-s, c]])), split_const(np.block([[c, -s], [s, c]]))])


def shears():
    theta = np.pi * (np.arange(ANGLES) + 0.5) / ANGLES - np.pi / 2
    return -np.tan(theta / 2), np.sin(theta)


def cos_sin(phase):
    return np.stack([np.cos(phase), np.sin(phase)], 1)


def phase_tables():
    shear_x, shear_y = shears()
    cells = np.arange(N) - N / 2
    unit_one = -2.0 * np.pi / N * shear_x
    unit_two = -2.0 * np.pi / N * shear_y[:PAIRS]
    by_y = unit_one[:, None, None] * np.concatenate([cells[:H], cells[:H - 1:-1]])[None, None, :]
    nyquist = np.ones((ANGLES, 8, N))
    nyquist[:, 0] = 0.5 * np.cos(by_y[:, 0] * H)
    factors = np.concatenate(
        [
            cos_sin(by_y * (8 * np.arange(H // 8))[None, :, None]).reshape(ANGLES, H // 4, N),
            cos_sin(by_y * np.arange(8)[None, :, None]).reshape(ANGLES, 16, N),
            nyquist,
        ],
        1,
    )
    freq = np.arange(H, dtype=np.float64)
    freq[0] = H
    by_k = unit_one[:PAIRS, None, None] * freq[None, None, :]
    rows_coarse = cos_sin(by_k * cells[::8][None, :, None])
    rows_fine = cos_sin(by_k * np.arange(8)[None, :, None])
    rows_tables = np.concatenate([rows_coarse, rows_fine], 2)
    frequencies = np.arange(H, dtype=np.float64)
    turns = unit_two[:, None, None] * frequencies[None, :, None] * (H - 0.5 - np.arange(H))[None, None, :]
    low = np.cos(unit_two[:, None] * H * cells[None, :H])
    high = np.cos(unit_two[:, None] * H * cells[None, :H - 1:-1])
    table = np.concatenate([np.cos(turns), np.sin(turns)], 1)
    table[:, H] = 0.5 * (low - high)
    beams = np.ascontiguousarray(np.moveaxis(split_const(table), 0, 1))
    edges = np.zeros((PAIRS, 8, H))
    edges[:, 0] = 0.5 * (low + high)
    middle = 0.5 * unit_two[:, None] * frequencies[None, :]
    ordered = np.stack([middle, -middle], 1).reshape(ANGLES, H)
    middles = np.concatenate([np.cos(ordered), np.sin(ordered)], 0)
    return [t if t.dtype == BF16 else t.astype(np.float32) for t in (factors, rows_tables, beams, edges, middles)]


def mm(a, b):
    return lax.dot_general(a, b, (((1,), (0,)), ((), ())), preferred_element_type=F32)


def mm_t(a, b):
    return lax.dot_general(a, b, (((1,), (1,)), ((), ())), preferred_element_type=F32)


def split(value):
    high = value.astype(BF16)
    return high, (value - high.astype(F32)).astype(BF16)


def three(dot, a, b):
    return dot(a[0], b[0]) + (dot(a[0], b[1]) + dot(a[1], b[0]))


def forward_kernel(
    sc, volume, dft_hbm, dft_t_hbm, factors_hbm, beams_hbm, edges_hbm, out,
    slab, dft, dft_t, factors, beams, edges, spec, turned, field, sems,
):
    number = sc[0]
    mirrored = number >= PAIRS
    sign = jnp.where(mirrored, -1.0, 1.0)
    folded = jnp.where(mirrored, ANGLES - 1 - number, number)
    copies = [
        (volume.at[0], slab),
        (dft_hbm, dft),
        (factors_hbm.at[number], factors),
        (dft_t_hbm.at[:, pl.ds(0, H), :], dft_t),
        (beams_hbm.at[folded], beams),
        (edges_hbm.at[folded], edges),
    ]
    moves = [pltpu.make_async_copy(source, target, sems.at[i]) for i, (source, target) in enumerate(copies)]
    for move in moves:
        move.start()
    halves = (slice(0, H), slice(H, N))
    rows, lanes = (lax.broadcasted_iota(jnp.int32, (H, H), axis) for axis in (0, 1))
    reverse = jnp.where(rows + lanes == H - 1, 1.0, 0.0).astype(BF16)
    moves[0].wait()
    backward = mm(slab[:, H:], reverse).astype(BF16)
    moves[1].wait()
    for lanes, columns in zip(halves, (slab[:, :H], backward)):
        spec[:, lanes] = mm(dft[0], columns) + mm(dft[1], columns)
    moves[2].wait()
    half_row = jnp.where(lax.broadcasted_iota(jnp.int32, (8, H), 0) == 0, 0.5, 1.0)
    for lanes in halves:
        cb, sb = factors[64:72, lanes], factors[72:80, lanes]
        for pair in range(H // 16):
            reals, imags = [], []
            for u in (2 * pair, 2 * pair + 1):
                ca, sa = factors[u : u + 1, lanes], factors[32 + u : 33 + u, lanes]
                c, s = ca * cb - sa * sb, sa * cb + ca * sb
                a, b = spec[8 * u : 8 * u + 8, lanes], spec[H + 8 * u : H + 8 * u + 8, lanes]
                real, imag = a * c - b * s, a * s + b * c
                if u == 0:
                    real, imag = real * half_row, imag * factors[80:88, lanes]
                reals.append(real)
                imags.append(imag)
            for base, parts in ((16 * pair, reals), (H + 16 * pair, imags)):
                at = slice(base, base + 16)
                turned[0, at, lanes], turned[1, at, lanes] = split(jnp.concatenate(parts, 0))
    moves[3].wait()
    for part, comps in enumerate(halves):
        both = three(mm, (dft_t[0, :, comps], dft_t[1, :, comps]), (turned[0, comps, :], turned[1, comps, :]))
        field[0, 0, comps, :], field[0, 1, comps, :] = split(both[:, :H] + both[:, H:])
        field[1, 0, comps, :], field[1, 1, comps, :] = split(both[:, :H] - both[:, H:])
    for part, comps in enumerate(halves):
        spec[comps, :] = three(mm_t, (dft[0, comps, :H], dft[1, comps, :H]), (field[part, 0], field[part, 1]))
    moves[4].wait()
    moves[5].wait()
    total = jnp.zeros((8, N), F32)
    for r in range(0, H, 32):
        real_even, real_odd = spec[r : r + 32, :H], spec[r : r + 32, H:]
        imag_even, imag_odd = spec[H + r : H + r + 32, :H], spec[H + r : H + r + 32, H:]
        c = beams[0, r : r + 32, :].astype(F32) + beams[1, r : r + 32, :].astype(F32)
        s = beams[0, H + r : H + r + 32, :].astype(F32) + beams[1, H + r : H + r + 32, :].astype(F32)
        c_imag, s_imag, extra = c, s * sign, None
        if r == 0:
            top = lax.broadcasted_iota(jnp.int32, (32, H), 0) == 0
            extra = jnp.where(top, imag_odd * s, 0.0)
            c_imag = jnp.where(top, edges[0:1, :], c)
            s_imag = jnp.where(top, 0.0, s_imag)
        real_terms = real_even * c + imag_odd * s_imag
        imag_terms = imag_even * c_imag - real_odd * s_imag
        if extra is not None:
            imag_terms = imag_terms + extra
        real = jnp.sum(real_terms, axis=1, keepdims=True)
        imag = jnp.sum(imag_terms, axis=1, keepdims=True)
        if r == 0:
            weight = jnp.where(lax.broadcasted_iota(jnp.int32, (32, 1), 0) == 0, 0.5, 1.0)
            real, imag = real * weight, imag * weight
        c_mid, s_mid = c[:, H - 1 :], s_imag[:, H - 1 :]
        real, imag = real * c_mid + imag * s_mid, imag * c_mid - real * s_mid
        f_real = dft[0, r : r + 32, :].astype(F32) + dft[1, r : r + 32, :].astype(F32)
        f_imag = dft[0, H + r : H + r + 32, :].astype(F32) + dft[1, H + r : H + r + 32, :].astype(F32)
        terms = real * f_real + imag * f_imag
        total = total + jnp.sum(terms.reshape(4, 8, N), axis=0)
    row = jnp.sum(total, axis=0, keepdims=True) * (8.0 / (N * N))
    for t in range(4):
        out[pl.ds(t, ROWS, stride=4), :] = jnp.broadcast_to(row[:, t * W : (t + 1) * W], (ROWS, W))


def turn(block):
    return jnp.concatenate(
        [
            jnp.concatenate([block[:W, :W], block[W:, :W]], 1),
            jnp.concatenate([block[:W, W:], block[W:, W:]], 1),
        ],
        0,
    )


def window_kernel(row_ref, col_ref, whole, probe, measured, dfts, keep, send, stage, far, pieces):
    row, col, core = jnp.max(row_ref[...]), jnp.max(col_ref[...]), lax.axis_index("core")
    rows = jnp.concatenate([whole[pl.ds(t, ROWS, stride=4), :] for t in range(4)], axis=1)
    band = pltpu.roll(rows, lax.rem(N - col, N), 1)[:, :W]
    pad = jnp.zeros((W - ROWS, W), F32)
    obj_real = pltpu.roll(jnp.concatenate([jnp.cos(band) - 1.0, pad], 0), -row, 0) + 1.0
    obj_imag = pltpu.roll(jnp.concatenate([jnp.sin(band), pad], 0), -row, 0)
    lefts, rights = (dfts[0, 0], dfts[0, 1]), (dfts[1, 0], dfts[1, 1])
    pairs = [(j, j + MODES // 2) for j in range(MODES // 2)]
    sides = (slice(0, W), slice(W, 2 * W))

    def put(j, value):
        stage[0, j], stage[1, j] = split(value)

    def get(j):
        return stage[0, j], stage[1, j]

    for j, pair in enumerate(pairs):
        reals = [probe[m, 0] * obj_real - probe[m, 1] * obj_imag for m in pair]
        imags = [probe[m, 0] * obj_imag + probe[m, 1] * obj_real for m in pair]
        put(j, jnp.concatenate([jnp.concatenate(reals, 1), jnp.concatenate(imags, 1)], 0))
    for j in range(MODES // 2):
        put(j, turn(three(mm, lefts, get(j))))
    intensity = jnp.zeros((W, W), F32)
    for j in range(MODES // 2):
        waves = three(mm, get(j), rights)
        far[j] = waves
        power = waves * waves
        power = power[:W] + power[W:]
        intensity = intensity + (power[:, :W] + power[:, W:])
    factor = (1.0 - jnp.sqrt(measured[0, 0] + 1.0) / jnp.sqrt(intensity + 1.0)) * (1.0 / W)
    factors = jnp.concatenate([jnp.concatenate([factor, factor], 1)] * 2, 0)
    for j in range(MODES // 2):
        put(j, far[j] * factors)
    for j in range(MODES // 2):
        put(j, turn(three(mm, get(j), lefts)))
    grad_real, grad_imag = jnp.zeros((W, W), F32), jnp.zeros((W, W), F32)
    for j, pair in enumerate(pairs):
        back = three(mm, rights, get(j))
        grads = []
        for m, lanes in zip(pair, sides):
            b_real, b_imag = back[:W, lanes], back[W:, lanes]
            p_real, p_imag = probe[m, 0], probe[m, 1]
            grad_real = grad_real + (p_real * b_real + p_imag * b_imag)
            grad_imag = grad_imag + (p_real * b_imag - p_imag * b_real)
            grads.append((obj_real * b_real + obj_imag * b_imag, obj_real * b_imag - obj_imag * b_real))
        for part in range(2):
            at = slice((2 * j + part) * W, (2 * j + part + 1) * W)
            keep[at, :] = jnp.where(core == 0, grads[0][part], grads[1][part])
            send[at, :] = jnp.where(core == 0, grads[1][part], grads[0][part])
    patch = grad_imag * obj_real - grad_real * obj_imag
    shown = pltpu.roll(patch, W + row, 0)[:ROWS]
    wide = pltpu.roll(jnp.concatenate([shown, jnp.zeros((ROWS, N - W), F32)], 1), col, 1)
    for t in range(4):
        pieces[t] = wide[:, t * W : (t + 1) * W]
    for t in range(4):
        at = slice(HALF + 16 * t, HALF + 16 * (t + 1))
        even, odd = pieces[t, pl.ds(0, 16, stride=2), :], pieces[t, pl.ds(1, 16, stride=2), :]
        keep[at, :] = jnp.where(core == 0, even, odd)
        send[at, :] = jnp.where(core == 0, odd, even)


def pack_kernel(sc, keep, other, out):
    angle = jnp.broadcast_to(sc[0].astype(F32), (8, W))
    for peer in range(16):
        rows = slice(CHUNK * peer, CHUNK * (peer + 1))
        out[peer, :CHUNK, :] = keep[rows, :] + other[rows, :]
        for t in range(4):
            base = HALF + 16 * t + 8 * (peer % 2)
            out[peer, CHUNK + 8 * t : CHUNK + 8 * t + 8, :] = keep[base : base + 8, :] + other[base : base + 8, :]
        out[peer, CHUNK + 32 :, :] = angle


def relay_kernel(received, out, pieces):
    total = received[0, :CHUNK, :]
    for peer in range(1, 16):
        total = total + received[peer, :CHUNK, :]
    for a in range(ANGLES):
        number = jnp.max(received[2 * a, CHUNK + 32 :, :]).astype(jnp.int32)
        slot = jnp.where(number >= PAIRS, 2 * (ANGLES - 1 - number) + 1, 2 * number)
        pieces[pl.ds(pl.multiple_of(32 * slot, 32), 32), :] = (
            received[2 * a, CHUNK : CHUNK + 32, :] + received[2 * a + 1, CHUNK : CHUNK + 32, :]
        )
    for z in range(8):
        out[z, :CHUNK, :] = total
        out[z, CHUNK:, :] = pieces[pl.ds(z, 32, stride=8), :]


def adjoint_kernel(received, dft_t, rows_tables, edges, middles, *refs):
    beams, (out, pieces, shifted, sheared) = refs[:PAIRS], refs[PAIRS:]
    block = 2 * lax.axis_index("y") + lax.axis_index("xh")
    total = received[0]
    for z in range(1, 8):
        total = total + received[z]
    chunk = total[:CHUNK] * (1.0 / 16.0)
    pieces[...] = total[CHUNK:]
    rows = jnp.concatenate([pieces[pl.ds(t, 8, stride=4), :] for t in range(4)], axis=1)
    spectrum = three(mm, split(rows), (dft_t[0], dft_t[1]))
    weight = jnp.where(lax.broadcasted_iota(jnp.int32, (8, N), 1) % H == 0, 0.5 / N, 1.0 / N)
    cbar = spectrum * weight
    c_mid, s_mid = middles[:ANGLES, :], middles[ANGLES:, :]
    c_reals = cbar[:, :H] * c_mid - cbar[:, H:] * s_mid
    c_imags = cbar[:, H:] * c_mid + cbar[:, :H] * s_mid
    at = pl.ds(pl.multiple_of(64 * block, 64), 64)
    rows_dft = dft_t[0, at, :].astype(F32) + dft_t[1, at, :].astype(F32)
    lane_zero = lax.broadcasted_iota(jnp.int32, (64, H), 1) == 0
    r_cos, r_sin = rows_dft[:, :H], rows_dft[:, H:]
    r_sin_real = jnp.where(lane_zero, 0.0, r_sin)
    r_cos_imag = jnp.where(lane_zero, r_sin, r_cos)
    mirror = jnp.where(lane_zero, 1.0, -1.0)
    nyquist = []
    for slot in range(ANGLES):
        c_real, c_imag = c_reals[slot : slot + 1, :], c_imags[slot : slot + 1, :]
        cosines = c_real * r_cos + c_imag * r_sin_real
        sines = c_imag * r_cos_imag - c_real * r_sin_real
        if slot % 2 == 0:
            sines = sines * mirror
        nyquist.append(sines[:, :1])
        at = slice(64 * slot, 64 * slot + 64)
        shifted[0, at, :H], shifted[1, at, :H] = split(cosines)
        shifted[0, at, H:], shifted[1, at, H:] = split(sines)
    for q in range(PAIRS):
        at = slice(2 * 64 * q, 2 * 64 * (q + 1))
        even = three(mm, (shifted[0, at, :H], shifted[1, at, :H]), (beams[q][0, :H, :], beams[q][1, :H, :]))
        odd = three(mm, (shifted[0, at, H:], shifted[1, at, H:]), (beams[q][0, H:, :], beams[q][1, H:, :]))
        even = even + jnp.concatenate(nyquist[2 * q : 2 * q + 2], 0) * edges[q, 0:1, :]
        sheared[0, at, :H], sheared[1, at, :H] = split(even)
        sheared[0, at, H:], sheared[1, at, H:] = split(odd)
    spectrum = jnp.concatenate(
        [
            three(
                mm, (sheared[0, :, part], sheared[1, :, part]), (dft_t[0, :H, part], dft_t[1, :H, part])
            )
            for part in (slice(0, H), slice(H, N))
        ],
        1,
    )
    lane_first = lax.broadcasted_iota(jnp.int32, (8, H), 1) == 0
    sums = [None] * 8
    for q in range(PAIRS):
        cb, sb = rows_tables[q, 0, 64:72, :], rows_tables[q, 1, 64:72, :]
        near = rows_tables[q, :, pl.ds(pl.multiple_of(8 * block, 8), 8), :]
        for u in range(8):
            ca, sa = near[0, u : u + 1, :], near[1, u : u + 1, :]
            c, s = ca * cb - sa * sb, sa * cb + ca * sb
            c_first, s_first = jnp.where(lane_first, 1.0, c), jnp.where(lane_first, 0.0, s)
            base = 2 * 64 * q + 8 * u
            one, two = spectrum[base : base + 8, :], spectrum[base + 64 : base + 72, :]
            both, apart = one + two, one - two
            unturned = jnp.concatenate(
                [both[:, :H] * c_first + apart[:, H:] * s_first, both[:, H:] * c - apart[:, :H] * s_first], 1
            )
            sums[u] = unturned if q == 0 else sums[u] + unturned
    weight = jnp.where(lax.broadcasted_iota(jnp.int32, (64, N), 1) % H == 0, 1.0 / 32.0, 1.0 / 16.0)
    whole = jnp.concatenate(sums, 0) * weight
    zeros = jnp.zeros((64, N), BF16)
    high, low = split(whole)
    result = None
    for side in range(2):
        dft_rows = [
            jnp.concatenate([dft_t[p, 64 * a + 32 * side : 64 * a + 32 * side + 32, :] for a in range(ANGLES)], 0)
            for p in range(2)
        ]
        order = (lambda v: [v, zeros]) if side == 0 else (lambda v: [zeros, v])
        columns = (jnp.concatenate(order(high), 0), jnp.concatenate(order(low), 0))
        part = three(mm_t, dft_rows, columns)
        result = part if result is None else result + part
    for peer in range(16):
        a = peer // 2
        out[peer, :CHUNK, :] = chunk
        out[peer, CHUNK:, :] = result[32 * a : 32 * a + 32, :]


def assemble_kernel(received, out):
    xl = lax.axis_index("xl")
    lower = lax.broadcasted_iota(jnp.int32, (32, W), 1) < 64
    for b in range(4):
        even = received[4 * b + xl, CHUNK:, :]
        odd = received[4 * b + 2 + xl, CHUNK:, :]
        lanes = slice(b * W, (b + 1) * W)
        out[0, :32, lanes] = jnp.where(lower, even, pltpu.roll(odd, 64, 1))
        out[0, 32:, lanes] = jnp.where(lower, pltpu.roll(even, 64, 1), odd)


def forward_call(*args):
    return pl.pallas_call(
        forward_kernel,
        in_specs=[pl.BlockSpec(memory_space=pltpu.SMEM)] + [pl.BlockSpec(memory_space=pl.ANY)] * 6,
        out_specs=pl.BlockSpec(memory_space=pltpu.VMEM),
        out_shape=jax.ShapeDtypeStruct((4 * ROWS, W), F32),
        scratch_shapes=[
            pltpu.VMEM((N, N), BF16),
            pltpu.VMEM((2, N, N), BF16),
            pltpu.VMEM((2, H, N), BF16),
            pltpu.VMEM((H // 4 + 24, N), F32),
            pltpu.VMEM((2, N, H), BF16),
            pltpu.VMEM((8, H), F32),
            pltpu.VMEM((N, N), F32),
            pltpu.VMEM((2, N, N), BF16),
            pltpu.VMEM((2, 2, N, H), BF16),
            pltpu.SemaphoreType.DMA((6,)),
        ],
        compiler_params=pltpu.CompilerParams(vmem_limit_bytes=60 * 1024 * 1024),
        cost_estimate=pl.CostEstimate(flops=4 * 10**9, bytes_accessed=4 * 10**6, transcendentals=0),
        name="forward",
    )(*args)


def vmem_call(kernel, outs, scratch, name, *args):
    result = pl.pallas_call(
        kernel,
        in_specs=[
            pl.BlockSpec(memory_space=pltpu.SMEM if a.shape == (1,) else pltpu.VMEM) for a in args
        ],
        out_specs=[pl.BlockSpec(memory_space=pltpu.VMEM)] * len(outs),
        out_shape=[jax.ShapeDtypeStruct(o, F32) for o in outs],
        scratch_shapes=scratch,
        compiler_params=pltpu.CompilerParams(vmem_limit_bytes=32 * 1024 * 1024),
        cost_estimate=pl.CostEstimate(flops=3 * 10**9, bytes_accessed=4 * 10**6, transcendentals=0),
        name=name,
    )(*args)
    return result if len(outs) > 1 else result[0]


GZ = ("xl", "z", "core")
PLANE = ("y", "xh", "xl")


def exchange(blocks, axes):
    return lax.all_to_all(blocks, axes, split_axis=0, concat_axis=0, tiled=True)


def swap(rows):
    return lax.ppermute(rows, "core", [(0, 1), (1, 0)])


def local(volume, probe, measured, angle_index, row_offset, col_offset):
    dft, dft_t = (jnp.asarray(t) for t in dft_tables())
    dfts = jnp.asarray(window_tables())
    factors, rows_tables, all_beams, edges, middles = (jnp.asarray(t) for t in phase_tables())
    beams = [jnp.asarray(b) for b in phase_tables()[2]]
    row = forward_call(angle_index, volume, dft, dft_t, factors, all_beams, edges)
    whole = exchange(row.reshape(ROWS, 4, W), GZ).reshape(4 * ROWS, W)
    keep, send = vmem_call(
        window_kernel,
        [(HALF + 64, W)] * 2,
        [
            pltpu.VMEM((2, MODES // 2, 2 * W, 2 * W), BF16),
            pltpu.VMEM((MODES // 2, 2 * W, 2 * W), F32),
            pltpu.VMEM((4, ROWS, W), F32),
        ],
        "window",
        row_offset,
        col_offset,
        whole,
        probe,
        measured,
        dfts,
    )
    packed = vmem_call(pack_kernel, [(16, CHUNK + 40, W)], [], "pack", angle_index, keep, swap(send))
    shared = exchange(packed, PLANE)
    relay = vmem_call(relay_kernel, [(8, CHUNK + 32, W)], [pltpu.VMEM((256, W), F32)], "relay", shared)
    rows = exchange(relay, "z")
    blocks = vmem_call(
        adjoint_kernel,
        [(16, CHUNK + 32, W)],
        [pltpu.VMEM((32, W), F32), pltpu.VMEM((2, N, N), BF16), pltpu.VMEM((2, N, N), BF16)],
        "adjoint",
        rows,
        dft_t,
        rows_tables,
        edges,
        middles,
        *beams,
    )
    final = exchange(blocks, PLANE)
    mine = final[:, :CHUNK, :].reshape(HALF, W)
    other = swap(mine)
    volume_update = vmem_call(assemble_kernel, [(1, 64, N)], [], "assemble", final)
    core = lax.axis_index("core")
    held = lax.optimization_barrier(jnp.stack([mine, mine]))
    probe_update = lax.dynamic_update_slice(held, other[None], (1 - core, 0, 0))
    return volume_update, probe_update.reshape(MODES, 2, W, W)


def solution(mesh):
    split_mesh = Mesh(mesh.devices.reshape(4, 2, 2, 8, 2), ("y", "xh", "xl", "z", "core"))
    angle, gz = ("y", "xh"), GZ
    return jax.shard_map(
        local,
        mesh=split_mesh,
        in_specs=(
            P(gz, None, None),
            P(),
            P(angle, gz, None, None),
            P(angle),
            P(angle, gz),
            P(angle, gz),
        ),
        out_specs=(P(gz, angle, None), P()),
        check_vma=False,
    )
```

time: 95.8 us -> 92.2 us (0.962)
  Pallas kernels: 14.6 us -> 11 us
  local copies, waits for them, and re-layouts: 0.08 us -> 1.09 us
  other arithmetic: 1.04 us -> 0.07 us
    pallas_call x5, Pallas kernels: 9.04 us -> 6.28 us  [vmem_call(): pl.pallas_call(kernel, in_specs=[pl.BlockSpec(memory_space=pltpu.SMEM if...]
    select_n x1 -> x0, other arithmetic: 1.04 us -> none  [local(): jnp.where(core == 0, jnp.stack([mine, other]), jnp.stack([other, mine]))]
    unnamed x18 -> x24, local copies, waits for them, and re-layouts: 0.04 us -> 1.02 us
where the time goes in v3:
time: 92.2 us; the launch traced here: 92 us
  blocking collectives  52.3 us (57%)
  starting transfers between devices  15.7 us (17%)
  Pallas kernels  11 us (12%)
  waiting for transfers between devices  9.06 us (10%)
  between operations  2.74 us (3%)
  local copies, waits for them, and re-layouts  1.09 us (1%)
    all_to_all x3, blocking collectives, exchange(): return lax.all_to_all(blocks, axes, split_axis=0, concat_axis=0, tiled=True)  52.3 us
    all_to_all x1, starting transfers between devices, exchange(): return lax.all_to_all(blocks, axes, split_axis=0, concat_axis=0, tiled=True)  11.1 us
    all_to_all x1, waiting for transfers between devices, exchange(): return lax.all_to_all(blocks, axes, split_axis=0, concat_axis=0, tiled=True)  6.78 us
    pallas_call x5, Pallas kernels, vmem_call(): pl.pallas_call(kernel, in_specs=[pl.BlockSpec(memory_space=pltpu.SMEM if...  6.28 us
    pallas_call x1, Pallas kernels, forward_call(): pl.pallas_call(forward_kernel, in_specs=[pl.BlockSpec(memory_space=pltpu....  4.75 us
    ppermute x2, starting transfers between devices, swap(): return lax.ppermute(rows, 'core', [(0, 1), (1, 0)])  4.62 us
    ppermute x2, waiting for transfers between devices, swap(): return lax.ppermute(rows, 'core', [(0, 1), (1, 0)])  2.28 us
  transfers between devices with their start and end apart: 3, of which 3 were waited for; matrix products, arithmetic and copies ran while one was open for 0% of the time, Pallas kernels for 1%

profile of v3, /device:TPU:1, one launch (start us, length us, event | category | flops | bytes accessed | tf_op | source)
XLA Modules:
  0.0 92.0 jit_solution(17301205503285611007)
XLA Ops:
  1.3 0.0 copy-start
  1.3 0.0 copy-start.1
  1.3 0.0 copy-start.8
  1.3 4.8 %forward.1 = f32[128,128]{1,0:T(8,128)} custom-call(s32[1]{0:T(128)S(6)} %copy.21.sc, bf16[1,512,512]{2,1,0:T(8,128)(2,1)} %volume.1, bf16[2,512,512]{2,1,0:T(8,128)(2,1)} %constant.35.clone.dft_hbm, bf16[2,512,512]{2,1,0:T(8,128)(2,1)} %constant.36.clone.dft_t_hbm.dft_t, f32[8,88,512]{2,1,0:T(8,128)} %constant.38.clone.factors_hbm, ...), custom_call_target="tpu_custom_call" | custom-call | flops 4000000000 | bytes 4000000 | tf_op jit(solution)/shard_map/forward/pallas_call | solution.py:389
  6.1 11.1 %all-to-all-start = ((f32[32,4,128]{2,1,0:T(4,128)}), f32[32,4,128]{2,1,0:T(4,128)S(1)}, u32[]{:S(2)}, u32[]{:S(2)}) async-start(f32[32,4,128]{2,1,0:T(4,128)} %bitcast.11), calls=%async_computation | async-start | bytes 131072 | tf_op jit(solution)/shard_map/all_to_all | solution.py:433
  18.4 6.8 %all-to-all-done = f32[32,4,128]{2,1,0:T(4,128)S(1)} async-done(((f32[32,4,128]{2,1,0:T(4,128)}), f32[32,4,128]{2,1,0:T(4,128)S(1)}, u32[]{:S(2)}, u32[]{:S(2)}) %all-to-all-start) | async-done | bytes 65568 | tf_op jit(solution)/shard_map/all_to_all | solution.py:433
  25.2 0.0 copy-done
  25.2 0.0 copy-done.1
  25.2 0.0 copy-done.8
  25.2 2.6 %window.1 = (f32[1088,128]{1,0:T(8,128)S(1)}, f32[1088,128]{1,0:T(8,128)S(1)}) custom-call(s32[1,1]{1,0:T(1,128)S(6)} %copy.22.row_ref, s32[1,1]{1,0:T(1,128)S(6)} %copy.23.col_ref, f32[128,128]{1,0:T(8,128)S(1)} %bitcast.7, f32[8,2,128,128]{3,2,1,0:T(8,128)S(1)} %copy-done, f32[1,1,128,128]{3,2,1,0:T(8,128)S(1)} %copy-done.1, ...), custom_call_target="tpu_custom_call" | custom-call | flops 3000000000 | bytes 4000000 | tf_op jit(solution)/shard_map/window/pallas_call | solution.py:413
  27.8 1.3 %collective-permute-start = (f32[1088,128]{1,0:T(8,128)S(1)}, f32[1088,128]{1,0:T(8,128)S(1)}, u32[]{:S(2)}, u32[]{:S(2)}) collective-permute-start(f32[1088,128]{1,0:T(8,128)S(1)} %get-tuple-element.5), channel_id=1, source_target_pairs={{0,1},{1,0},{2,3},{3,2},{4,5},{5,4},{6,7},{7,6},{8,9},{9,8},{10,11... | collective-permute-start | bytes 1671176 | tf_op jit(solution)/shard_map/ppermute | solution.py:437
  29.2 1.6 %collective-permute-done.other = f32[1088,128]{1,0:T(8,128)S(1)} collective-permute-done((f32[1088,128]{1,0:T(8,128)S(1)}, f32[1088,128]{1,0:T(8,128)S(1)}, u32[]{:S(2)}, u32[]{:S(2)}) %collective-permute-start) | collective-permute-done | bytes 557088 | tf_op jit(solution)/shard_map/ppermute | solution.py:437
  30.7 0.1 pack.1
  30.8 20.8 %all_to_all.20.received = f32[16,104,128]{2,1,0:T(8,128)S(1)} all-to-all(f32[16,104,128]{2,1,0:T(8,128)S(1)} %pack.1), channel_id=1, replica_groups=mesh['y'=4,'xh'=2,'xl'=2,'z'=8,'core'=2] {'y','xh','xl'}, dimensions={0} | all-to-all | bytes 1703936 | tf_op jit(solution)/shard_map/all_to_all | solution.py:433
  51.6 0.0 copy-start.2
  51.6 0.0 copy-start.3
  51.6 0.0 copy-start.4
  51.6 0.0 copy-start.5
  51.6 0.0 copy-start.6
  51.6 0.0 copy-start.7
  51.6 0.0 copy-start.9
  51.7 0.0 copy-start.10
  51.7 0.2 relay.1
  51.8 15.7 %all_to_all.21.received = f32[8,96,128]{2,1,0:T(8,128)S(1)} all-to-all(f32[8,96,128]{2,1,0:T(8,128)S(1)} %relay.1), channel_id=1, replica_groups=mesh['y'=4,'xh'=2,'xl'=2,'z'=8,'core'=2] {'z'}, dimensions={0} | all-to-all | bytes 786432 | tf_op jit(solution)/shard_map/all_to_all | solution.py:433
  67.6 0.0 copy-done.2
  67.6 0.0 copy-done.3
  67.6 0.0 copy-done.4
  67.6 0.0 copy-done.5
  67.6 0.0 copy-done.6
  67.6 0.0 copy-done.7
  67.6 0.0 copy-done.9
  67.6 0.0 copy-done.10
  67.6 2.7 %adjoint.1 = f32[16,96,128]{2,1,0:T(8,128)S(1)} custom-call(f32[8,96,128]{2,1,0:T(8,128)S(1)} %all_to_all.21.received, bf16[2,512,512]{2,1,0:T(8,128)(2,1)S(1)} %copy-done.2, f32[4,2,72,256]{3,2,1,0:T(8,128)S(1)} %copy-done.3, f32[4,8,256]{2,1,0:T(8,128)S(1)} %copy-done.9, f32[16,256]{1,0:T(8,128)S(1)} %copy-done.10, bf16[2,512,256]{2,1,0:T(8,128)(2,1)S(1)} %copy-done.7, ...), custom_call_target="tpu_custom_call" | custom-call | flops 3000000000 | bytes 4000000 | tf_op jit(solution)/shard_map/adjoint/pallas_call | solution.py:413
  70.3 15.8 %all_to_all.22.received = f32[16,96,128]{2,1,0:T(8,128)S(1)} all-to-all(f32[16,96,128]{2,1,0:T(8,128)S(1)} %adjoint.1), channel_id=1, replica_groups=mesh['y'=4,'xh'=2,'xl'=2,'z'=8,'core'=2] {'y','xh','xl'}, dimensions={0} | all-to-all | bytes 1572864 | tf_op jit(solution)/shard_map/all_to_all | solution.py:433
  86.1 3.3 %collective-permute-start.1 = (f32[1024,128]{1,0:T(8,128)S(1)}, f32[1024,128]{1,0:T(8,128)S(1)}, u32[]{:S(2)}, u32[]{:S(2)}) collective-permute-start(f32[1024,128]{1,0:T(8,128)S(1)} %bitcast.8), channel_id=1, source_target_pairs={{0,1},{1,0},{2,3},{3,2},{4,5},{5,4},{6,7},{7,6},{8,9},{9,8},{10,11... | collective-permute-start | bytes 1572872 | tf_op jit(solution)/shard_map/ppermute | solution.py:437
  89.4 0.1 pad_maximum_fusion
  89.5 0.8 assemble.1
  90.2 0.7 collective-permute-done.1
  91.0 0.0 copy-start.11
  91.0 1.0 %copy-done.11 = f32[2,1024,128]{2,1,0:T(8,128)} copy-done((f32[2,1024,128]{2,1,0:T(8,128)}, f32[2,1024,128]{2,1,0:T(8,128)S(1)}, u32[]{:S(2)}) %copy-start.11) | copy-done | bytes 1048600
  (2 shorter events, 0.1 us)
Async XLA Ops:
  1.3 23.9 %copy-start = (f32[8,2,128,128]{3,2,1,0:T(8,128)S(1)}, f32[8,2,128,128]{3,2,1,0:T(8,128)}, u32[]{:S(2)}) copy-start(f32[8,2,128,128]{3,2,1,0:T(8,128)} %probe.1) | copy-start | bytes 3145732
  1.3 23.9 %copy-start.1 = (f32[1,1,128,128]{3,2,1,0:T(8,128)S(1)}, f32[1,1,128,128]{3,2,1,0:T(8,128)}, u32[]{:S(2)}) copy-start(f32[1,1,128,128]{3,2,1,0:T(8,128)} %measured.1) | copy-start | bytes 196612
  1.3 23.9 %copy-start.8 = (bf16[2,2,256,256]{3,2,1,0:T(8,128)(2,1)S(1)}, bf16[2,2,256,256]{3,2,1,0:T(8,128)(2,1)}, u32[]{:S(2)}) copy-start(bf16[2,2,256,256]{3,2,1,0:T(8,128)(2,1)} %constant.37.clone.dfts) | copy-start | bytes 1572868
  6.1 19.1 %all-to-all-start = ((f32[32,4,128]{2,1,0:T(4,128)}), f32[32,4,128]{2,1,0:T(4,128)S(1)}, u32[]{:S(2)}, u32[]{:S(2)}) async-start(f32[32,4,128]{2,1,0:T(4,128)} %bitcast.11), calls=%async_computation | async-start | bytes 131072 | tf_op jit(solution)/shard_map/all_to_all | solution.py:433
  27.8 2.9 %collective-permute-start = (f32[1088,128]{1,0:T(8,128)S(1)}, f32[1088,128]{1,0:T(8,128)S(1)}, u32[]{:S(2)}, u32[]{:S(2)}) collective-permute-start(f32[1088,128]{1,0:T(8,128)S(1)} %get-tuple-element.5), channel_id=1, source_target_pairs={{0,1},{1,0},{2,3},{3,2},{4,5},{5,4},{6,7},{7,6},{8,9},{9,8},{10,11... | collective-permute-start | bytes 1671176 | tf_op jit(solution)/shard_map/ppermute | solution.py:437
  51.6 16.0 %copy-start.2 = (bf16[2,512,512]{2,1,0:T(8,128)(2,1)S(1)}, bf16[2,512,512]{2,1,0:T(8,128)(2,1)}, u32[]{:S(2)}) copy-start(bf16[2,512,512]{2,1,0:T(8,128)(2,1)} %constant.36.clone.dft_t_hbm.dft_t) | copy-start | bytes 3145732
  51.6 16.0 %copy-start.3 = (f32[4,2,72,256]{3,2,1,0:T(8,128)S(1)}, f32[4,2,72,256]{3,2,1,0:T(8,128)}, u32[]{:S(2)}) copy-start(f32[4,2,72,256]{3,2,1,0:T(8,128)} %constant.39.clone.rows_tables) | copy-start | bytes 1769476
  51.6 16.0 %copy-start.4 = (bf16[2,512,256]{2,1,0:T(8,128)(2,1)S(1)}, bf16[2,512,256]{2,1,0:T(8,128)(2,1)}, u32[]{:S(2)}) copy-start(bf16[2,512,256]{2,1,0:T(8,128)(2,1)} %constant.46.clone.refs_3_) | copy-start | bytes 1572868
  51.6 16.0 %copy-start.5 = (bf16[2,512,256]{2,1,0:T(8,128)(2,1)S(1)}, bf16[2,512,256]{2,1,0:T(8,128)(2,1)}, u32[]{:S(2)}) copy-start(bf16[2,512,256]{2,1,0:T(8,128)(2,1)} %constant.45.clone.refs_2_) | copy-start | bytes 1572868
  51.6 16.0 %copy-start.6 = (bf16[2,512,256]{2,1,0:T(8,128)(2,1)S(1)}, bf16[2,512,256]{2,1,0:T(8,128)(2,1)}, u32[]{:S(2)}) copy-start(bf16[2,512,256]{2,1,0:T(8,128)(2,1)} %constant.44.clone.refs_1_) | copy-start | bytes 1572868
  51.6 16.0 %copy-start.7 = (bf16[2,512,256]{2,1,0:T(8,128)(2,1)S(1)}, bf16[2,512,256]{2,1,0:T(8,128)(2,1)}, u32[]{:S(2)}) copy-start(bf16[2,512,256]{2,1,0:T(8,128)(2,1)} %constant.43.clone.refs_0_) | copy-start | bytes 1572868
  51.6 16.0 %copy-start.9 = (f32[4,8,256]{2,1,0:T(8,128)S(1)}, f32[4,8,256]{2,1,0:T(8,128)}, u32[]{:S(2)}) copy-start(f32[4,8,256]{2,1,0:T(8,128)} %constant.41.clone.edges_hbm.edges) | copy-start | bytes 98308
  51.7 16.0 %copy-start.10 = (f32[16,256]{1,0:T(8,128)S(1)}, f32[16,256]{1,0:T(8,128)}, u32[]{:S(2)}) copy-start(f32[16,256]{1,0:T(8,128)} %constant.42.clone.middles) | copy-start | bytes 49156
  86.1 4.8 %collective-permute-start.1 = (f32[1024,128]{1,0:T(8,128)S(1)}, f32[1024,128]{1,0:T(8,128)S(1)}, u32[]{:S(2)}, u32[]{:S(2)}) collective-permute-start(f32[1024,128]{1,0:T(8,128)S(1)} %bitcast.8), channel_id=1, source_target_pairs={{0,1},{1,0},{2,3},{3,2},{4,5},{5,4},{6,7},{7,6},{8,9},{9,8},{10,11... | collective-permute-start | bytes 1572872 | tf_op jit(solution)/shard_map/ppermute | solution.py:437
  91.0 1.0 %copy-start.11 = (f32[2,1024,128]{2,1,0:T(8,128)}, f32[2,1024,128]{2,1,0:T(8,128)S(1)}, u32[]{:S(2)}) copy-start(f32[2,1024,128]{2,1,0:T(8,128)S(1)} %bitcast_dynamic-update-slice_fusion) | copy-start | bytes 3145732

commit v4 on v3

--- a/solution.py
+++ b/solution.py
@@ -17,6 +17,7 @@
 ROWS = 32
 HALF = MODES * 2 * W // 2
 CHUNK = HALF // 16
+MESSAGE = CHUNK + 17
 F32 = jnp.float32
 BF16 = jnp.bfloat16
 
@@ -102,7 +103,9 @@
 
 
 def three(dot, a, b):
-    return dot(a[0], b[0]) + (dot(a[0], b[1]) + dot(a[1], b[0]))
+    rows = a[0].shape[0]
+    both = dot(jnp.concatenate([a[0], a[1]], 0), b[0])
+    return both[:rows] + (both[rows:] + dot(a[0], b[1]))
 
 
 def forward_kernel(
@@ -130,9 +133,9 @@
     moves[0].wait()
     backward = mm(slab[:, H:], reverse).astype(BF16)
     moves[1].wait()
+    moves[2].wait()
     for lanes, columns in zip(halves, (slab[:, :H], backward)):
         spec[:, lanes] = mm(dft[0], columns) + mm(dft[1], columns)
-    moves[2].wait()
     half_row = jnp.where(lax.broadcasted_iota(jnp.int32, (8, H), 0) == 0, 0.5, 1.0)
     for lanes in halves:
         cb, sb = factors[64:72, lanes], factors[72:80, lanes]
@@ -253,37 +256,59 @@
             send[at, :] = jnp.where(core == 0, grads[1][part], grads[0][part])
     patch = grad_imag * obj_real - grad_real * obj_imag
     shown = pltpu.roll(patch, W + row, 0)[:ROWS]
-    wide = pltpu.roll(jnp.concatenate([shown, jnp.zeros((ROWS, N - W), F32)], 1), col, 1)
-    for t in range(4):
-        pieces[t] = wide[:, t * W : (t + 1) * W]
-    for t in range(4):
-        at = slice(HALF + 16 * t, HALF + 16 * (t + 1))
-        even, odd = pieces[t, pl.ds(0, 16, stride=2), :], pieces[t, pl.ds(1, 16, stride=2), :]
-        keep[at, :] = jnp.where(core == 0, even, odd)
-        send[at, :] = jnp.where(core == 0, odd, even)
+    pieces[...] = shown
+    even, odd = pieces[pl.ds(0, 16, stride=2), :], pieces[pl.ds(1, 16, stride=2), :]
+    keep[HALF : HALF + 16, :] = jnp.where(core == 0, even, odd)
+    send[HALF : HALF + 16, :] = jnp.where(core == 0, odd, even)
+    column = jnp.full((8, W), col, jnp.int32).astype(F32)
+    keep[HALF + 16 :, :] = column
+    send[HALF + 16 :, :] = column
 
 
 def pack_kernel(sc, keep, other, out):
-    angle = jnp.broadcast_to(sc[0].astype(F32), (8, W))
+    lane = lax.broadcasted_iota(jnp.int32, (1, W), 1)
+    first, second = keep[HALF + 16 : HALF + 17, :], other[HALF + 16 : HALF + 17, :]
+    numbers = jnp.where(lane < 32, sc[0].astype(F32), jnp.where(lane < 64, first, second))
     for peer in range(16):
         rows = slice(CHUNK * peer, CHUNK * (peer + 1))
-        out[peer, :CHUNK, :] = keep[rows, :] + other[rows, :]
+        at = MESSAGE * peer
+        out[at : at + CHUNK, :] = keep[rows, :] + other[rows, :]
+        rows = slice(HALF + 8 * (peer % 2), HALF + 8 * (peer % 2) + 8)
+        out[at + CHUNK : at + CHUNK + 8, :] = keep[rows, :]
+        out[at + CHUNK + 8 : at + CHUNK + 16, :] = other[rows, :]
+        out[at + CHUNK + 16 : at + MESSAGE, :] = numbers
+
+
+def relay_kernel(received, out, pieces, numbers):
+    total = received[:CHUNK, :]
+    for peer in range(1, 16):
+        total = total + received[MESSAGE * peer : MESSAGE * peer + CHUNK, :]
+    heads = jnp.concatenate([received[pl.ds(MESSAGE * p + MESSAGE - 1, 1), :] for p in range(16)], 0)
+    rolls = [heads] + [pltpu.roll(heads, 32 * i, 1) for i in (1, 2, 3)]
+    quarter = lax.broadcasted_iota(jnp.int32, (16, W), 1) // 32
+    for i in range(3):
+        value = rolls[0]
+        for shift in (1, 2, 3):
+            value = jnp.where(quarter == (i + shift) % 4, rolls[shift], value)
+        numbers[i] = value
+    windows = [(peer, side) for peer in range(16) for side in range(2)]
+    rows = jnp.concatenate(
+        [received[MESSAGE * p + CHUNK + 8 * i : MESSAGE * p + CHUNK + 8 * i + 8, :] for p, i in windows], 0
+    )
+    columns = jnp.concatenate(
+        [jnp.broadcast_to(numbers[1 + i, p : p + 1, :], (8, W)) for p, i in windows], 0
+    ).astype(jnp.int32)
+    for bit in range(7):
+        rows = jnp.where(columns & (1 << bit) != 0, pltpu.roll(rows, 1 << bit, 1), rows)
+    lane = lax.broadcasted_iota(jnp.int32, rows.shape, 1)
+    tiles = (columns >> 7) + jnp.where(lane < (columns & (W - 1)), 1, 0)
+    for a in range(ANGLES):
+        angle = jnp.max(numbers[0, 2 * a : 2 * a + 1, :]).astype(jnp.int32)
+        slot = jnp.where(angle >= PAIRS, 2 * (ANGLES - 1 - angle) + 1, 2 * angle)
+        at = pl.multiple_of(32 * slot, 32)
         for t in range(4):
-            base = HALF + 16 * t + 8 * (peer % 2)
-            out[peer, CHUNK + 8 * t : CHUNK + 8 * t + 8, :] = keep[base : base + 8, :] + other[base : base + 8, :]
-        out[peer, CHUNK + 32 :, :] = angle
-
-
-def relay_kernel(received, out, pieces):
-    total = received[0, :CHUNK, :]
-    for peer in range(1, 16):
-        total = total + received[peer, :CHUNK, :]
-    for a in range(ANGLES):
-        number = jnp.max(received[2 * a, CHUNK + 32 :, :]).astype(jnp.int32)
-        slot = jnp.where(number >= PAIRS, 2 * (ANGLES - 1 - number) + 1, 2 * number)
-        pieces[pl.ds(pl.multiple_of(32 * slot, 32), 32), :] = (
-            received[2 * a, CHUNK : CHUNK + 32, :] + received[2 * a + 1, CHUNK : CHUNK + 32, :]
-        )
+            part = jnp.where(tiles[32 * a : 32 * a + 32] == t, rows[32 * a : 32 * a + 32], 0.0)
+            pieces[pl.ds(at + 8 * t, 8), :] = jnp.sum(part.reshape(4, 8, W), axis=0)
     for z in range(8):
         out[z, :CHUNK, :] = total
         out[z, CHUNK:, :] = pieces[pl.ds(z, 32, stride=8), :]
@@ -374,7 +399,9 @@
         out[peer, CHUNK:, :] = result[32 * a : 32 * a + 32, :]
 
 
-def assemble_kernel(received, out):
+def assemble_kernel(received, out, probe_out, sem):
+    move = pltpu.make_async_copy(received.at[:, pl.ds(0, CHUNK), :], probe_out.at[lax.axis_index("core")], sem)
+    move.start()
     xl = lax.axis_index("xl")
     lower = lax.broadcasted_iota(jnp.int32, (32, W), 1) < 64
     for b in range(4):
@@ -383,6 +410,7 @@
         lanes = slice(b * W, (b + 1) * W)
         out[0, :32, lanes] = jnp.where(lower, even, pltpu.roll(odd, 64, 1))
         out[0, 32:, lanes] = jnp.where(lower, pltpu.roll(even, 64, 1), odd)
+    move.wait()
 
 
 def forward_call(*args):
@@ -409,13 +437,14 @@
     )(*args)
 
 
-def vmem_call(kernel, outs, scratch, name, *args):
+def vmem_call(kernel, outs, scratch, name, *args, far=0):
     result = pl.pallas_call(
         kernel,
         in_specs=[
             pl.BlockSpec(memory_space=pltpu.SMEM if a.shape == (1,) else pltpu.VMEM) for a in args
         ],
-        out_specs=[pl.BlockSpec(memory_space=pltpu.VMEM)] * len(outs),
+        out_specs=[pl.BlockSpec(memory_space=pltpu.VMEM)] * (len(outs) - far)
+        + [pl.BlockSpec(memory_space=pl.ANY)] * far,
         out_shape=[jax.ShapeDtypeStruct(o, F32) for o in outs],
         scratch_shapes=scratch,
         compiler_params=pltpu.CompilerParams(vmem_limit_bytes=32 * 1024 * 1024),
@@ -446,11 +475,11 @@
     whole = exchange(row.reshape(ROWS, 4, W), GZ).reshape(4 * ROWS, W)
     keep, send = vmem_call(
         window_kernel,
-        [(HALF + 64, W)] * 2,
+        [(HALF + 24, W)] * 2,
         [
             pltpu.VMEM((2, MODES // 2, 2 * W, 2 * W), BF16),
             pltpu.VMEM((MODES // 2, 2 * W, 2 * W), F32),
-            pltpu.VMEM((4, ROWS, W), F32),
+            pltpu.VMEM((ROWS, W), F32),
         ],
         "window",
         row_offset,
@@ -460,9 +489,9 @@
         measured,
         dfts,
     )
-    packed = vmem_call(pack_kernel, [(16, CHUNK + 40, W)], [], "pack", angle_index, keep, swap(send))
-    shared = exchange(packed, PLANE)
-    relay = vmem_call(relay_kernel, [(8, CHUNK + 32, W)], [pltpu.VMEM((256, W), F32)], "relay", shared)
+    packed = vmem_call(pack_kernel, [(16 * MESSAGE, W)], [], "pack", angle_index, keep, swap(send))
+    shared = exchange(packed.reshape(16, MESSAGE, 1, W), PLANE).reshape(16 * MESSAGE, W)
+    relay = vmem_call(relay_kernel, [(8, CHUNK + 32, W)], [pltpu.VMEM((256, W), F32), pltpu.VMEM((3, 16, W), F32)], "relay", shared)
     rows = exchange(relay, "z")
     blocks = vmem_call(
         adjoint_kernel,
@@ -477,12 +506,17 @@
         *beams,
     )
     final = exchange(blocks, PLANE)
-    mine = final[:, :CHUNK, :].reshape(HALF, W)
-    other = swap(mine)
-    volume_update = vmem_call(assemble_kernel, [(1, 64, N)], [], "assemble", final)
+    other = swap(final[:, :CHUNK, :])
+    volume_update, half = vmem_call(
+        assemble_kernel,
+        [(1, 64, N), (2, 16, CHUNK, W)],
+        [pltpu.SemaphoreType.DMA],
+        "assemble",
+        final,
+        far=1,
+    )
     core = lax.axis_index("core")
-    held = lax.optimization_barrier(jnp.stack([mine, mine]))
-    probe_update = lax.dynamic_update_slice(held, other[None], (1 - core, 0, 0))
+    probe_update = lax.dynamic_update_slice(half, other[None], (1 - core, 0, 0, 0))
     return volume_update, probe_update.reshape(MODES, 2, W, W)
 
 

time: 92.2 us -> 89.8 us (0.974)
  blocking collectives: 52.3 us -> 49.9 us
    all_to_all x3, blocking collectives: 52.3 us -> 49.9 us  [exchange(): return lax.all_to_all(blocks, axes, split_axis=0, concat_axis=0, tiled=True)]
    pallas_call x5, Pallas kernels: 6.28 us -> 7.25 us  [vmem_call(): pl.pallas_call(kernel, in_specs=[pl.BlockSpec(memory_space=pltpu.SMEM if...]
    unnamed x24 -> x22, local copies, waits for them, and re-layouts: 1.02 us -> 0.06 us
  transfers between devices with their start and end apart: 3 -> 3, of which waited for: 3 -> 3; matrix products, arithmetic and copies ran while one was open for 0% -> 0% of each run, Pallas kernels for 1% -> 2%
where the time goes in v4:
time: 89.8 us; the launch traced here: 89.6 us
  blocking collectives  49.9 us (56%)
  starting transfers between devices  15.9 us (18%)
  Pallas kernels  11.8 us (13%)
  waiting for transfers between devices  8.41 us (9%)
  between operations  2.73 us (3%)
  local copies, waits for them, and re-layouts  0.92 us (1%)
    all_to_all x3, blocking collectives, exchange(): return lax.all_to_all(blocks, axes, split_axis=0, concat_axis=0, tiled=True)  49.9 us
    all_to_all x1, starting transfers between devices, exchange(): return lax.all_to_all(blocks, axes, split_axis=0, concat_axis=0, tiled=True)  11.1 us
    pallas_call x5, Pallas kernels, vmem_call(): pl.pallas_call(kernel, in_specs=[pl.BlockSpec(memory_space=pltpu.SMEM if...  7.25 us
    all_to_all x1, waiting for transfers between devices, exchange(): return lax.all_to_all(blocks, axes, split_axis=0, concat_axis=0, tiled=True)  6.78 us
    ppermute x2, starting transfers between devices, swap(): return lax.ppermute(rows, 'core', [(0, 1), (1, 0)])  4.79 us
    pallas_call x1, Pallas kernels, forward_call(): pl.pallas_call(forward_kernel, in_specs=[pl.BlockSpec(memory_space=pltpu....  4.53 us
  transfers between devices with their start and end apart: 3, of which 3 were waited for; matrix products, arithmetic and copies ran while one was open for 0% of the time, Pallas kernels for 2%

profile of v4, /device:TPU:1, one launch (start us, length us, event | category | flops | bytes accessed | tf_op | source)
XLA Modules:
  0.0 89.6 jit_solution(16446997638357915509)
XLA Ops:
  1.3 0.0 copy-start
  1.3 0.0 copy-start.1
  1.3 0.0 copy-start.8
  1.3 4.5 %forward.1 = f32[128,128]{1,0:T(8,128)} custom-call(s32[1]{0:T(128)S(6)} %copy.22.sc, bf16[1,512,512]{2,1,0:T(8,128)(2,1)} %volume.1, bf16[2,512,512]{2,1,0:T(8,128)(2,1)} %constant.35.clone.dft_hbm, bf16[2,512,512]{2,1,0:T(8,128)(2,1)} %constant.36.clone.dft_t_hbm.dft_t, f32[8,88,512]{2,1,0:T(8,128)} %constant.38.clone.factors_hbm, ...), custom_call_target="tpu_custom_call" | custom-call | flops 4000000000 | bytes 4000000 | tf_op jit(solution)/shard_map/forward/pallas_call | solution.py:417
  5.8 11.1 %all-to-all-start = ((f32[32,4,128]{2,1,0:T(4,128)}), f32[32,4,128]{2,1,0:T(4,128)S(1)}, u32[]{:S(2)}, u32[]{:S(2)}) async-start(f32[32,4,128]{2,1,0:T(4,128)} %bitcast.10), calls=%async_computation | async-start | bytes 131072 | tf_op jit(solution)/shard_map/all_to_all | solution.py:462
  18.2 6.8 %all-to-all-done = f32[32,4,128]{2,1,0:T(4,128)S(1)} async-done(((f32[32,4,128]{2,1,0:T(4,128)}), f32[32,4,128]{2,1,0:T(4,128)S(1)}, u32[]{:S(2)}, u32[]{:S(2)}) %all-to-all-start) | async-done | bytes 65568 | tf_op jit(solution)/shard_map/all_to_all | solution.py:462
  25.0 0.0 copy-done
  25.0 0.0 copy-done.1
  25.0 0.0 copy-done.8
  25.0 2.5 %window.1 = (f32[1048,128]{1,0:T(8,128)S(1)}, f32[1048,128]{1,0:T(8,128)S(1)}) custom-call(s32[1,1]{1,0:T(1,128)S(6)} %copy.23.row_ref, s32[1,1]{1,0:T(1,128)S(6)} %copy.24.col_ref, f32[128,128]{1,0:T(8,128)S(1)} %bitcast.9, f32[8,2,128,128]{3,2,1,0:T(8,128)S(1)} %copy-done, f32[1,1,128,128]{3,2,1,0:T(8,128)S(1)} %copy-done.1, ...), custom_call_target="tpu_custom_call" | custom-call | flops 3000000000 | bytes 4000000 | tf_op jit(solution)/shard_map/window/pallas_call | solution.py:441
  27.5 1.3 %collective-permute-start = (f32[1048,128]{1,0:T(8,128)S(1)}, f32[1048,128]{1,0:T(8,128)S(1)}, u32[]{:S(2)}, u32[]{:S(2)}) collective-permute-start(f32[1048,128]{1,0:T(8,128)S(1)} %get-tuple-element.7), channel_id=1, source_target_pairs={{0,1},{1,0},{2,3},{3,2},{4,5},{5,4},{6,7},{7,6},{8,9},{9,8},{10,11... | collective-permute-start | bytes 1609736 | tf_op jit(solution)/shard_map/ppermute | solution.py:466
  28.9 1.6 %collective-permute-done.other = f32[1048,128]{1,0:T(8,128)S(1)} collective-permute-done((f32[1048,128]{1,0:T(8,128)S(1)}, f32[1048,128]{1,0:T(8,128)S(1)}, u32[]{:S(2)}, u32[]{:S(2)}) %collective-permute-start) | collective-permute-done | bytes 536608 | tf_op jit(solution)/shard_map/ppermute | solution.py:466
  30.4 0.1 pack.1
  30.5 18.8 %all_to_all.20 = f32[16,81,1,128]{3,2,1,0:T(1,128)S(1)} all-to-all(f32[16,81,1,128]{3,2,1,0:T(1,128)S(1)} %bitcast.7), channel_id=1, replica_groups=mesh['y'=4,'xh'=2,'xl'=2,'z'=8,'core'=2] {'y','xh','xl'}, dimensions={0} | all-to-all | bytes 1327104 | tf_op jit(solution)/shard_map/all_to_all | solution.py:462
  49.2 0.0 copy-start.2
  49.2 0.0 copy-start.3
  49.3 0.0 copy-start.4
  49.3 0.0 copy-start.5
  49.3 0.0 copy-start.6
  49.3 0.0 copy-start.7
  49.3 0.0 copy-start.9
  49.3 0.0 copy-start.10
  49.3 0.6 relay.1
  49.9 15.6 %all_to_all.21.received = f32[8,96,128]{2,1,0:T(8,128)S(1)} all-to-all(f32[8,96,128]{2,1,0:T(8,128)S(1)} %relay.1), channel_id=1, replica_groups=mesh['y'=4,'xh'=2,'xl'=2,'z'=8,'core'=2] {'z'}, dimensions={0} | all-to-all | bytes 786432 | tf_op jit(solution)/shard_map/all_to_all | solution.py:462
  65.5 0.0 copy-done.2
  65.5 0.0 copy-done.3
  65.5 0.0 copy-done.4
  65.5 0.0 copy-done.5
  65.5 0.0 copy-done.6
  65.5 0.0 copy-done.7
  65.6 0.0 copy-done.9
  65.6 0.0 copy-done.10
  65.6 2.6 %adjoint.1 = f32[16,96,128]{2,1,0:T(8,128)S(1)} custom-call(f32[8,96,128]{2,1,0:T(8,128)S(1)} %all_to_all.21.received, bf16[2,512,512]{2,1,0:T(8,128)(2,1)S(1)} %copy-done.2, f32[4,2,72,256]{3,2,1,0:T(8,128)S(1)} %copy-done.3, f32[4,8,256]{2,1,0:T(8,128)S(1)} %copy-done.9, f32[16,256]{1,0:T(8,128)S(1)} %copy-done.10, bf16[2,512,256]{2,1,0:T(8,128)(2,1)S(1)} %copy-done.7, ...), custom_call_target="tpu_custom_call" | custom-call | flops 3000000000 | bytes 4000000 | tf_op jit(solution)/shard_map/adjoint/pallas_call | solution.py:441
  68.2 15.5 %all_to_all.22.received = f32[16,96,128]{2,1,0:T(8,128)S(1)} all-to-all(f32[16,96,128]{2,1,0:T(8,128)S(1)} %adjoint.1), channel_id=1, replica_groups=mesh['y'=4,'xh'=2,'xl'=2,'z'=8,'core'=2] {'y','xh','xl'}, dimensions={0} | all-to-all | bytes 1572864 | tf_op jit(solution)/shard_map/all_to_all | solution.py:462
  83.7 3.5 %collective-permute-start.1 = (f32[16,64,128]{2,1,0:T(8,128)S(1)}, f32[16,64,128]{2,1,0:T(8,128)S(1)}, u32[]{:S(2)}, u32[]{:S(2)}) collective-permute-start(f32[16,64,128]{2,1,0:T(8,128)S(1)} %slice.4), channel_id=1, source_target_pairs={{0,1},{1,0},{2,3},{3,2},{4,5},{5,4},{6,7},{7,6},{8,9},{9,8},{10,11... | collective-permute-start | bytes 1572872 | tf_op jit(solution)/shard_map/ppermute | solution.py:466
  87.2 1.5 %assemble.1 = (f32[1,64,512]{2,1,0:T(8,128)}, f32[2,16,64,128]{3,2,1,0:T(8,128)}) custom-call(f32[16,96,128]{2,1,0:T(8,128)S(1)} %all_to_all.22.received), custom_call_target="tpu_custom_call" | custom-call | flops 3000000000 | bytes 4000000 | tf_op jit(solution)/shard_map/assemble/pallas_call | solution.py:441
  88.7 0.1 collective-permute-done.1
  88.7 0.8 bitcast_dynamic-update-slice_fusion
  (1 shorter events, 0.0 us)
Async XLA Ops:
  1.3 23.7 %copy-start = (f32[8,2,128,128]{3,2,1,0:T(8,128)S(1)}, f32[8,2,128,128]{3,2,1,0:T(8,128)}, u32[]{:S(2)}) copy-start(f32[8,2,128,128]{3,2,1,0:T(8,128)} %probe.1) | copy-start | bytes 3145732
  1.3 23.7 %copy-start.1 = (f32[1,1,128,128]{3,2,1,0:T(8,128)S(1)}, f32[1,1,128,128]{3,2,1,0:T(8,128)}, u32[]{:S(2)}) copy-start(f32[1,1,128,128]{3,2,1,0:T(8,128)} %measured.1) | copy-start | bytes 196612
  1.3 23.7 %copy-start.8 = (bf16[2,2,256,256]{3,2,1,0:T(8,128)(2,1)S(1)}, bf16[2,2,256,256]{3,2,1,0:T(8,128)(2,1)}, u32[]{:S(2)}) copy-start(bf16[2,2,256,256]{3,2,1,0:T(8,128)(2,1)} %constant.37.clone.dfts) | copy-start | bytes 1572868
  5.8 19.2 %all-to-all-start = ((f32[32,4,128]{2,1,0:T(4,128)}), f32[32,4,128]{2,1,0:T(4,128)S(1)}, u32[]{:S(2)}, u32[]{:S(2)}) async-start(f32[32,4,128]{2,1,0:T(4,128)} %bitcast.10), calls=%async_computation | async-start | bytes 131072 | tf_op jit(solution)/shard_map/all_to_all | solution.py:462
  27.5 2.9 %collective-permute-start = (f32[1048,128]{1,0:T(8,128)S(1)}, f32[1048,128]{1,0:T(8,128)S(1)}, u32[]{:S(2)}, u32[]{:S(2)}) collective-permute-start(f32[1048,128]{1,0:T(8,128)S(1)} %get-tuple-element.7), channel_id=1, source_target_pairs={{0,1},{1,0},{2,3},{3,2},{4,5},{5,4},{6,7},{7,6},{8,9},{9,8},{10,11... | collective-permute-start | bytes 1609736 | tf_op jit(solution)/shard_map/ppermute | solution.py:466
  49.2 16.3 %copy-start.2 = (bf16[2,512,512]{2,1,0:T(8,128)(2,1)S(1)}, bf16[2,512,512]{2,1,0:T(8,128)(2,1)}, u32[]{:S(2)}) copy-start(bf16[2,512,512]{2,1,0:T(8,128)(2,1)} %constant.36.clone.dft_t_hbm.dft_t) | copy-start | bytes 3145732
  49.2 16.3 %copy-start.3 = (f32[4,2,72,256]{3,2,1,0:T(8,128)S(1)}, f32[4,2,72,256]{3,2,1,0:T(8,128)}, u32[]{:S(2)}) copy-start(f32[4,2,72,256]{3,2,1,0:T(8,128)} %constant.39.clone.rows_tables) | copy-start | bytes 1769476
  49.3 16.3 %copy-start.4 = (bf16[2,512,256]{2,1,0:T(8,128)(2,1)S(1)}, bf16[2,512,256]{2,1,0:T(8,128)(2,1)}, u32[]{:S(2)}) copy-start(bf16[2,512,256]{2,1,0:T(8,128)(2,1)} %constant.46.clone.refs_3_) | copy-start | bytes 1572868
  49.3 16.3 %copy-start.5 = (bf16[2,512,256]{2,1,0:T(8,128)(2,1)S(1)}, bf16[2,512,256]{2,1,0:T(8,128)(2,1)}, u32[]{:S(2)}) copy-start(bf16[2,512,256]{2,1,0:T(8,128)(2,1)} %constant.45.clone.refs_2_) | copy-start | bytes 1572868
  49.3 16.3 %copy-start.6 = (bf16[2,512,256]{2,1,0:T(8,128)(2,1)S(1)}, bf16[2,512,256]{2,1,0:T(8,128)(2,1)}, u32[]{:S(2)}) copy-start(bf16[2,512,256]{2,1,0:T(8,128)(2,1)} %constant.44.clone.refs_1_) | copy-start | bytes 1572868
  49.3 16.3 %copy-start.7 = (bf16[2,512,256]{2,1,0:T(8,128)(2,1)S(1)}, bf16[2,512,256]{2,1,0:T(8,128)(2,1)}, u32[]{:S(2)}) copy-start(bf16[2,512,256]{2,1,0:T(8,128)(2,1)} %constant.43.clone.refs_0_) | copy-start | bytes 1572868
  49.3 16.3 %copy-start.9 = (f32[4,8,256]{2,1,0:T(8,128)S(1)}, f32[4,8,256]{2,1,0:T(8,128)}, u32[]{:S(2)}) copy-start(f32[4,8,256]{2,1,0:T(8,128)} %constant.41.clone.edges_hbm.edges) | copy-start | bytes 98308
  49.3 16.3 %copy-start.10 = (f32[16,256]{1,0:T(8,128)S(1)}, f32[16,256]{1,0:T(8,128)}, u32[]{:S(2)}) copy-start(f32[16,256]{1,0:T(8,128)} %constant.42.clone.middles) | copy-start | bytes 49156
  83.7 5.0 %collective-permute-start.1 = (f32[16,64,128]{2,1,0:T(8,128)S(1)}, f32[16,64,128]{2,1,0:T(8,128)S(1)}, u32[]{:S(2)}, u32[]{:S(2)}) collective-permute-start(f32[16,64,128]{2,1,0:T(8,128)S(1)} %slice.4), channel_id=1, source_target_pairs={{0,1},{1,0},{2,3},{3,2},{4,5},{5,4},{6,7},{7,6},{8,9},{9,8},{10,11... | collective-permute-start | bytes 1572872 | tf_op jit(solution)/shard_map/ppermute | solution.py:466

commit v5 on v4

--- a/solution.py
+++ b/solution.py
@@ -204,15 +204,42 @@
     )
 
 
-def window_kernel(row_ref, col_ref, whole, probe, measured, dfts, keep, send, stage, far, pieces):
-    row, col, core = jnp.max(row_ref[...]), jnp.max(col_ref[...]), lax.axis_index("core")
+def pairs_of_modes():
+    return [(j, j + MODES // 2) for j in range(MODES // 2)]
+
+
+def prepare_kernel(row_ref, probe, dfts, waves, band_dft, band_probe, stage):
+    start = -row_ref[0, 0]
+    lefts, rights = (dfts[0, 0], dfts[0, 1]), (dfts[1, 0], dfts[1, 1])
+    for j, pair in enumerate(pairs_of_modes()):
+        reals = jnp.concatenate([probe[m, 0] for m in pair], 1)
+        imags = jnp.concatenate([probe[m, 1] for m in pair], 1)
+        stage[0, j], stage[1, j] = split(jnp.concatenate([reals, imags], 0))
+    for j in range(MODES // 2):
+        stage[0, j], stage[1, j] = split(turn(three(mm, lefts, (stage[0, j], stage[1, j]))))
+    for j in range(MODES // 2):
+        waves[j] = three(mm, (stage[0, j], stage[1, j]), rights)
+    source = lax.broadcasted_iota(jnp.int32, (2 * W, 2 * W), 0)
+    target = lax.broadcasted_iota(jnp.int32, (2 * W, 2 * W), 1)
+    wanted = start + (target & (ROWS - 1)) + jnp.where(target & ROWS != 0, W, 0)
+    chosen = jnp.where(source == wanted, 1.0, 0.0)
+    first = jnp.where(target < 4 * ROWS, chosen, 0.0).astype(BF16)
+    second = jnp.where((target >= 4 * ROWS) & (target < 6 * ROWS), chosen, 0.0).astype(BF16)
+    band_dft[...] = (mm(lefts[0], first) + mm(lefts[1], second)).astype(BF16)
+    for m in range(MODES):
+        for part in range(2):
+            band_probe[m, part] = probe[m, part, pl.ds(start, ROWS), :]
+
+
+def window_kernel(
+    row_ref, col_ref, whole, probe, measured, dfts, waves, band_dft, band_probe, keep, send, stage, far, pieces
+):
+    row, col, core = row_ref[0, 0], col_ref[0, 0], lax.axis_index("core")
     rows = jnp.concatenate([whole[pl.ds(t, ROWS, stride=4), :] for t in range(4)], axis=1)
     band = pltpu.roll(rows, lax.rem(N - col, N), 1)[:, :W]
-    pad = jnp.zeros((W - ROWS, W), F32)
-    obj_real = pltpu.roll(jnp.concatenate([jnp.cos(band) - 1.0, pad], 0), -row, 0) + 1.0
-    obj_imag = pltpu.roll(jnp.concatenate([jnp.sin(band), pad], 0), -row, 0)
+    band_real, band_imag = jnp.cos(band) - 1.0, jnp.sin(band)
     lefts, rights = (dfts[0, 0], dfts[0, 1]), (dfts[1, 0], dfts[1, 1])
-    pairs = [(j, j + MODES // 2) for j in range(MODES // 2)]
+    pairs = pairs_of_modes()
     sides = (slice(0, W), slice(W, 2 * W))
 
     def put(j, value):
@@ -221,19 +248,31 @@
     def get(j):
         return stage[0, j], stage[1, j]
 
-    for j, pair in enumerate(pairs):
-        reals = [probe[m, 0] * obj_real - probe[m, 1] * obj_imag for m in pair]
-        imags = [probe[m, 0] * obj_imag + probe[m, 1] * obj_real for m in pair]
-        put(j, jnp.concatenate([jnp.concatenate(reals, 1), jnp.concatenate(imags, 1)], 0))
-    for j in range(MODES // 2):
-        put(j, turn(three(mm, lefts, get(j))))
+    lines = []
+    for m in [m for pair in pairs for m in pair]:
+        p_real, p_imag = band_probe[m, 0], band_probe[m, 1]
+        lines.append(
+            jnp.concatenate(
+                [p_real * band_real - p_imag * band_imag, p_real * band_imag + p_imag * band_real], 1
+            )
+        )
+    lines = three(mm, split(jnp.concatenate(lines, 0)), rights)
     intensity = jnp.zeros((W, W), F32)
     for j in range(MODES // 2):
-        waves = three(mm, get(j), rights)
-        far[j] = waves
-        power = waves * waves
+        one, two = (lines[2 * ROWS * j + ROWS * i : 2 * ROWS * j + ROWS * (i + 1)] for i in range(2))
+        both = jnp.concatenate(
+            [jnp.concatenate([one[:, :W], two[:, :W]], 1), jnp.concatenate([one[:, W:], two[:, W:]], 1)], 0
+        )
+        high, low = split(both)
+        blank = jnp.zeros((2 * ROWS, 2 * W), BF16)
+        total = waves[j] + turn(mm(band_dft[...], jnp.concatenate([high, low, high, blank], 0)))
+        far[j] = total
+        power = total * total
         power = power[:W] + power[W:]
         intensity = intensity + (power[:, :W] + power[:, W:])
+    pad = jnp.zeros((W - ROWS, W), F32)
+    obj_real = pltpu.roll(jnp.concatenate([band_real, pad], 0), -row, 0) + 1.0
+    obj_imag = pltpu.roll(jnp.concatenate([band_imag, pad], 0), -row, 0)
     factor = (1.0 - jnp.sqrt(measured[0, 0] + 1.0) / jnp.sqrt(intensity + 1.0)) * (1.0 / W)
     factors = jnp.concatenate([jnp.concatenate([factor, factor], 1)] * 2, 0)
     for j in range(MODES // 2):
@@ -441,11 +480,11 @@
     result = pl.pallas_call(
         kernel,
         in_specs=[
-            pl.BlockSpec(memory_space=pltpu.SMEM if a.shape == (1,) else pltpu.VMEM) for a in args
+            pl.BlockSpec(memory_space=pltpu.SMEM if a.dtype == jnp.int32 else pltpu.VMEM) for a in args
         ],
         out_specs=[pl.BlockSpec(memory_space=pltpu.VMEM)] * (len(outs) - far)
         + [pl.BlockSpec(memory_space=pl.ANY)] * far,
-        out_shape=[jax.ShapeDtypeStruct(o, F32) for o in outs],
+        out_shape=[jax.ShapeDtypeStruct(*o) if o[-1] == BF16 else jax.ShapeDtypeStruct(o, F32) for o in outs],
         scratch_shapes=scratch,
         compiler_params=pltpu.CompilerParams(vmem_limit_bytes=32 * 1024 * 1024),
         cost_estimate=pl.CostEstimate(flops=3 * 10**9, bytes_accessed=4 * 10**6, transcendentals=0),
@@ -473,14 +512,20 @@
     beams = [jnp.asarray(b) for b in phase_tables()[2]]
     row = forward_call(angle_index, volume, dft, dft_t, factors, all_beams, edges)
     whole = exchange(row.reshape(ROWS, 4, W), GZ).reshape(4 * ROWS, W)
+    split_modes = pltpu.VMEM((2, MODES // 2, 2 * W, 2 * W), BF16)
+    waves, band_dft, band_probe = vmem_call(
+        prepare_kernel,
+        [(MODES // 2, 2 * W, 2 * W), ((2 * W, 2 * W), BF16), (MODES, 2, ROWS, W)],
+        [split_modes],
+        "prepare",
+        row_offset,
+        probe,
+        dfts,
+    )
     keep, send = vmem_call(
         window_kernel,
         [(HALF + 24, W)] * 2,
-        [
-            pltpu.VMEM((2, MODES // 2, 2 * W, 2 * W), BF16),
-            pltpu.VMEM((MODES // 2, 2 * W, 2 * W), F32),
-            pltpu.VMEM((ROWS, W), F32),
-        ],
+        [split_modes, pltpu.VMEM((MODES // 2, 2 * W, 2 * W), F32), pltpu.VMEM((ROWS, W), F32)],
         "window",
         row_offset,
         col_offset,
@@ -488,6 +533,9 @@
         probe,
         measured,
         dfts,
+        waves,
+        band_dft,
+        band_probe,
     )
     packed = vmem_call(pack_kernel, [(16 * MESSAGE, W)], [], "pack", angle_index, keep, swap(send))
     shared = exchange(packed.reshape(16, MESSAGE, 1, W), PLANE).reshape(16 * MESSAGE, W)

time: 89.8 us -> 89.4 us (level)
  waiting for transfers between devices: 8.41 us -> 7.29 us
    all_to_all x1, waiting for transfers between devices: 6.78 us -> 5.66 us  [exchange(): return lax.all_to_all(blocks, axes, split_axis=0, concat_axis=0, tiled=True)]
    pallas_call x5 -> x6, Pallas kernels: 7.25 us -> 7.88 us  [vmem_call(): pl.pallas_call(kernel, in_specs=[pl.BlockSpec(memory_space=pltpu.SMEM if...]
  transfers between devices with their start and end apart: 3 -> 3, of which waited for: 3 -> 3; matrix products, arithmetic and copies ran while one was open for 0% -> 0% of each run, Pallas kernels for 2% -> 3%
where the time goes in v5:
time: 89.4 us; the launch traced here: 89.1 us
  blocking collectives  49.8 us (56%)
  starting transfers between devices  15.8 us (18%)
  Pallas kernels  12.4 us (14%)
  waiting for transfers between devices  7.29 us (8%)
  between operations  2.75 us (3%)
  local copies, waits for them, and re-layouts  0.94 us (1%)
    all_to_all x3, blocking collectives, exchange(): return lax.all_to_all(blocks, axes, split_axis=0, concat_axis=0, tiled=True)  49.8 us
    all_to_all x1, starting transfers between devices, exchange(): return lax.all_to_all(blocks, axes, split_axis=0, concat_axis=0, tiled=True)  11.1 us
    pallas_call x6, Pallas kernels, vmem_call(): pl.pallas_call(kernel, in_specs=[pl.BlockSpec(memory_space=pltpu.SMEM if...  7.88 us
    all_to_all x1, waiting for transfers between devices, exchange(): return lax.all_to_all(blocks, axes, split_axis=0, concat_axis=0, tiled=True)  5.66 us
    ppermute x2, starting transfers between devices, swap(): return lax.ppermute(rows, 'core', [(0, 1), (1, 0)])  4.78 us
    pallas_call x1, Pallas kernels, forward_call(): pl.pallas_call(forward_kernel, in_specs=[pl.BlockSpec(memory_space=pltpu....  4.54 us
  transfers between devices with their start and end apart: 3, of which 3 were waited for; matrix products, arithmetic and copies ran while one was open for 0% of the time, Pallas kernels for 3%

profile of v5, /device:TPU:1, one launch (start us, length us, event | category | flops | bytes accessed | tf_op | source)
XLA Modules:
  0.0 89.1 jit_solution(523481490078633130)
XLA Ops:
  1.3 0.0 copy-start
  1.3 0.0 copy-start.8
  1.3 4.5 %forward.1 = f32[128,128]{1,0:T(8,128)} custom-call(s32[1]{0:T(128)S(6)} %copy.22.sc, bf16[1,512,512]{2,1,0:T(8,128)(2,1)} %volume.1, bf16[2,512,512]{2,1,0:T(8,128)(2,1)} %constant.35.clone.dft_hbm, bf16[2,512,512]{2,1,0:T(8,128)(2,1)} %constant.36.clone.dft_t_hbm.dft_t, f32[8,88,512]{2,1,0:T(8,128)} %constant.38.clone.factors_hbm, ...), custom_call_target="tpu_custom_call" | custom-call | flops 4000000000 | bytes 4000000 | tf_op jit(solution)/shard_map/forward/pallas_call | solution.py:456
  5.8 11.1 %all-to-all-start = ((f32[32,4,128]{2,1,0:T(4,128)}), f32[32,4,128]{2,1,0:T(4,128)S(1)}, u32[]{:S(2)}, u32[]{:S(2)}) async-start(f32[32,4,128]{2,1,0:T(4,128)} %bitcast.10), calls=%async_computation | async-start | bytes 131072 | tf_op jit(solution)/shard_map/all_to_all | solution.py:501
  17.6 0.0 copy-done
  17.6 0.0 copy-done.8
  17.6 0.0 copy-start.1
  17.6 1.1 %prepare.1 = (f32[4,256,256]{2,1,0:T(8,128)S(1)}, bf16[256,256]{1,0:T(8,128)(2,1)S(1)}, f32[8,2,32,128]{3,2,1,0:T(8,128)S(1)}) custom-call(s32[1,1]{1,0:T(1,128)S(6)} %copy.23.row_ref, f32[8,2,128,128]{3,2,1,0:T(8,128)S(1)} %copy-done, bf16[2,2,256,256]{3,2,1,0:T(8,128)(2,1)S(1)} %copy-done.8), custom_call_target="tpu_custom_call" | custom-call | flops 3000000000 | bytes 4000000 | tf_op jit(solution)/shard_map/prepare/pallas_call | solution.py:480
  19.3 5.7 %all-to-all-done = f32[32,4,128]{2,1,0:T(4,128)S(1)} async-done(((f32[32,4,128]{2,1,0:T(4,128)}), f32[32,4,128]{2,1,0:T(4,128)S(1)}, u32[]{:S(2)}, u32[]{:S(2)}) %all-to-all-start) | async-done | bytes 65568 | tf_op jit(solution)/shard_map/all_to_all | solution.py:501
  25.0 0.0 copy-done.1
  25.0 2.1 %window.1 = (f32[1048,128]{1,0:T(8,128)S(1)}, f32[1048,128]{1,0:T(8,128)S(1)}) custom-call(s32[1,1]{1,0:T(1,128)S(6)} %copy.23.row_ref, s32[1,1]{1,0:T(1,128)S(6)} %copy.24.col_ref, f32[128,128]{1,0:T(8,128)S(1)} %bitcast.9, f32[8,2,128,128]{3,2,1,0:T(8,128)S(1)} %copy-done, f32[1,1,128,128]{3,2,1,0:T(8,128)S(1)} %copy-done.1, ...), custom_call_target="tpu_custom_call" | custom-call | flops 3000000000 | bytes 4000000 | tf_op jit(solution)/shard_map/window/pallas_call | solution.py:480
  27.0 1.3 %collective-permute-start = (f32[1048,128]{1,0:T(8,128)S(1)}, f32[1048,128]{1,0:T(8,128)S(1)}, u32[]{:S(2)}, u32[]{:S(2)}) collective-permute-start(f32[1048,128]{1,0:T(8,128)S(1)} %get-tuple-element.13), channel_id=1, source_target_pairs={{0,1},{1,0},{2,3},{3,2},{4,5},{5,4},{6,7},{7,6},{8,9},{9,8},{10,11... | collective-permute-start | bytes 1609736 | tf_op jit(solution)/shard_map/ppermute | solution.py:505
  28.4 1.6 %collective-permute-done.other = f32[1048,128]{1,0:T(8,128)S(1)} collective-permute-done((f32[1048,128]{1,0:T(8,128)S(1)}, f32[1048,128]{1,0:T(8,128)S(1)}, u32[]{:S(2)}, u32[]{:S(2)}) %collective-permute-start) | collective-permute-done | bytes 536608 | tf_op jit(solution)/shard_map/ppermute | solution.py:505
  29.9 0.1 pack.1
  30.0 18.8 %all_to_all.20 = f32[16,81,1,128]{3,2,1,0:T(1,128)S(1)} all-to-all(f32[16,81,1,128]{3,2,1,0:T(1,128)S(1)} %bitcast.7), channel_id=1, replica_groups=mesh['y'=4,'xh'=2,'xl'=2,'z'=8,'core'=2] {'y','xh','xl'}, dimensions={0} | all-to-all | bytes 1327104 | tf_op jit(solution)/shard_map/all_to_all | solution.py:501
  48.8 0.0 copy-start.2
  48.8 0.0 copy-start.3
  48.8 0.0 copy-start.4
  48.8 0.0 copy-start.5
  48.8 0.0 copy-start.6
  48.8 0.0 copy-start.7
  48.8 0.0 copy-start.9
  48.8 0.0 copy-start.10
  48.8 0.6 relay.1
  49.4 15.6 %all_to_all.21.received = f32[8,96,128]{2,1,0:T(8,128)S(1)} all-to-all(f32[8,96,128]{2,1,0:T(8,128)S(1)} %relay.1), channel_id=1, replica_groups=mesh['y'=4,'xh'=2,'xl'=2,'z'=8,'core'=2] {'z'}, dimensions={0} | all-to-all | bytes 786432 | tf_op jit(solution)/shard_map/all_to_all | solution.py:501
  65.0 0.0 copy-done.2
  65.0 0.0 copy-done.3
  65.0 0.0 copy-done.4
  65.0 0.0 copy-done.5
  65.0 0.0 copy-done.6
  65.1 0.0 copy-done.7
  65.1 0.0 copy-done.9
  65.1 0.0 copy-done.10
  65.1 2.6 %adjoint.1 = f32[16,96,128]{2,1,0:T(8,128)S(1)} custom-call(f32[8,96,128]{2,1,0:T(8,128)S(1)} %all_to_all.21.received, bf16[2,512,512]{2,1,0:T(8,128)(2,1)S(1)} %copy-done.2, f32[4,2,72,256]{3,2,1,0:T(8,128)S(1)} %copy-done.3, f32[4,8,256]{2,1,0:T(8,128)S(1)} %copy-done.9, f32[16,256]{1,0:T(8,128)S(1)} %copy-done.10, bf16[2,512,256]{2,1,0:T(8,128)(2,1)S(1)} %copy-done.7, ...), custom_call_target="tpu_custom_call" | custom-call | flops 3000000000 | bytes 4000000 | tf_op jit(solution)/shard_map/adjoint/pallas_call | solution.py:480
  67.7 15.5 %all_to_all.22.received = f32[16,96,128]{2,1,0:T(8,128)S(1)} all-to-all(f32[16,96,128]{2,1,0:T(8,128)S(1)} %adjoint.1), channel_id=1, replica_groups=mesh['y'=4,'xh'=2,'xl'=2,'z'=8,'core'=2] {'y','xh','xl'}, dimensions={0} | all-to-all | bytes 1572864 | tf_op jit(solution)/shard_map/all_to_all | solution.py:501
  83.2 3.5 %collective-permute-start.1 = (f32[16,64,128]{2,1,0:T(8,128)S(1)}, f32[16,64,128]{2,1,0:T(8,128)S(1)}, u32[]{:S(2)}, u32[]{:S(2)}) collective-permute-start(f32[16,64,128]{2,1,0:T(8,128)S(1)} %slice.4), channel_id=1, source_target_pairs={{0,1},{1,0},{2,3},{3,2},{4,5},{5,4},{6,7},{7,6},{8,9},{9,8},{10,11... | collective-permute-start | bytes 1572872 | tf_op jit(solution)/shard_map/ppermute | solution.py:505
  86.7 1.5 %assemble.1 = (f32[1,64,512]{2,1,0:T(8,128)}, f32[2,16,64,128]{3,2,1,0:T(8,128)}) custom-call(f32[16,96,128]{2,1,0:T(8,128)S(1)} %all_to_all.22.received), custom_call_target="tpu_custom_call" | custom-call | flops 3000000000 | bytes 4000000 | tf_op jit(solution)/shard_map/assemble/pallas_call | solution.py:480
  88.2 0.1 collective-permute-done.1
  88.2 0.8 bitcast_dynamic-update-slice_fusion
  (1 shorter events, 0.0 us)
Async XLA Ops:
  1.3 16.3 %copy-start = (f32[8,2,128,128]{3,2,1,0:T(8,128)S(1)}, f32[8,2,128,128]{3,2,1,0:T(8,128)}, u32[]{:S(2)}) copy-start(f32[8,2,128,128]{3,2,1,0:T(8,128)} %probe.3) | copy-start | bytes 3145732
  1.3 16.3 %copy-start.8 = (bf16[2,2,256,256]{3,2,1,0:T(8,128)(2,1)S(1)}, bf16[2,2,256,256]{3,2,1,0:T(8,128)(2,1)}, u32[]{:S(2)}) copy-start(bf16[2,2,256,256]{3,2,1,0:T(8,128)(2,1)} %constant.37.clone.dfts) | copy-start | bytes 1572868
  5.8 19.1 %all-to-all-start = ((f32[32,4,128]{2,1,0:T(4,128)}), f32[32,4,128]{2,1,0:T(4,128)S(1)}, u32[]{:S(2)}, u32[]{:S(2)}) async-start(f32[32,4,128]{2,1,0:T(4,128)} %bitcast.10), calls=%async_computation | async-start | bytes 131072 | tf_op jit(solution)/shard_map/all_to_all | solution.py:501
  17.6 7.4 %copy-start.1 = (f32[1,1,128,128]{3,2,1,0:T(8,128)S(1)}, f32[1,1,128,128]{3,2,1,0:T(8,128)}, u32[]{:S(2)}) copy-start(f32[1,1,128,128]{3,2,1,0:T(8,128)} %measured.1) | copy-start | bytes 196612
  27.0 2.9 %collective-permute-start = (f32[1048,128]{1,0:T(8,128)S(1)}, f32[1048,128]{1,0:T(8,128)S(1)}, u32[]{:S(2)}, u32[]{:S(2)}) collective-permute-start(f32[1048,128]{1,0:T(8,128)S(1)} %get-tuple-element.13), channel_id=1, source_target_pairs={{0,1},{1,0},{2,3},{3,2},{4,5},{5,4},{6,7},{7,6},{8,9},{9,8},{10,11... | collective-permute-start | bytes 1609736 | tf_op jit(solution)/shard_map/ppermute | solution.py:505
  48.8 16.3 %copy-start.2 = (bf16[2,512,512]{2,1,0:T(8,128)(2,1)S(1)}, bf16[2,512,512]{2,1,0:T(8,128)(2,1)}, u32[]{:S(2)}) copy-start(bf16[2,512,512]{2,1,0:T(8,128)(2,1)} %constant.36.clone.dft_t_hbm.dft_t) | copy-start | bytes 3145732
  48.8 16.3 %copy-start.3 = (f32[4,2,72,256]{3,2,1,0:T(8,128)S(1)}, f32[4,2,72,256]{3,2,1,0:T(8,128)}, u32[]{:S(2)}) copy-start(f32[4,2,72,256]{3,2,1,0:T(8,128)} %constant.39.clone.rows_tables) | copy-start | bytes 1769476
  48.8 16.3 %copy-start.4 = (bf16[2,512,256]{2,1,0:T(8,128)(2,1)S(1)}, bf16[2,512,256]{2,1,0:T(8,128)(2,1)}, u32[]{:S(2)}) copy-start(bf16[2,512,256]{2,1,0:T(8,128)(2,1)} %constant.46.clone.refs_3_) | copy-start | bytes 1572868
  48.8 16.3 %copy-start.5 = (bf16[2,512,256]{2,1,0:T(8,128)(2,1)S(1)}, bf16[2,512,256]{2,1,0:T(8,128)(2,1)}, u32[]{:S(2)}) copy-start(bf16[2,512,256]{2,1,0:T(8,128)(2,1)} %constant.45.clone.refs_2_) | copy-start | bytes 1572868
  48.8 16.3 %copy-start.6 = (bf16[2,512,256]{2,1,0:T(8,128)(2,1)S(1)}, bf16[2,512,256]{2,1,0:T(8,128)(2,1)}, u32[]{:S(2)}) copy-start(bf16[2,512,256]{2,1,0:T(8,128)(2,1)} %constant.44.clone.refs_1_) | copy-start | bytes 1572868
  48.8 16.3 %copy-start.7 = (bf16[2,512,256]{2,1,0:T(8,128)(2,1)S(1)}, bf16[2,512,256]{2,1,0:T(8,128)(2,1)}, u32[]{:S(2)}) copy-start(bf16[2,512,256]{2,1,0:T(8,128)(2,1)} %constant.43.clone.refs_0_) | copy-start | bytes 1572868
  48.8 16.3 %copy-start.9 = (f32[4,8,256]{2,1,0:T(8,128)S(1)}, f32[4,8,256]{2,1,0:T(8,128)}, u32[]{:S(2)}) copy-start(f32[4,8,256]{2,1,0:T(8,128)} %constant.41.clone.edges_hbm.edges) | copy-start | bytes 98308
  48.8 16.3 %copy-start.10 = (f32[16,256]{1,0:T(8,128)S(1)}, f32[16,256]{1,0:T(8,128)}, u32[]{:S(2)}) copy-start(f32[16,256]{1,0:T(8,128)} %constant.42.clone.middles) | copy-start | bytes 49156
  83.2 5.0 %collective-permute-start.1 = (f32[16,64,128]{2,1,0:T(8,128)S(1)}, f32[16,64,128]{2,1,0:T(8,128)S(1)}, u32[]{:S(2)}, u32[]{:S(2)}) collective-permute-start(f32[16,64,128]{2,1,0:T(8,128)S(1)} %slice.4), channel_id=1, source_target_pairs={{0,1},{1,0},{2,3},{3,2},{4,5},{5,4},{6,7},{7,6},{8,9},{9,8},{10,11... | collective-permute-start | bytes 1572872 | tf_op jit(solution)/shard_map/ppermute | solution.py:505

commit v6 on v5

--- a/solution.py
+++ b/solution.py
@@ -33,7 +33,8 @@
     turns = np.pi / N * (k * (2 * n + 1) % (2 * N))
     table = np.concatenate([np.cos(turns), -np.sin(turns)], 0)
     table[H] = 2.0 * (np.arange(N) % 2) - 1.0
-    return split_const(table), split_const(np.ascontiguousarray(table.T))
+    order = np.arange(N).reshape(2, 4, 2, 32).transpose(0, 2, 1, 3).reshape(N)
+    return [split_const(np.ascontiguousarray(t)) for t in (table, table.T, table[:, order])]
 
 
 def window_tables():
@@ -135,7 +136,8 @@
     moves[1].wait()
     moves[2].wait()
     for lanes, columns in zip(halves, (slab[:, :H], backward)):
-        spec[:, lanes] = mm(dft[0], columns) + mm(dft[1], columns)
+        both = mm(jnp.concatenate([dft[0], dft[1]], 0), columns)
+        spec[:, lanes] = both[:N] + both[N:]
     half_row = jnp.where(lax.broadcasted_iota(jnp.int32, (8, H), 0) == 0, 0.5, 1.0)
     for lanes in halves:
         cb, sb = factors[64:72, lanes], factors[72:80, lanes]
@@ -154,40 +156,49 @@
                 at = slice(base, base + 16)
                 turned[0, at, lanes], turned[1, at, lanes] = split(jnp.concatenate(parts, 0))
     moves[3].wait()
-    for part, comps in enumerate(halves):
-        both = three(mm, (dft_t[0, :, comps], dft_t[1, :, comps]), (turned[0, comps, :], turned[1, comps, :]))
-        field[0, 0, comps, :], field[0, 1, comps, :] = split(both[:, :H] + both[:, H:])
-        field[1, 0, comps, :], field[1, 1, comps, :] = split(both[:, :H] - both[:, H:])
-    for part, comps in enumerate(halves):
-        spec[comps, :] = three(mm_t, (dft[0, comps, :H], dft[1, comps, :H]), (field[part, 0], field[part, 1]))
+    for comps in halves:
+        for t in range(2):
+            near, far = slice(t * W, (t + 1) * W), slice(H + t * W, H + (t + 1) * W)
+            both = three(
+                mm,
+                (dft_t[0, :, comps], dft_t[1, :, comps]),
+                [jnp.concatenate([turned[p, comps, near], turned[p, comps, far]], 1) for p in range(2)],
+            )
+            field[0, 0, comps, near], field[0, 1, comps, near] = split(both[:, :W] + both[:, W:])
+            field[1, 0, comps, near], field[1, 1, comps, near] = split(both[:, :W] - both[:, W:])
     moves[4].wait()
     moves[5].wait()
+    c = beams[0, :H, :].astype(F32) + beams[1, :H, :].astype(F32)
+    s = beams[0, H:, :].astype(F32) + beams[1, H:, :].astype(F32)
+    top = lax.broadcasted_iota(jnp.int32, (8, H), 0) == 0
+    c_imag = jnp.concatenate([jnp.where(top, edges[:1, :], c[:8]), c[8:]], 0)
+    s_imag = jnp.concatenate([jnp.where(top, 0.0, s[:8]), s[8:]], 0) * sign
+
+    def fold(value):
+        return value[:, :W] + value[:, W:]
+
+    def beam(part, rows):
+        comps = halves[part]
+        return three(mm_t, (dft[0, comps, :H], dft[1, comps, :H]), (field[part, 0, rows], field[part, 1, rows]))
+
+    real = fold(beam(0, halves[0]) * c)
+    imag = fold(beam(1, halves[0]) * c_imag)
+    odd = beam(1, halves[1])
+    real = real + fold(odd * s_imag)
+    extra = jnp.where(top[:, :W], fold(odd[:8] * s[:8]), 0.0)
+    imag = imag - fold(beam(0, halves[1]) * s_imag)
+    imag = jnp.concatenate([imag[:8] + extra, imag[8:]], 0)
+    real, imag = jnp.sum(real, axis=1, keepdims=True), jnp.sum(imag, axis=1, keepdims=True)
+    weight = jnp.where(lax.broadcasted_iota(jnp.int32, (H, 1), 0) == 0, 0.5, 1.0)
+    real, imag = real * weight, imag * weight
+    c_mid, s_mid = c[:, H - 1 :], s_imag[:, H - 1 :]
+    real, imag = real * c_mid + imag * s_mid, imag * c_mid - real * s_mid
     total = jnp.zeros((8, N), F32)
     for r in range(0, H, 32):
-        real_even, real_odd = spec[r : r + 32, :H], spec[r : r + 32, H:]
-        imag_even, imag_odd = spec[H + r : H + r + 32, :H], spec[H + r : H + r + 32, H:]
-        c = beams[0, r : r + 32, :].astype(F32) + beams[1, r : r + 32, :].astype(F32)
-        s = beams[0, H + r : H + r + 32, :].astype(F32) + beams[1, H + r : H + r + 32, :].astype(F32)
-        c_imag, s_imag, extra = c, s * sign, None
-        if r == 0:
-            top = lax.broadcasted_iota(jnp.int32, (32, H), 0) == 0
-            extra = jnp.where(top, imag_odd * s, 0.0)
-            c_imag = jnp.where(top, edges[0:1, :], c)
-            s_imag = jnp.where(top, 0.0, s_imag)
-        real_terms = real_even * c + imag_odd * s_imag
-        imag_terms = imag_even * c_imag - real_odd * s_imag
-        if extra is not None:
-            imag_terms = imag_terms + extra
-        real = jnp.sum(real_terms, axis=1, keepdims=True)
-        imag = jnp.sum(imag_terms, axis=1, keepdims=True)
-        if r == 0:
-            weight = jnp.where(lax.broadcasted_iota(jnp.int32, (32, 1), 0) == 0, 0.5, 1.0)
-            real, imag = real * weight, imag * weight
-        c_mid, s_mid = c[:, H - 1 :], s_imag[:, H - 1 :]
-        real, imag = real * c_mid + imag * s_mid, imag * c_mid - real * s_mid
-        f_real = dft[0, r : r + 32, :].astype(F32) + dft[1, r : r + 32, :].astype(F32)
-        f_imag = dft[0, H + r : H + r + 32, :].astype(F32) + dft[1, H + r : H + r + 32, :].astype(F32)
-        terms = real * f_real + imag * f_imag
+        at, below = slice(r, r + 32), slice(H + r, H + r + 32)
+        f_real = dft[0, at, :].astype(F32) + dft[1, at, :].astype(F32)
+        f_imag = dft[0, below, :].astype(F32) + dft[1, below, :].astype(F32)
+        terms = real[at] * f_real + imag[at] * f_imag
         total = total + jnp.sum(terms.reshape(4, 8, N), axis=0)
     row = jnp.sum(total, axis=0, keepdims=True) * (8.0 / (N * N))
     for t in range(4):
@@ -295,7 +306,7 @@
             send[at, :] = jnp.where(core == 0, grads[1][part], grads[0][part])
     patch = grad_imag * obj_real - grad_real * obj_imag
     shown = pltpu.roll(patch, W + row, 0)[:ROWS]
-    pieces[...] = shown
+    pieces[...] = pltpu.roll(shown, lax.rem(col, W), 1)
     even, odd = pieces[pl.ds(0, 16, stride=2), :], pieces[pl.ds(1, 16, stride=2), :]
     keep[HALF : HALF + 16, :] = jnp.where(core == 0, even, odd)
     send[HALF : HALF + 16, :] = jnp.where(core == 0, odd, even)
@@ -337,8 +348,6 @@
     columns = jnp.concatenate(
         [jnp.broadcast_to(numbers[1 + i, p : p + 1, :], (8, W)) for p, i in windows], 0
     ).astype(jnp.int32)
-    for bit in range(7):
-        rows = jnp.where(columns & (1 << bit) != 0, pltpu.roll(rows, 1 << bit, 1), rows)
     lane = lax.broadcasted_iota(jnp.int32, rows.shape, 1)
     tiles = (columns >> 7) + jnp.where(lane < (columns & (W - 1)), 1, 0)
     for a in range(ANGLES):
@@ -353,7 +362,7 @@
         out[z, CHUNK:, :] = pieces[pl.ds(z, 32, stride=8), :]
 
 
-def adjoint_kernel(received, dft_t, rows_tables, edges, middles, *refs):
+def adjoint_kernel(received, dft_t, leaving, rows_tables, edges, middles, *refs):
     beams, (out, pieces, shifted, sheared) = refs[:PAIRS], refs[PAIRS:]
     block = 2 * lax.axis_index("y") + lax.axis_index("xh")
     total = received[0]
@@ -393,49 +402,39 @@
         even = even + jnp.concatenate(nyquist[2 * q : 2 * q + 2], 0) * edges[q, 0:1, :]
         sheared[0, at, :H], sheared[1, at, :H] = split(even)
         sheared[0, at, H:], sheared[1, at, H:] = split(odd)
-    spectrum = jnp.concatenate(
-        [
-            three(
-                mm, (sheared[0, :, part], sheared[1, :, part]), (dft_t[0, :H, part], dft_t[1, :H, part])
-            )
-            for part in (slice(0, H), slice(H, N))
-        ],
-        1,
-    )
     lane_first = lax.broadcasted_iota(jnp.int32, (8, H), 1) == 0
     sums = [None] * 8
     for q in range(PAIRS):
+        at = slice(2 * 64 * q, 2 * 64 * (q + 1))
+        real, imag = (
+            three(mm, (sheared[0, at, part], sheared[1, at, part]), (dft_t[0, :H, part], dft_t[1, :H, part]))
+            for part in (slice(0, H), slice(H, N))
+        )
         cb, sb = rows_tables[q, 0, 64:72, :], rows_tables[q, 1, 64:72, :]
         near = rows_tables[q, :, pl.ds(pl.multiple_of(8 * block, 8), 8), :]
         for u in range(8):
             ca, sa = near[0, u : u + 1, :], near[1, u : u + 1, :]
             c, s = ca * cb - sa * sb, sa * cb + ca * sb
             c_first, s_first = jnp.where(lane_first, 1.0, c), jnp.where(lane_first, 0.0, s)
-            base = 2 * 64 * q + 8 * u
-            one, two = spectrum[base : base + 8, :], spectrum[base + 64 : base + 72, :]
-            both, apart = one + two, one - two
+            one, two = slice(8 * u, 8 * u + 8), slice(64 + 8 * u, 72 + 8 * u)
             unturned = jnp.concatenate(
-                [both[:, :H] * c_first + apart[:, H:] * s_first, both[:, H:] * c - apart[:, :H] * s_first], 1
+                [
+                    (real[one] + real[two]) * c_first + (imag[one] - imag[two]) * s_first,
+                    (imag[one] + imag[two]) * c - (real[one] - real[two]) * s_first,
+                ],
+                1,
             )
             sums[u] = unturned if q == 0 else sums[u] + unturned
     weight = jnp.where(lax.broadcasted_iota(jnp.int32, (64, N), 1) % H == 0, 1.0 / 32.0, 1.0 / 16.0)
     whole = jnp.concatenate(sums, 0) * weight
-    zeros = jnp.zeros((64, N), BF16)
-    high, low = split(whole)
-    result = None
-    for side in range(2):
-        dft_rows = [
-            jnp.concatenate([dft_t[p, 64 * a + 32 * side : 64 * a + 32 * side + 32, :] for a in range(ANGLES)], 0)
-            for p in range(2)
-        ]
-        order = (lambda v: [v, zeros]) if side == 0 else (lambda v: [zeros, v])
-        columns = (jnp.concatenate(order(high), 0), jnp.concatenate(order(low), 0))
-        part = three(mm_t, dft_rows, columns)
-        result = part if result is None else result + part
-    for peer in range(16):
-        a = peer // 2
-        out[peer, :CHUNK, :] = chunk
-        out[peer, CHUNK:, :] = result[32 * a : 32 * a + 32, :]
+    columns = three(mm, split(whole), (leaving[0], leaving[1]))
+    for part in range(2):
+        first, second = (columns[:, (2 * part + i) * W : (2 * part + i + 1) * W] for i in range(2))
+        blocks = jnp.concatenate([first, second], 0).T
+        for peer in range(8 * part, 8 * part + 8):
+            out[peer, :CHUNK, :] = chunk
+            a = peer // 2 - 4 * part
+            out[peer, CHUNK:, :] = blocks[32 * a : 32 * a + 32, :]
 
 
 def assemble_kernel(received, out, probe_out, sem):
@@ -506,7 +505,7 @@
 
 
 def local(volume, probe, measured, angle_index, row_offset, col_offset):
-    dft, dft_t = (jnp.asarray(t) for t in dft_tables())
+    dft, dft_t, leaving = (jnp.asarray(t) for t in dft_tables())
     dfts = jnp.asarray(window_tables())
     factors, rows_tables, all_beams, edges, middles = (jnp.asarray(t) for t in phase_tables())
     beams = [jnp.asarray(b) for b in phase_tables()[2]]
@@ -548,6 +547,7 @@
         "adjoint",
         rows,
         dft_t,
+        leaving,
         rows_tables,
         edges,
         middles,

time: 89.4 us -> 88.2 us (0.987)
  Pallas kernels: 12.4 us -> 11.2 us
    pallas_call x6, Pallas kernels: 7.88 us -> 6.62 us  [vmem_call(): pl.pallas_call(kernel, in_specs=[pl.BlockSpec(memory_space=pltpu.SMEM if...]
where the time goes in v6:
time: 88.2 us; the launch traced here: 87.9 us
  blocking collectives  50 us (57%)
  starting transfers between devices  15.8 us (18%)
  Pallas kernels  11.2 us (13%)
  waiting for transfers between devices  7.28 us (8%)
  between operations  2.77 us (3%)
  local copies, waits for them, and re-layouts  0.94 us (1%)
    all_to_all x3, blocking collectives, exchange(): return lax.all_to_all(blocks, axes, split_axis=0, concat_axis=0, tiled=True)  50 us
    all_to_all x1, starting transfers between devices, exchange(): return lax.all_to_all(blocks, axes, split_axis=0, concat_axis=0, tiled=True)  11.1 us
    pallas_call x6, Pallas kernels, vmem_call(): pl.pallas_call(kernel, in_specs=[pl.BlockSpec(memory_space=pltpu.SMEM if...  6.62 us
    all_to_all x1, waiting for transfers between devices, exchange(): return lax.all_to_all(blocks, axes, split_axis=0, concat_axis=0, tiled=True)  5.65 us
    ppermute x2, starting transfers between devices, swap(): return lax.ppermute(rows, 'core', [(0, 1), (1, 0)])  4.73 us
    pallas_call x1, Pallas kernels, forward_call(): pl.pallas_call(forward_kernel, in_specs=[pl.BlockSpec(memory_space=pltpu....  4.56 us
  transfers between devices with their start and end apart: 3, of which 3 were waited for; matrix products, arithmetic and copies ran while one was open for 0% of the time, Pallas kernels for 3%

profile of v6, /device:TPU:1, one launch (start us, length us, event | category | flops | bytes accessed | tf_op | source)
XLA Modules:
  0.0 87.9 jit_solution(10299057978842198871)
XLA Ops:
  1.3 0.0 copy-start
  1.3 0.0 copy-start.9
  1.3 4.6 %forward.1 = f32[128,128]{1,0:T(8,128)} custom-call(s32[1]{0:T(128)S(6)} %copy.23.sc, bf16[1,512,512]{2,1,0:T(8,128)(2,1)} %volume.1, bf16[2,512,512]{2,1,0:T(8,128)(2,1)} %constant.37.clone.dft_hbm, bf16[2,512,512]{2,1,0:T(8,128)(2,1)} %constant.38.clone.dft_t_hbm.dft_t, f32[8,88,512]{2,1,0:T(8,128)} %constant.41.clone.factors_hbm, ...), custom_call_target="tpu_custom_call" | custom-call | flops 4000000000 | bytes 4000000 | tf_op jit(solution)/shard_map/forward/pallas_call | solution.py:455
  5.9 11.1 %all-to-all-start = ((f32[32,4,128]{2,1,0:T(4,128)}), f32[32,4,128]{2,1,0:T(4,128)S(1)}, u32[]{:S(2)}, u32[]{:S(2)}) async-start(f32[32,4,128]{2,1,0:T(4,128)} %bitcast.10), calls=%async_computation | async-start | bytes 131072 | tf_op jit(solution)/shard_map/all_to_all | solution.py:500
  17.6 0.0 copy-done
  17.6 0.0 copy-done.9
  17.6 0.0 copy-start.1
  17.6 1.1 %prepare.1 = (f32[4,256,256]{2,1,0:T(8,128)S(1)}, bf16[256,256]{1,0:T(8,128)(2,1)S(1)}, f32[8,2,32,128]{3,2,1,0:T(8,128)S(1)}) custom-call(s32[1,1]{1,0:T(1,128)S(6)} %copy.24.row_ref, f32[8,2,128,128]{3,2,1,0:T(8,128)S(1)} %copy-done, bf16[2,2,256,256]{3,2,1,0:T(8,128)(2,1)S(1)} %copy-done.9), custom_call_target="tpu_custom_call" | custom-call | flops 3000000000 | bytes 4000000 | tf_op jit(solution)/shard_map/prepare/pallas_call | solution.py:479
  19.4 5.6 %all-to-all-done = f32[32,4,128]{2,1,0:T(4,128)S(1)} async-done(((f32[32,4,128]{2,1,0:T(4,128)}), f32[32,4,128]{2,1,0:T(4,128)S(1)}, u32[]{:S(2)}, u32[]{:S(2)}) %all-to-all-start) | async-done | bytes 65568 | tf_op jit(solution)/shard_map/all_to_all | solution.py:500
  25.0 0.0 copy-done.1
  25.0 2.1 %window.1 = (f32[1048,128]{1,0:T(8,128)S(1)}, f32[1048,128]{1,0:T(8,128)S(1)}) custom-call(s32[1,1]{1,0:T(1,128)S(6)} %copy.24.row_ref, s32[1,1]{1,0:T(1,128)S(6)} %copy.25.col_ref, f32[128,128]{1,0:T(8,128)S(1)} %bitcast.9, f32[8,2,128,128]{3,2,1,0:T(8,128)S(1)} %copy-done, f32[1,1,128,128]{3,2,1,0:T(8,128)S(1)} %copy-done.1, ...), custom_call_target="tpu_custom_call" | custom-call | flops 3000000000 | bytes 4000000 | tf_op jit(solution)/shard_map/window/pallas_call | solution.py:479
  27.1 1.3 %collective-permute-start = (f32[1048,128]{1,0:T(8,128)S(1)}, f32[1048,128]{1,0:T(8,128)S(1)}, u32[]{:S(2)}, u32[]{:S(2)}) collective-permute-start(f32[1048,128]{1,0:T(8,128)S(1)} %get-tuple-element.13), channel_id=1, source_target_pairs={{0,1},{1,0},{2,3},{3,2},{4,5},{5,4},{6,7},{7,6},{8,9},{9,8},{10,11... | collective-permute-start | bytes 1609736 | tf_op jit(solution)/shard_map/ppermute | solution.py:504
  28.4 1.6 %collective-permute-done.other = f32[1048,128]{1,0:T(8,128)S(1)} collective-permute-done((f32[1048,128]{1,0:T(8,128)S(1)}, f32[1048,128]{1,0:T(8,128)S(1)}, u32[]{:S(2)}, u32[]{:S(2)}) %collective-permute-start) | collective-permute-done | bytes 536608 | tf_op jit(solution)/shard_map/ppermute | solution.py:504
  30.0 0.1 pack.1
  30.0 18.8 %all_to_all.20 = f32[16,81,1,128]{3,2,1,0:T(1,128)S(1)} all-to-all(f32[16,81,1,128]{3,2,1,0:T(1,128)S(1)} %bitcast.7), channel_id=1, replica_groups=mesh['y'=4,'xh'=2,'xl'=2,'z'=8,'core'=2] {'y','xh','xl'}, dimensions={0} | all-to-all | bytes 1327104 | tf_op jit(solution)/shard_map/all_to_all | solution.py:500
  48.8 0.0 copy-start.2
  48.8 0.0 copy-start.3
  48.8 0.0 copy-start.4
  48.8 0.0 copy-start.5
  48.8 0.0 copy-start.6
  48.8 0.0 copy-start.7
  48.8 0.0 copy-start.8
  48.8 0.0 copy-start.10
  48.8 0.0 copy-start.11
  48.9 0.3 relay.1
  49.1 15.7 %all_to_all.21.received = f32[8,96,128]{2,1,0:T(8,128)S(1)} all-to-all(f32[8,96,128]{2,1,0:T(8,128)S(1)} %relay.1), channel_id=1, replica_groups=mesh['y'=4,'xh'=2,'xl'=2,'z'=8,'core'=2] {'z'}, dimensions={0} | all-to-all | bytes 786432 | tf_op jit(solution)/shard_map/all_to_all | solution.py:500
  64.9 0.0 copy-done.2
  64.9 0.0 copy-done.3
  64.9 0.0 copy-done.4
  64.9 0.0 copy-done.5
  64.9 0.0 copy-done.6
  64.9 0.0 copy-done.7
  64.9 0.0 copy-done.8
  64.9 0.0 copy-done.10
  64.9 0.0 copy-done.11
  64.9 1.6 %adjoint.1 = f32[16,96,128]{2,1,0:T(8,128)S(1)} custom-call(f32[8,96,128]{2,1,0:T(8,128)S(1)} %all_to_all.21.received, bf16[2,512,512]{2,1,0:T(8,128)(2,1)S(1)} %copy-done.2, bf16[2,512,512]{2,1,0:T(8,128)(2,1)S(1)} %copy-done.3, f32[4,2,72,256]{3,2,1,0:T(8,128)S(1)} %copy-done.4, f32[4,8,256]{2,1,0:T(8,128)S(1)} %copy-done.10, f32[16,256]{1,0:T(8,128)S(1)} %copy-done.11, ...), custom_call_target="tpu_custom_call" | custom-call | flops 3000000000 | bytes 4000000 | tf_op jit(solution)/shard_map/adjoint/pallas_call | solution.py:479
  66.6 15.5 %all_to_all.22.received = f32[16,96,128]{2,1,0:T(8,128)S(1)} all-to-all(f32[16,96,128]{2,1,0:T(8,128)S(1)} %adjoint.1), channel_id=1, replica_groups=mesh['y'=4,'xh'=2,'xl'=2,'z'=8,'core'=2] {'y','xh','xl'}, dimensions={0} | all-to-all | bytes 1572864 | tf_op jit(solution)/shard_map/all_to_all | solution.py:500
  82.1 3.5 %collective-permute-start.1 = (f32[16,64,128]{2,1,0:T(8,128)S(1)}, f32[16,64,128]{2,1,0:T(8,128)S(1)}, u32[]{:S(2)}, u32[]{:S(2)}) collective-permute-start(f32[16,64,128]{2,1,0:T(8,128)S(1)} %slice.4), channel_id=1, source_target_pairs={{0,1},{1,0},{2,3},{3,2},{4,5},{5,4},{6,7},{7,6},{8,9},{9,8},{10,11... | collective-permute-start | bytes 1572872 | tf_op jit(solution)/shard_map/ppermute | solution.py:504
  85.6 1.5 %assemble.1 = (f32[1,64,512]{2,1,0:T(8,128)}, f32[2,16,64,128]{3,2,1,0:T(8,128)}) custom-call(f32[16,96,128]{2,1,0:T(8,128)S(1)} %all_to_all.22.received), custom_call_target="tpu_custom_call" | custom-call | flops 3000000000 | bytes 4000000 | tf_op jit(solution)/shard_map/assemble/pallas_call | solution.py:479
  87.0 0.1 collective-permute-done.1
  87.1 0.8 bitcast_dynamic-update-slice_fusion
  (1 shorter events, 0.0 us)
Async XLA Ops:
  1.3 16.3 %copy-start = (f32[8,2,128,128]{3,2,1,0:T(8,128)S(1)}, f32[8,2,128,128]{3,2,1,0:T(8,128)}, u32[]{:S(2)}) copy-start(f32[8,2,128,128]{3,2,1,0:T(8,128)} %probe.3) | copy-start | bytes 3145732
  1.3 16.3 %copy-start.9 = (bf16[2,2,256,256]{3,2,1,0:T(8,128)(2,1)S(1)}, bf16[2,2,256,256]{3,2,1,0:T(8,128)(2,1)}, u32[]{:S(2)}) copy-start(bf16[2,2,256,256]{3,2,1,0:T(8,128)(2,1)} %constant.40.clone.dfts) | copy-start | bytes 1572868
  5.9 19.1 %all-to-all-start = ((f32[32,4,128]{2,1,0:T(4,128)}), f32[32,4,128]{2,1,0:T(4,128)S(1)}, u32[]{:S(2)}, u32[]{:S(2)}) async-start(f32[32,4,128]{2,1,0:T(4,128)} %bitcast.10), calls=%async_computation | async-start | bytes 131072 | tf_op jit(solution)/shard_map/all_to_all | solution.py:500
  17.6 7.4 %copy-start.1 = (f32[1,1,128,128]{3,2,1,0:T(8,128)S(1)}, f32[1,1,128,128]{3,2,1,0:T(8,128)}, u32[]{:S(2)}) copy-start(f32[1,1,128,128]{3,2,1,0:T(8,128)} %measured.1) | copy-start | bytes 196612
  27.1 2.8 %collective-permute-start = (f32[1048,128]{1,0:T(8,128)S(1)}, f32[1048,128]{1,0:T(8,128)S(1)}, u32[]{:S(2)}, u32[]{:S(2)}) collective-permute-start(f32[1048,128]{1,0:T(8,128)S(1)} %get-tuple-element.13), channel_id=1, source_target_pairs={{0,1},{1,0},{2,3},{3,2},{4,5},{5,4},{6,7},{7,6},{8,9},{9,8},{10,11... | collective-permute-start | bytes 1609736 | tf_op jit(solution)/shard_map/ppermute | solution.py:504
  48.8 16.1 %copy-start.2 = (bf16[2,512,512]{2,1,0:T(8,128)(2,1)S(1)}, bf16[2,512,512]{2,1,0:T(8,128)(2,1)}, u32[]{:S(2)}) copy-start(bf16[2,512,512]{2,1,0:T(8,128)(2,1)} %constant.38.clone.dft_t_hbm.dft_t) | copy-start | bytes 3145732
  48.8 16.1 %copy-start.3 = (bf16[2,512,512]{2,1,0:T(8,128)(2,1)S(1)}, bf16[2,512,512]{2,1,0:T(8,128)(2,1)}, u32[]{:S(2)}) copy-start(bf16[2,512,512]{2,1,0:T(8,128)(2,1)} %constant.39.clone.leaving) | copy-start | bytes 3145732
  48.8 16.1 %copy-start.4 = (f32[4,2,72,256]{3,2,1,0:T(8,128)S(1)}, f32[4,2,72,256]{3,2,1,0:T(8,128)}, u32[]{:S(2)}) copy-start(f32[4,2,72,256]{3,2,1,0:T(8,128)} %constant.42.clone.rows_tables) | copy-start | bytes 1769476
  48.8 16.1 %copy-start.5 = (bf16[2,512,256]{2,1,0:T(8,128)(2,1)S(1)}, bf16[2,512,256]{2,1,0:T(8,128)(2,1)}, u32[]{:S(2)}) copy-start(bf16[2,512,256]{2,1,0:T(8,128)(2,1)} %constant.49.clone.refs_3_) | copy-start | bytes 1572868
  48.8 16.1 %copy-start.6 = (bf16[2,512,256]{2,1,0:T(8,128)(2,1)S(1)}, bf16[2,512,256]{2,1,0:T(8,128)(2,1)}, u32[]{:S(2)}) copy-start(bf16[2,512,256]{2,1,0:T(8,128)(2,1)} %constant.48.clone.refs_2_) | copy-start | bytes 1572868
  48.8 16.1 %copy-start.7 = (bf16[2,512,256]{2,1,0:T(8,128)(2,1)S(1)}, bf16[2,512,256]{2,1,0:T(8,128)(2,1)}, u32[]{:S(2)}) copy-start(bf16[2,512,256]{2,1,0:T(8,128)(2,1)} %constant.47.clone.refs_1_) | copy-start | bytes 1572868
  48.8 16.1 %copy-start.8 = (bf16[2,512,256]{2,1,0:T(8,128)(2,1)S(1)}, bf16[2,512,256]{2,1,0:T(8,128)(2,1)}, u32[]{:S(2)}) copy-start(bf16[2,512,256]{2,1,0:T(8,128)(2,1)} %constant.46.clone.refs_0_) | copy-start | bytes 1572868
  48.8 16.1 %copy-start.10 = (f32[4,8,256]{2,1,0:T(8,128)S(1)}, f32[4,8,256]{2,1,0:T(8,128)}, u32[]{:S(2)}) copy-start(f32[4,8,256]{2,1,0:T(8,128)} %constant.44.clone.edges_hbm.edges) | copy-start | bytes 98308
  48.8 16.1 %copy-start.11 = (f32[16,256]{1,0:T(8,128)S(1)}, f32[16,256]{1,0:T(8,128)}, u32[]{:S(2)}) copy-start(f32[16,256]{1,0:T(8,128)} %constant.45.clone.middles) | copy-start | bytes 49156
  82.1 5.0 %collective-permute-start.1 = (f32[16,64,128]{2,1,0:T(8,128)S(1)}, f32[16,64,128]{2,1,0:T(8,128)S(1)}, u32[]{:S(2)}, u32[]{:S(2)}) collective-permute-start(f32[16,64,128]{2,1,0:T(8,128)S(1)} %slice.4), channel_id=1, source_target_pairs={{0,1},{1,0},{2,3},{3,2},{4,5},{5,4},{6,7},{7,6},{8,9},{9,8},{10,11... | collective-permute-start | bytes 1572872 | tf_op jit(solution)/shard_map/ppermute | solution.py:504

commit v7 on v6

--- a/solution.py
+++ b/solution.py
@@ -17,7 +17,8 @@
 ROWS = 32
 HALF = MODES * 2 * W // 2
 CHUNK = HALF // 16
-MESSAGE = CHUNK + 17
+PART = CHUNK // 2
+MESSAGE = PART + 9
 F32 = jnp.float32
 BF16 = jnp.bfloat16
 
@@ -319,57 +320,58 @@
     lane = lax.broadcasted_iota(jnp.int32, (1, W), 1)
     first, second = keep[HALF + 16 : HALF + 17, :], other[HALF + 16 : HALF + 17, :]
     numbers = jnp.where(lane < 32, sc[0].astype(F32), jnp.where(lane < 64, first, second))
-    for peer in range(16):
-        rows = slice(CHUNK * peer, CHUNK * (peer + 1))
+    for peer in range(32):
+        rows = slice(PART * peer, PART * (peer + 1))
         at = MESSAGE * peer
-        out[at : at + CHUNK, :] = keep[rows, :] + other[rows, :]
-        rows = slice(HALF + 8 * (peer % 2), HALF + 8 * (peer % 2) + 8)
-        out[at + CHUNK : at + CHUNK + 8, :] = keep[rows, :]
-        out[at + CHUNK + 8 : at + CHUNK + 16, :] = other[rows, :]
-        out[at + CHUNK + 16 : at + MESSAGE, :] = numbers
+        out[at : at + PART, :] = keep[rows, :] + other[rows, :]
+        rows = pl.ds(HALF + 8 * (peer // 2 % 2) + peer % 2, 4, stride=2)
+        out[at + PART : at + PART + 4, :] = keep[rows, :]
+        out[at + PART + 4 : at + PART + 8, :] = other[rows, :]
+        out[at + PART + 8 : at + MESSAGE, :] = numbers
 
 
 def relay_kernel(received, out, pieces, numbers):
-    total = received[:CHUNK, :]
-    for peer in range(1, 16):
-        total = total + received[MESSAGE * peer : MESSAGE * peer + CHUNK, :]
-    heads = jnp.concatenate([received[pl.ds(MESSAGE * p + MESSAGE - 1, 1), :] for p in range(16)], 0)
+    total = received[:PART, :]
+    for peer in range(1, 32):
+        total = total + received[MESSAGE * peer : MESSAGE * peer + PART, :]
+    heads = jnp.concatenate([received[pl.ds(MESSAGE * p + MESSAGE - 1, 1), :] for p in range(32)], 0)
     rolls = [heads] + [pltpu.roll(heads, 32 * i, 1) for i in (1, 2, 3)]
-    quarter = lax.broadcasted_iota(jnp.int32, (16, W), 1) // 32
+    quarter = lax.broadcasted_iota(jnp.int32, (32, W), 1) // 32
     for i in range(3):
         value = rolls[0]
         for shift in (1, 2, 3):
             value = jnp.where(quarter == (i + shift) % 4, rolls[shift], value)
         numbers[i] = value
-    windows = [(peer, side) for peer in range(16) for side in range(2)]
-    rows = jnp.concatenate(
-        [received[MESSAGE * p + CHUNK + 8 * i : MESSAGE * p + CHUNK + 8 * i + 8, :] for p, i in windows], 0
-    )
-    columns = jnp.concatenate(
-        [jnp.broadcast_to(numbers[1 + i, p : p + 1, :], (8, W)) for p, i in windows], 0
-    ).astype(jnp.int32)
+    rows = jnp.concatenate([received[MESSAGE * p + PART : MESSAGE * p + PART + 8, :] for p in range(32)], 0)
+    first, second = (
+        jnp.concatenate([jnp.broadcast_to(numbers[1 + i, p : p + 1, :], (8, W)) for p in range(32)], 0)
+        for i in range(2)
+    )
+    row = lax.broadcasted_iota(jnp.int32, rows.shape, 0)
+    columns = jnp.where(row % 8 < 4, first, second).astype(jnp.int32)
     lane = lax.broadcasted_iota(jnp.int32, rows.shape, 1)
     tiles = (columns >> 7) + jnp.where(lane < (columns & (W - 1)), 1, 0)
     for a in range(ANGLES):
-        angle = jnp.max(numbers[0, 2 * a : 2 * a + 1, :]).astype(jnp.int32)
+        angle = jnp.max(numbers[0, 4 * a : 4 * a + 1, :]).astype(jnp.int32)
         slot = jnp.where(angle >= PAIRS, 2 * (ANGLES - 1 - angle) + 1, 2 * angle)
         at = pl.multiple_of(32 * slot, 32)
         for t in range(4):
             part = jnp.where(tiles[32 * a : 32 * a + 32] == t, rows[32 * a : 32 * a + 32], 0.0)
-            pieces[pl.ds(at + 8 * t, 8), :] = jnp.sum(part.reshape(4, 8, W), axis=0)
+            part = jnp.sum(part.reshape(4, 8, W), axis=0)
+            pieces[pl.ds(at + 8 * t, 8), :] = part + pltpu.roll(part, 4, 0)
     for z in range(8):
-        out[z, :CHUNK, :] = total
-        out[z, CHUNK:, :] = pieces[pl.ds(z, 32, stride=8), :]
+        out[z, :PART, :] = total
+        out[z, PART:, :] = pieces[pl.ds(z // 2, 32, stride=8), :]
 
 
 def adjoint_kernel(received, dft_t, leaving, rows_tables, edges, middles, *refs):
     beams, (out, pieces, shifted, sheared) = refs[:PAIRS], refs[PAIRS:]
     block = 2 * lax.axis_index("y") + lax.axis_index("xh")
-    total = received[0]
-    for z in range(1, 8):
-        total = total + received[z]
-    chunk = total[:CHUNK] * (1.0 / 16.0)
-    pieces[...] = total[CHUNK:]
+    even, odd = received[0], received[1]
+    for z in range(2, 8, 2):
+        even, odd = even + received[z], odd + received[z + 1]
+    chunk = jnp.concatenate([even[:PART], odd[:PART]], 0) * (1.0 / 16.0)
+    pieces[...] = jnp.where(lax.axis_index("zp") == 0, even[PART:], odd[PART:])
     rows = jnp.concatenate([pieces[pl.ds(t, 8, stride=4), :] for t in range(4)], axis=1)
     spectrum = three(mm, split(rows), (dft_t[0], dft_t[1]))
     weight = jnp.where(lax.broadcasted_iota(jnp.int32, (8, N), 1) % H == 0, 0.5 / N, 1.0 / N)
@@ -492,7 +494,8 @@
     return result if len(outs) > 1 else result[0]
 
 
-GZ = ("xl", "z", "core")
+Z = ("zq", "zp")
+GZ = ("xl", "zq", "zp", "core")
 PLANE = ("y", "xh", "xl")
 
 
@@ -536,10 +539,11 @@
         band_dft,
         band_probe,
     )
-    packed = vmem_call(pack_kernel, [(16 * MESSAGE, W)], [], "pack", angle_index, keep, swap(send))
-    shared = exchange(packed.reshape(16, MESSAGE, 1, W), PLANE).reshape(16 * MESSAGE, W)
-    relay = vmem_call(relay_kernel, [(8, CHUNK + 32, W)], [pltpu.VMEM((256, W), F32), pltpu.VMEM((3, 16, W), F32)], "relay", shared)
-    rows = exchange(relay, "z")
+    packed = vmem_call(pack_kernel, [(32 * MESSAGE, W)], [], "pack", angle_index, keep, swap(send))
+    shared = exchange(packed.reshape(32, MESSAGE, 1, W), PLANE + ("zp",)).reshape(32 * MESSAGE, W)
+    scratch = [pltpu.VMEM((256, W), F32), pltpu.VMEM((3, 32, W), F32)]
+    relay = vmem_call(relay_kernel, [(8, PART + 32, W)], scratch, "relay", shared)
+    rows = exchange(relay, Z)
     blocks = vmem_call(
         adjoint_kernel,
         [(16, CHUNK + 32, W)],
@@ -569,7 +573,7 @@
 
 
 def solution(mesh):
-    split_mesh = Mesh(mesh.devices.reshape(4, 2, 2, 8, 2), ("y", "xh", "xl", "z", "core"))
+    split_mesh = Mesh(mesh.devices.reshape(4, 2, 2, 4, 2, 2), ("y", "xh", "xl", "zq", "zp", "core"))
     angle, gz = ("y", "xh"), GZ
     return jax.shard_map(
         local,

time: 88.2 us -> 85.2 us (0.966)
  blocking collectives: 50 us -> 46.2 us
    all_to_all x3, blocking collectives: 50 us -> 46.2 us  [exchange(): return lax.all_to_all(blocks, axes, split_axis=0, concat_axis=0, tiled=True)]
where the time goes in v7:
time: 85.2 us; the launch traced here: 84.9 us
  blocking collectives  46.2 us (54%)
  starting transfers between devices  16.6 us (19%)
  Pallas kernels  11.1 us (13%)
  waiting for transfers between devices  7.28 us (9%)
  between operations  2.76 us (3%)
  local copies, waits for them, and re-layouts  0.94 us (1%)
    all_to_all x3, blocking collectives, exchange(): return lax.all_to_all(blocks, axes, split_axis=0, concat_axis=0, tiled=True)  46.2 us
    all_to_all x1, starting transfers between devices, exchange(): return lax.all_to_all(blocks, axes, split_axis=0, concat_axis=0, tiled=True)  11.1 us
    pallas_call x6, Pallas kernels, vmem_call(): pl.pallas_call(kernel, in_specs=[pl.BlockSpec(memory_space=pltpu.SMEM if...  6.58 us
    all_to_all x1, waiting for transfers between devices, exchange(): return lax.all_to_all(blocks, axes, split_axis=0, concat_axis=0, tiled=True)  5.65 us
    ppermute x2, starting transfers between devices, swap(): return lax.ppermute(rows, 'core', [(0, 1), (1, 0)])  5.53 us
    pallas_call x1, Pallas kernels, forward_call(): pl.pallas_call(forward_kernel, in_specs=[pl.BlockSpec(memory_space=pltpu....  4.56 us
  transfers between devices with their start and end apart: 3, of which 3 were waited for; matrix products, arithmetic and copies ran while one was open for 0% of the time, Pallas kernels for 3%

profile of v7, /device:TPU:1, one launch (start us, length us, event | category | flops | bytes accessed | tf_op | source)
XLA Modules:
  0.0 84.9 jit_solution(8762513255257914549)
XLA Ops:
  1.3 0.0 copy-start
  1.3 0.0 copy-start.9
  1.3 4.6 %forward.1 = f32[128,128]{1,0:T(8,128)} custom-call(s32[1]{0:T(128)S(6)} %copy.23.sc, bf16[1,512,512]{2,1,0:T(8,128)(2,1)} %volume.1, bf16[2,512,512]{2,1,0:T(8,128)(2,1)} %constant.37.clone.dft_hbm, bf16[2,512,512]{2,1,0:T(8,128)(2,1)} %constant.38.clone.dft_t_hbm.dft_t, f32[8,88,512]{2,1,0:T(8,128)} %constant.41.clone.factors_hbm, ...), custom_call_target="tpu_custom_call" | custom-call | flops 4000000000 | bytes 4000000 | tf_op jit(solution)/shard_map/forward/pallas_call | solution.py:457
  5.9 11.1 %all-to-all-start = ((f32[32,4,128]{2,1,0:T(4,128)}), f32[32,4,128]{2,1,0:T(4,128)S(1)}, u32[]{:S(2)}, u32[]{:S(2)}) async-start(f32[32,4,128]{2,1,0:T(4,128)} %bitcast.10), calls=%async_computation | async-start | bytes 131072 | tf_op jit(solution)/shard_map/all_to_all | solution.py:503
  17.6 0.0 copy-done
  17.6 0.0 copy-done.9
  17.6 0.0 copy-start.1
  17.6 1.1 %prepare.1 = (f32[4,256,256]{2,1,0:T(8,128)S(1)}, bf16[256,256]{1,0:T(8,128)(2,1)S(1)}, f32[8,2,32,128]{3,2,1,0:T(8,128)S(1)}) custom-call(s32[1,1]{1,0:T(1,128)S(6)} %copy.24.row_ref, f32[8,2,128,128]{3,2,1,0:T(8,128)S(1)} %copy-done, bf16[2,2,256,256]{3,2,1,0:T(8,128)(2,1)S(1)} %copy-done.9), custom_call_target="tpu_custom_call" | custom-call | flops 3000000000 | bytes 4000000 | tf_op jit(solution)/shard_map/prepare/pallas_call | solution.py:481
  19.4 5.7 %all-to-all-done = f32[32,4,128]{2,1,0:T(4,128)S(1)} async-done(((f32[32,4,128]{2,1,0:T(4,128)}), f32[32,4,128]{2,1,0:T(4,128)S(1)}, u32[]{:S(2)}, u32[]{:S(2)}) %all-to-all-start) | async-done | bytes 65568 | tf_op jit(solution)/shard_map/all_to_all | solution.py:503
  25.0 0.0 copy-done.1
  25.0 2.1 %window.1 = (f32[1048,128]{1,0:T(8,128)S(1)}, f32[1048,128]{1,0:T(8,128)S(1)}) custom-call(s32[1,1]{1,0:T(1,128)S(6)} %copy.24.row_ref, s32[1,1]{1,0:T(1,128)S(6)} %copy.25.col_ref, f32[128,128]{1,0:T(8,128)S(1)} %bitcast.9, f32[8,2,128,128]{3,2,1,0:T(8,128)S(1)} %copy-done, f32[1,1,128,128]{3,2,1,0:T(8,128)S(1)} %copy-done.1, ...), custom_call_target="tpu_custom_call" | custom-call | flops 3000000000 | bytes 4000000 | tf_op jit(solution)/shard_map/window/pallas_call | solution.py:481
  27.1 1.3 %collective-permute-start = (f32[1048,128]{1,0:T(8,128)S(1)}, f32[1048,128]{1,0:T(8,128)S(1)}, u32[]{:S(2)}, u32[]{:S(2)}) collective-permute-start(f32[1048,128]{1,0:T(8,128)S(1)} %get-tuple-element.13), channel_id=1, source_target_pairs={{0,1},{1,0},{2,3},{3,2},{4,5},{5,4},{6,7},{7,6},{8,9},{9,8},{10,11... | collective-permute-start | bytes 1609736 | tf_op jit(solution)/shard_map/ppermute | solution.py:507
  28.4 1.6 %collective-permute-done.other = f32[1048,128]{1,0:T(8,128)S(1)} collective-permute-done((f32[1048,128]{1,0:T(8,128)S(1)}, f32[1048,128]{1,0:T(8,128)S(1)}, u32[]{:S(2)}, u32[]{:S(2)}) %collective-permute-start) | collective-permute-done | bytes 536608 | tf_op jit(solution)/shard_map/ppermute | solution.py:507
  30.0 0.1 pack.1
  30.0 19.6 %all_to_all.20 = f32[32,41,1,128]{3,2,1,0:T(1,128)S(1)} all-to-all(f32[32,41,1,128]{3,2,1,0:T(1,128)S(1)} %bitcast.7), channel_id=1, replica_groups=mesh['y'=4,'xh'=2,'xl'=2,'zq'=4,'zp'=2,'core'=2] {'y','xh','xl','zp'}, dimensions={0} | all-to-all | bytes 1343488 | tf_op jit(solution)/shard_map/all_to_all | solution.py:503
  49.6 0.0 copy-start.2
  49.6 0.0 copy-start.3
  49.6 0.0 copy-start.4
  49.6 0.0 copy-start.5
  49.6 0.0 copy-start.6
  49.6 0.0 copy-start.7
  49.6 0.0 copy-start.8
  49.6 0.0 copy-start.10
  49.6 0.0 copy-start.11
  49.7 0.3 relay.1
  49.9 12.1 %all_to_all.21.received = f32[8,64,128]{2,1,0:T(8,128)S(1)} all-to-all(f32[8,64,128]{2,1,0:T(8,128)S(1)} %relay.1), channel_id=1, replica_groups=mesh['y'=4,'xh'=2,'xl'=2,'zq'=4,'zp'=2,'core'=2] {'zq','zp'}, dimensions={0} | all-to-all | bytes 524288 | tf_op jit(solution)/shard_map/all_to_all | solution.py:503
  62.0 0.0 copy-done.2
  62.0 0.0 copy-done.3
  62.0 0.0 copy-done.4
  62.1 0.0 copy-done.5
  62.1 0.0 copy-done.6
  62.1 0.0 copy-done.7
  62.1 0.0 copy-done.8
  62.1 0.0 copy-done.10
  62.1 0.0 copy-done.11
  62.1 1.6 %adjoint.1 = f32[16,96,128]{2,1,0:T(8,128)S(1)} custom-call(f32[8,64,128]{2,1,0:T(8,128)S(1)} %all_to_all.21.received, bf16[2,512,512]{2,1,0:T(8,128)(2,1)S(1)} %copy-done.2, bf16[2,512,512]{2,1,0:T(8,128)(2,1)S(1)} %copy-done.3, f32[4,2,72,256]{3,2,1,0:T(8,128)S(1)} %copy-done.4, f32[4,8,256]{2,1,0:T(8,128)S(1)} %copy-done.10, f32[16,256]{1,0:T(8,128)S(1)} %copy-done.11, ...), custom_call_target="tpu_custom_call" | custom-call | flops 3000000000 | bytes 4000000 | tf_op jit(solution)/shard_map/adjoint/pallas_call | solution.py:481
  63.7 14.5 %all_to_all.22.received = f32[16,96,128]{2,1,0:T(8,128)S(1)} all-to-all(f32[16,96,128]{2,1,0:T(8,128)S(1)} %adjoint.1), channel_id=1, replica_groups=mesh['y'=4,'xh'=2,'xl'=2,'zq'=4,'zp'=2,'core'=2] {'y','xh','xl'}, dimensions={0} | all-to-all | bytes 1572864 | tf_op jit(solution)/shard_map/all_to_all | solution.py:503
  78.3 4.3 %collective-permute-start.1 = (f32[16,64,128]{2,1,0:T(8,128)S(1)}, f32[16,64,128]{2,1,0:T(8,128)S(1)}, u32[]{:S(2)}, u32[]{:S(2)}) collective-permute-start(f32[16,64,128]{2,1,0:T(8,128)S(1)} %slice.4), channel_id=1, source_target_pairs={{0,1},{1,0},{2,3},{3,2},{4,5},{5,4},{6,7},{7,6},{8,9},{9,8},{10,11... | collective-permute-start | bytes 1572872 | tf_op jit(solution)/shard_map/ppermute | solution.py:507
  82.5 1.5 %assemble.1 = (f32[1,64,512]{2,1,0:T(8,128)}, f32[2,16,64,128]{3,2,1,0:T(8,128)}) custom-call(f32[16,96,128]{2,1,0:T(8,128)S(1)} %all_to_all.22.received), custom_call_target="tpu_custom_call" | custom-call | flops 3000000000 | bytes 4000000 | tf_op jit(solution)/shard_map/assemble/pallas_call | solution.py:481
  84.0 0.1 collective-permute-done.1
  84.1 0.8 bitcast_dynamic-update-slice_fusion
  (1 shorter events, 0.0 us)
Async XLA Ops:
  1.3 16.3 %copy-start = (f32[8,2,128,128]{3,2,1,0:T(8,128)S(1)}, f32[8,2,128,128]{3,2,1,0:T(8,128)}, u32[]{:S(2)}) copy-start(f32[8,2,128,128]{3,2,1,0:T(8,128)} %probe.3) | copy-start | bytes 3145732
  1.3 16.3 %copy-start.9 = (bf16[2,2,256,256]{3,2,1,0:T(8,128)(2,1)S(1)}, bf16[2,2,256,256]{3,2,1,0:T(8,128)(2,1)}, u32[]{:S(2)}) copy-start(bf16[2,2,256,256]{3,2,1,0:T(8,128)(2,1)} %constant.40.clone.dfts) | copy-start | bytes 1572868
  5.9 19.1 %all-to-all-start = ((f32[32,4,128]{2,1,0:T(4,128)}), f32[32,4,128]{2,1,0:T(4,128)S(1)}, u32[]{:S(2)}, u32[]{:S(2)}) async-start(f32[32,4,128]{2,1,0:T(4,128)} %bitcast.10), calls=%async_computation | async-start | bytes 131072 | tf_op jit(solution)/shard_map/all_to_all | solution.py:503
  17.6 7.4 %copy-start.1 = (f32[1,1,128,128]{3,2,1,0:T(8,128)S(1)}, f32[1,1,128,128]{3,2,1,0:T(8,128)}, u32[]{:S(2)}) copy-start(f32[1,1,128,128]{3,2,1,0:T(8,128)} %measured.1) | copy-start | bytes 196612
  27.1 2.8 %collective-permute-start = (f32[1048,128]{1,0:T(8,128)S(1)}, f32[1048,128]{1,0:T(8,128)S(1)}, u32[]{:S(2)}, u32[]{:S(2)}) collective-permute-start(f32[1048,128]{1,0:T(8,128)S(1)} %get-tuple-element.13), channel_id=1, source_target_pairs={{0,1},{1,0},{2,3},{3,2},{4,5},{5,4},{6,7},{7,6},{8,9},{9,8},{10,11... | collective-permute-start | bytes 1609736 | tf_op jit(solution)/shard_map/ppermute | solution.py:507
  49.6 12.5 %copy-start.2 = (bf16[2,512,512]{2,1,0:T(8,128)(2,1)S(1)}, bf16[2,512,512]{2,1,0:T(8,128)(2,1)}, u32[]{:S(2)}) copy-start(bf16[2,512,512]{2,1,0:T(8,128)(2,1)} %constant.38.clone.dft_t_hbm.dft_t) | copy-start | bytes 3145732
  49.6 12.5 %copy-start.3 = (bf16[2,512,512]{2,1,0:T(8,128)(2,1)S(1)}, bf16[2,512,512]{2,1,0:T(8,128)(2,1)}, u32[]{:S(2)}) copy-start(bf16[2,512,512]{2,1,0:T(8,128)(2,1)} %constant.39.clone.leaving) | copy-start | bytes 3145732
  49.6 12.5 %copy-start.4 = (f32[4,2,72,256]{3,2,1,0:T(8,128)S(1)}, f32[4,2,72,256]{3,2,1,0:T(8,128)}, u32[]{:S(2)}) copy-start(f32[4,2,72,256]{3,2,1,0:T(8,128)} %constant.42.clone.rows_tables) | copy-start | bytes 1769476
  49.6 12.5 %copy-start.5 = (bf16[2,512,256]{2,1,0:T(8,128)(2,1)S(1)}, bf16[2,512,256]{2,1,0:T(8,128)(2,1)}, u32[]{:S(2)}) copy-start(bf16[2,512,256]{2,1,0:T(8,128)(2,1)} %constant.49.clone.refs_3_) | copy-start | bytes 1572868
  49.6 12.5 %copy-start.6 = (bf16[2,512,256]{2,1,0:T(8,128)(2,1)S(1)}, bf16[2,512,256]{2,1,0:T(8,128)(2,1)}, u32[]{:S(2)}) copy-start(bf16[2,512,256]{2,1,0:T(8,128)(2,1)} %constant.48.clone.refs_2_) | copy-start | bytes 1572868
  49.6 12.5 %copy-start.7 = (bf16[2,512,256]{2,1,0:T(8,128)(2,1)S(1)}, bf16[2,512,256]{2,1,0:T(8,128)(2,1)}, u32[]{:S(2)}) copy-start(bf16[2,512,256]{2,1,0:T(8,128)(2,1)} %constant.47.clone.refs_1_) | copy-start | bytes 1572868
  49.6 12.5 %copy-start.8 = (bf16[2,512,256]{2,1,0:T(8,128)(2,1)S(1)}, bf16[2,512,256]{2,1,0:T(8,128)(2,1)}, u32[]{:S(2)}) copy-start(bf16[2,512,256]{2,1,0:T(8,128)(2,1)} %constant.46.clone.refs_0_) | copy-start | bytes 1572868
  49.6 12.5 %copy-start.10 = (f32[4,8,256]{2,1,0:T(8,128)S(1)}, f32[4,8,256]{2,1,0:T(8,128)}, u32[]{:S(2)}) copy-start(f32[4,8,256]{2,1,0:T(8,128)} %constant.44.clone.edges_hbm.edges) | copy-start | bytes 98308
  49.6 12.5 %copy-start.11 = (f32[16,256]{1,0:T(8,128)S(1)}, f32[16,256]{1,0:T(8,128)}, u32[]{:S(2)}) copy-start(f32[16,256]{1,0:T(8,128)} %constant.45.clone.middles) | copy-start | bytes 49156
  78.3 5.8 %collective-permute-start.1 = (f32[16,64,128]{2,1,0:T(8,128)S(1)}, f32[16,64,128]{2,1,0:T(8,128)S(1)}, u32[]{:S(2)}, u32[]{:S(2)}) collective-permute-start(f32[16,64,128]{2,1,0:T(8,128)S(1)} %slice.4), channel_id=1, source_target_pairs={{0,1},{1,0},{2,3},{3,2},{4,5},{5,4},{6,7},{7,6},{8,9},{9,8},{10,11... | collective-permute-start | bytes 1572872 | tf_op jit(solution)/shard_map/ppermute | solution.py:507

commit v8 on v7

--- a/solution.py
+++ b/solution.py
@@ -361,15 +361,15 @@
             pieces[pl.ds(at + 8 * t, 8), :] = part + pltpu.roll(part, 4, 0)
     for z in range(8):
         out[z, :PART, :] = total
-        out[z, PART:, :] = pieces[pl.ds(z // 2, 32, stride=8), :]
+        out[z, PART:, :] = pieces[pl.ds(z % 4, 32, stride=8), :]
 
 
 def adjoint_kernel(received, dft_t, leaving, rows_tables, edges, middles, *refs):
     beams, (out, pieces, shifted, sheared) = refs[:PAIRS], refs[PAIRS:]
     block = 2 * lax.axis_index("y") + lax.axis_index("xh")
-    even, odd = received[0], received[1]
-    for z in range(2, 8, 2):
-        even, odd = even + received[z], odd + received[z + 1]
+    even, odd = received[0], received[4]
+    for z in range(1, 4):
+        even, odd = even + received[z], odd + received[4 + z]
     chunk = jnp.concatenate([even[:PART], odd[:PART]], 0) * (1.0 / 16.0)
     pieces[...] = jnp.where(lax.axis_index("zp") == 0, even[PART:], odd[PART:])
     rows = jnp.concatenate([pieces[pl.ds(t, 8, stride=4), :] for t in range(4)], axis=1)
@@ -494,7 +494,7 @@
     return result if len(outs) > 1 else result[0]
 
 
-Z = ("zq", "zp")
+Z = ("zp", "zq")
 GZ = ("xl", "zq", "zp", "core")
 PLANE = ("y", "xh", "xl")
 

time: 85.2 us -> 83.1 us (0.975)
  blocking collectives: 46.2 us -> 44 us
    all_to_all x3, blocking collectives: 46.2 us -> 44 us  [exchange(): return lax.all_to_all(blocks, axes, split_axis=0, concat_axis=0, tiled=True)]
where the time goes in v8:
time: 83.1 us; the launch traced here: 82.9 us
  blocking collectives  44 us (53%)
  starting transfers between devices  16.8 us (20%)
  Pallas kernels  11.1 us (13%)
  waiting for transfers between devices  7.28 us (9%)
  between operations  2.77 us (3%)
  local copies, waits for them, and re-layouts  0.94 us (1%)
    all_to_all x3, blocking collectives, exchange(): return lax.all_to_all(blocks, axes, split_axis=0, concat_axis=0, tiled=True)  44 us
    all_to_all x1, starting transfers between devices, exchange(): return lax.all_to_all(blocks, axes, split_axis=0, concat_axis=0, tiled=True)  11.1 us
    pallas_call x6, Pallas kernels, vmem_call(): pl.pallas_call(kernel, in_specs=[pl.BlockSpec(memory_space=pltpu.SMEM if...  6.58 us
    ppermute x2, starting transfers between devices, swap(): return lax.ppermute(rows, 'core', [(0, 1), (1, 0)])  5.69 us
    all_to_all x1, waiting for transfers between devices, exchange(): return lax.all_to_all(blocks, axes, split_axis=0, concat_axis=0, tiled=True)  5.65 us
    pallas_call x1, Pallas kernels, forward_call(): pl.pallas_call(forward_kernel, in_specs=[pl.BlockSpec(memory_space=pltpu....  4.56 us
  transfers between devices with their start and end apart: 3, of which 3 were waited for; matrix products, arithmetic and copies ran while one was open for 0% of the time, Pallas kernels for 3%

profile of v8, /device:TPU:1, one launch (start us, length us, event | category | flops | bytes accessed | tf_op | source)
XLA Modules:
  0.0 82.9 jit_solution(5449036360948512022)
XLA Ops:
  1.3 0.0 copy-start
  1.3 0.0 copy-start.9
  1.3 4.6 %forward.1 = f32[128,128]{1,0:T(8,128)} custom-call(s32[1]{0:T(128)S(6)} %copy.23.sc, bf16[1,512,512]{2,1,0:T(8,128)(2,1)} %volume.1, bf16[2,512,512]{2,1,0:T(8,128)(2,1)} %constant.37.clone.dft_hbm, bf16[2,512,512]{2,1,0:T(8,128)(2,1)} %constant.38.clone.dft_t_hbm.dft_t, f32[8,88,512]{2,1,0:T(8,128)} %constant.41.clone.factors_hbm, ...), custom_call_target="tpu_custom_call" | custom-call | flops 4000000000 | bytes 4000000 | tf_op jit(solution)/shard_map/forward/pallas_call | solution.py:457
  5.9 11.1 %all-to-all-start = ((f32[32,4,128]{2,1,0:T(4,128)}), f32[32,4,128]{2,1,0:T(4,128)S(1)}, u32[]{:S(2)}, u32[]{:S(2)}) async-start(f32[32,4,128]{2,1,0:T(4,128)} %bitcast.10), calls=%async_computation | async-start | bytes 131072 | tf_op jit(solution)/shard_map/all_to_all | solution.py:503
  17.6 0.0 copy-done
  17.6 0.0 copy-done.9
  17.6 0.0 copy-start.1
  17.6 1.1 %prepare.1 = (f32[4,256,256]{2,1,0:T(8,128)S(1)}, bf16[256,256]{1,0:T(8,128)(2,1)S(1)}, f32[8,2,32,128]{3,2,1,0:T(8,128)S(1)}) custom-call(s32[1,1]{1,0:T(1,128)S(6)} %copy.24.row_ref, f32[8,2,128,128]{3,2,1,0:T(8,128)S(1)} %copy-done, bf16[2,2,256,256]{3,2,1,0:T(8,128)(2,1)S(1)} %copy-done.9), custom_call_target="tpu_custom_call" | custom-call | flops 3000000000 | bytes 4000000 | tf_op jit(solution)/shard_map/prepare/pallas_call | solution.py:481
  19.4 5.6 %all-to-all-done = f32[32,4,128]{2,1,0:T(4,128)S(1)} async-done(((f32[32,4,128]{2,1,0:T(4,128)}), f32[32,4,128]{2,1,0:T(4,128)S(1)}, u32[]{:S(2)}, u32[]{:S(2)}) %all-to-all-start) | async-done | bytes 65568 | tf_op jit(solution)/shard_map/all_to_all | solution.py:503
  25.0 0.0 copy-done.1
  25.0 2.1 %window.1 = (f32[1048,128]{1,0:T(8,128)S(1)}, f32[1048,128]{1,0:T(8,128)S(1)}) custom-call(s32[1,1]{1,0:T(1,128)S(6)} %copy.24.row_ref, s32[1,1]{1,0:T(1,128)S(6)} %copy.25.col_ref, f32[128,128]{1,0:T(8,128)S(1)} %bitcast.9, f32[8,2,128,128]{3,2,1,0:T(8,128)S(1)} %copy-done, f32[1,1,128,128]{3,2,1,0:T(8,128)S(1)} %copy-done.1, ...), custom_call_target="tpu_custom_call" | custom-call | flops 3000000000 | bytes 4000000 | tf_op jit(solution)/shard_map/window/pallas_call | solution.py:481
  27.1 1.3 %collective-permute-start = (f32[1048,128]{1,0:T(8,128)S(1)}, f32[1048,128]{1,0:T(8,128)S(1)}, u32[]{:S(2)}, u32[]{:S(2)}) collective-permute-start(f32[1048,128]{1,0:T(8,128)S(1)} %get-tuple-element.13), channel_id=1, source_target_pairs={{0,1},{1,0},{2,3},{3,2},{4,5},{5,4},{6,7},{7,6},{8,9},{9,8},{10,11... | collective-permute-start | bytes 1609736 | tf_op jit(solution)/shard_map/ppermute | solution.py:507
  28.4 1.6 %collective-permute-done.other = f32[1048,128]{1,0:T(8,128)S(1)} collective-permute-done((f32[1048,128]{1,0:T(8,128)S(1)}, f32[1048,128]{1,0:T(8,128)S(1)}, u32[]{:S(2)}, u32[]{:S(2)}) %collective-permute-start) | collective-permute-done | bytes 536608 | tf_op jit(solution)/shard_map/ppermute | solution.py:507
  30.0 0.1 pack.1
  30.0 19.6 %all_to_all.20 = f32[32,41,1,128]{3,2,1,0:T(1,128)S(1)} all-to-all(f32[32,41,1,128]{3,2,1,0:T(1,128)S(1)} %bitcast.7), channel_id=1, replica_groups=mesh['y'=4,'xh'=2,'xl'=2,'zq'=4,'zp'=2,'core'=2] {'y','xh','xl','zp'}, dimensions={0} | all-to-all | bytes 1343488 | tf_op jit(solution)/shard_map/all_to_all | solution.py:503
  49.6 0.0 copy-start.2
  49.6 0.0 copy-start.3
  49.6 0.0 copy-start.4
  49.6 0.0 copy-start.5
  49.6 0.0 copy-start.6
  49.6 0.0 copy-start.7
  49.6 0.0 copy-start.8
  49.6 0.0 copy-start.10
  49.6 0.0 copy-start.11
  49.7 0.3 relay.1
  49.9 10.4 %all_to_all.21.received = f32[8,64,128]{2,1,0:T(8,128)S(1)} all-to-all(f32[8,64,128]{2,1,0:T(8,128)S(1)} %relay.1), channel_id=1, replica_groups=mesh['y'=4,'xh'=2,'xl'=2,'zq'=4,'zp'=2,'core'=2] {'zp','zq'}, dimensions={0} | all-to-all | bytes 524288 | tf_op jit(solution)/shard_map/all_to_all | solution.py:503
  60.4 0.0 copy-done.2
  60.4 0.0 copy-done.3
  60.4 0.0 copy-done.4
  60.4 0.0 copy-done.5
  60.4 0.0 copy-done.6
  60.4 0.0 copy-done.7
  60.4 0.0 copy-done.8
  60.4 0.0 copy-done.10
  60.4 0.0 copy-done.11
  60.4 1.6 %adjoint.1 = f32[16,96,128]{2,1,0:T(8,128)S(1)} custom-call(f32[8,64,128]{2,1,0:T(8,128)S(1)} %all_to_all.21.received, bf16[2,512,512]{2,1,0:T(8,128)(2,1)S(1)} %copy-done.2, bf16[2,512,512]{2,1,0:T(8,128)(2,1)S(1)} %copy-done.3, f32[4,2,72,256]{3,2,1,0:T(8,128)S(1)} %copy-done.4, f32[4,8,256]{2,1,0:T(8,128)S(1)} %copy-done.10, f32[16,256]{1,0:T(8,128)S(1)} %copy-done.11, ...), custom_call_target="tpu_custom_call" | custom-call | flops 3000000000 | bytes 4000000 | tf_op jit(solution)/shard_map/adjoint/pallas_call | solution.py:481
  62.0 14.0 %all_to_all.22.received = f32[16,96,128]{2,1,0:T(8,128)S(1)} all-to-all(f32[16,96,128]{2,1,0:T(8,128)S(1)} %adjoint.1), channel_id=1, replica_groups=mesh['y'=4,'xh'=2,'xl'=2,'zq'=4,'zp'=2,'core'=2] {'y','xh','xl'}, dimensions={0} | all-to-all | bytes 1572864 | tf_op jit(solution)/shard_map/all_to_all | solution.py:503
  76.1 4.4 %collective-permute-start.1 = (f32[16,64,128]{2,1,0:T(8,128)S(1)}, f32[16,64,128]{2,1,0:T(8,128)S(1)}, u32[]{:S(2)}, u32[]{:S(2)}) collective-permute-start(f32[16,64,128]{2,1,0:T(8,128)S(1)} %slice.4), channel_id=1, source_target_pairs={{0,1},{1,0},{2,3},{3,2},{4,5},{5,4},{6,7},{7,6},{8,9},{9,8},{10,11... | collective-permute-start | bytes 1572872 | tf_op jit(solution)/shard_map/ppermute | solution.py:507
  80.5 1.5 %assemble.1 = (f32[1,64,512]{2,1,0:T(8,128)}, f32[2,16,64,128]{3,2,1,0:T(8,128)}) custom-call(f32[16,96,128]{2,1,0:T(8,128)S(1)} %all_to_all.22.received), custom_call_target="tpu_custom_call" | custom-call | flops 3000000000 | bytes 4000000 | tf_op jit(solution)/shard_map/assemble/pallas_call | solution.py:481
  82.0 0.1 collective-permute-done.1
  82.0 0.8 %bitcast_dynamic-update-slice_fusion = f32[2,16,64,128]{3,2,1,0:T(8,128)} fusion(f32[2,16,64,128]{3,2,1,0:T(8,128)} %get-tuple-element.15, s32[]{:T(128)S(6)} %select_n.3, f32[16,64,128]{2,1,0:T(8,128)S(1)} %collective-permute-done.1), kind=kLoop, calls=%fused_computation | loop fusion | bytes 1048580 | tf_op jit(solution)/shard_map/dynamic_update_slice | solution.py:571
  (1 shorter events, 0.0 us)
Async XLA Ops:
  1.3 16.3 %copy-start = (f32[8,2,128,128]{3,2,1,0:T(8,128)S(1)}, f32[8,2,128,128]{3,2,1,0:T(8,128)}, u32[]{:S(2)}) copy-start(f32[8,2,128,128]{3,2,1,0:T(8,128)} %probe.3) | copy-start | bytes 3145732
  1.3 16.3 %copy-start.9 = (bf16[2,2,256,256]{3,2,1,0:T(8,128)(2,1)S(1)}, bf16[2,2,256,256]{3,2,1,0:T(8,128)(2,1)}, u32[]{:S(2)}) copy-start(bf16[2,2,256,256]{3,2,1,0:T(8,128)(2,1)} %constant.40.clone.dfts) | copy-start | bytes 1572868
  5.9 19.1 %all-to-all-start = ((f32[32,4,128]{2,1,0:T(4,128)}), f32[32,4,128]{2,1,0:T(4,128)S(1)}, u32[]{:S(2)}, u32[]{:S(2)}) async-start(f32[32,4,128]{2,1,0:T(4,128)} %bitcast.10), calls=%async_computation | async-start | bytes 131072 | tf_op jit(solution)/shard_map/all_to_all | solution.py:503
  17.6 7.4 %copy-start.1 = (f32[1,1,128,128]{3,2,1,0:T(8,128)S(1)}, f32[1,1,128,128]{3,2,1,0:T(8,128)}, u32[]{:S(2)}) copy-start(f32[1,1,128,128]{3,2,1,0:T(8,128)} %measured.1) | copy-start | bytes 196612
  27.1 2.8 %collective-permute-start = (f32[1048,128]{1,0:T(8,128)S(1)}, f32[1048,128]{1,0:T(8,128)S(1)}, u32[]{:S(2)}, u32[]{:S(2)}) collective-permute-start(f32[1048,128]{1,0:T(8,128)S(1)} %get-tuple-element.13), channel_id=1, source_target_pairs={{0,1},{1,0},{2,3},{3,2},{4,5},{5,4},{6,7},{7,6},{8,9},{9,8},{10,11... | collective-permute-start | bytes 1609736 | tf_op jit(solution)/shard_map/ppermute | solution.py:507
  49.6 10.8 %copy-start.2 = (bf16[2,512,512]{2,1,0:T(8,128)(2,1)S(1)}, bf16[2,512,512]{2,1,0:T(8,128)(2,1)}, u32[]{:S(2)}) copy-start(bf16[2,512,512]{2,1,0:T(8,128)(2,1)} %constant.38.clone.dft_t_hbm.dft_t) | copy-start | bytes 3145732
  49.6 10.8 %copy-start.3 = (bf16[2,512,512]{2,1,0:T(8,128)(2,1)S(1)}, bf16[2,512,512]{2,1,0:T(8,128)(2,1)}, u32[]{:S(2)}) copy-start(bf16[2,512,512]{2,1,0:T(8,128)(2,1)} %constant.39.clone.leaving) | copy-start | bytes 3145732
  49.6 10.8 %copy-start.4 = (f32[4,2,72,256]{3,2,1,0:T(8,128)S(1)}, f32[4,2,72,256]{3,2,1,0:T(8,128)}, u32[]{:S(2)}) copy-start(f32[4,2,72,256]{3,2,1,0:T(8,128)} %constant.42.clone.rows_tables) | copy-start | bytes 1769476
  49.6 10.8 %copy-start.5 = (bf16[2,512,256]{2,1,0:T(8,128)(2,1)S(1)}, bf16[2,512,256]{2,1,0:T(8,128)(2,1)}, u32[]{:S(2)}) copy-start(bf16[2,512,256]{2,1,0:T(8,128)(2,1)} %constant.49.clone.refs_3_) | copy-start | bytes 1572868
  49.6 10.8 %copy-start.6 = (bf16[2,512,256]{2,1,0:T(8,128)(2,1)S(1)}, bf16[2,512,256]{2,1,0:T(8,128)(2,1)}, u32[]{:S(2)}) copy-start(bf16[2,512,256]{2,1,0:T(8,128)(2,1)} %constant.48.clone.refs_2_) | copy-start | bytes 1572868
  49.6 10.8 %copy-start.7 = (bf16[2,512,256]{2,1,0:T(8,128)(2,1)S(1)}, bf16[2,512,256]{2,1,0:T(8,128)(2,1)}, u32[]{:S(2)}) copy-start(bf16[2,512,256]{2,1,0:T(8,128)(2,1)} %constant.47.clone.refs_1_) | copy-start | bytes 1572868
  49.6 10.8 %copy-start.8 = (bf16[2,512,256]{2,1,0:T(8,128)(2,1)S(1)}, bf16[2,512,256]{2,1,0:T(8,128)(2,1)}, u32[]{:S(2)}) copy-start(bf16[2,512,256]{2,1,0:T(8,128)(2,1)} %constant.46.clone.refs_0_) | copy-start | bytes 1572868
  49.6 10.8 %copy-start.10 = (f32[4,8,256]{2,1,0:T(8,128)S(1)}, f32[4,8,256]{2,1,0:T(8,128)}, u32[]{:S(2)}) copy-start(f32[4,8,256]{2,1,0:T(8,128)} %constant.44.clone.edges_hbm.edges) | copy-start | bytes 98308
  49.6 10.8 %copy-start.11 = (f32[16,256]{1,0:T(8,128)S(1)}, f32[16,256]{1,0:T(8,128)}, u32[]{:S(2)}) copy-start(f32[16,256]{1,0:T(8,128)} %constant.45.clone.middles) | copy-start | bytes 49156
  76.1 6.0 %collective-permute-start.1 = (f32[16,64,128]{2,1,0:T(8,128)S(1)}, f32[16,64,128]{2,1,0:T(8,128)S(1)}, u32[]{:S(2)}, u32[]{:S(2)}) collective-permute-start(f32[16,64,128]{2,1,0:T(8,128)S(1)} %slice.4), channel_id=1, source_target_pairs={{0,1},{1,0},{2,3},{3,2},{4,5},{5,4},{6,7},{7,6},{8,9},{9,8},{10,11... | collective-permute-start | bytes 1572872 | tf_op jit(solution)/shard_map/ppermute | solution.py:507

commit v9 on v8

--- a/solution.py
+++ b/solution.py
@@ -324,7 +324,7 @@
         rows = slice(PART * peer, PART * (peer + 1))
         at = MESSAGE * peer
         out[at : at + PART, :] = keep[rows, :] + other[rows, :]
-        rows = pl.ds(HALF + 8 * (peer // 2 % 2) + peer % 2, 4, stride=2)
+        rows = pl.ds(HALF + 8 * BLOCKS[peer // 2][1] + peer % 2, 4, stride=2)
         out[at + PART : at + PART + 4, :] = keep[rows, :]
         out[at + PART + 4 : at + PART + 8, :] = other[rows, :]
         out[at + PART + 8 : at + MESSAGE, :] = numbers
@@ -342,9 +342,10 @@
         for shift in (1, 2, 3):
             value = jnp.where(quarter == (i + shift) % 4, rolls[shift], value)
         numbers[i] = value
-    rows = jnp.concatenate([received[MESSAGE * p + PART : MESSAGE * p + PART + 8, :] for p in range(32)], 0)
+    order = [2 * rank(a, xl) + zp for a in range(ANGLES) for xl in range(2) for zp in range(2)]
+    rows = jnp.concatenate([received[MESSAGE * p + PART : MESSAGE * p + PART + 8, :] for p in order], 0)
     first, second = (
-        jnp.concatenate([jnp.broadcast_to(numbers[1 + i, p : p + 1, :], (8, W)) for p in range(32)], 0)
+        jnp.concatenate([jnp.broadcast_to(numbers[1 + i, p : p + 1, :], (8, W)) for p in order], 0)
         for i in range(2)
     )
     row = lax.broadcasted_iota(jnp.int32, rows.shape, 0)
@@ -352,7 +353,7 @@
     lane = lax.broadcasted_iota(jnp.int32, rows.shape, 1)
     tiles = (columns >> 7) + jnp.where(lane < (columns & (W - 1)), 1, 0)
     for a in range(ANGLES):
-        angle = jnp.max(numbers[0, 4 * a : 4 * a + 1, :]).astype(jnp.int32)
+        angle = jnp.max(numbers[0, order[4 * a] : order[4 * a] + 1, :]).astype(jnp.int32)
         slot = jnp.where(angle >= PAIRS, 2 * (ANGLES - 1 - angle) + 1, 2 * angle)
         at = pl.multiple_of(32 * slot, 32)
         for t in range(4):
@@ -433,10 +434,10 @@
     for part in range(2):
         first, second = (columns[:, (2 * part + i) * W : (2 * part + i + 1) * W] for i in range(2))
         blocks = jnp.concatenate([first, second], 0).T
-        for peer in range(8 * part, 8 * part + 8):
-            out[peer, :CHUNK, :] = chunk
-            a = peer // 2 - 4 * part
-            out[peer, CHUNK:, :] = blocks[32 * a : 32 * a + 32, :]
+        for a in range(4):
+            for peer in (rank(4 * part + a, 0), rank(4 * part + a, 1)):
+                out[peer, :CHUNK, :] = chunk
+                out[peer, CHUNK:, :] = blocks[32 * a : 32 * a + 32, :]
 
 
 def assemble_kernel(received, out, probe_out, sem):
@@ -445,8 +446,8 @@
     xl = lax.axis_index("xl")
     lower = lax.broadcasted_iota(jnp.int32, (32, W), 1) < 64
     for b in range(4):
-        even = received[4 * b + xl, CHUNK:, :]
-        odd = received[4 * b + 2 + xl, CHUNK:, :]
+        even = received[rank(2 * b, xl), CHUNK:, :]
+        odd = received[rank(2 * b + 1, xl), CHUNK:, :]
         lanes = slice(b * W, (b + 1) * W)
         out[0, :32, lanes] = jnp.where(lower, even, pltpu.roll(odd, 64, 1))
         out[0, 32:, lanes] = jnp.where(lower, pltpu.roll(even, 64, 1), odd)
@@ -496,7 +497,14 @@
 
 Z = ("zp", "zq")
 GZ = ("xl", "zq", "zp", "core")
-PLANE = ("y", "xh", "xl")
+PLANE = ("xl", "xh", "y")
+
+
+def rank(block, xl):
+    return 8 * xl + 4 * (block % 2) + block // 2
+
+
+BLOCKS = {rank(block, xl): (block, xl) for block in range(ANGLES) for xl in range(2)}
 
 
 def exchange(blocks, axes):

time: 83.1 us -> 82.6 us (level)
  blocking collectives: 44 us -> 43.1 us
    all_to_all x3, blocking collectives: 44 us -> 43.1 us  [exchange(): return lax.all_to_all(blocks, axes, split_axis=0, concat_axis=0, tiled=True)]
where the time goes in v9:
time: 82.6 us; the launch traced here: 82.3 us
  blocking collectives  43.1 us (52%)
  starting transfers between devices  17.1 us (21%)
  Pallas kernels  11.2 us (14%)
  waiting for transfers between devices  7.28 us (9%)
  between operations  2.76 us (3%)
  local copies, waits for them, and re-layouts  0.94 us (1%)
    all_to_all x3, blocking collectives, exchange(): return lax.all_to_all(blocks, axes, split_axis=0, concat_axis=0, tiled=True)  43.1 us
    all_to_all x1, starting transfers between devices, exchange(): return lax.all_to_all(blocks, axes, split_axis=0, concat_axis=0, tiled=True)  11.1 us
    pallas_call x6, Pallas kernels, vmem_call(): pl.pallas_call(kernel, in_specs=[pl.BlockSpec(memory_space=pltpu.SMEM if...  6.59 us
    ppermute x2, starting transfers between devices, swap(): return lax.ppermute(rows, 'core', [(0, 1), (1, 0)])  6.04 us
    all_to_all x1, waiting for transfers between devices, exchange(): return lax.all_to_all(blocks, axes, split_axis=0, concat_axis=0, tiled=True)  5.65 us
    pallas_call x1, Pallas kernels, forward_call(): pl.pallas_call(forward_kernel, in_specs=[pl.BlockSpec(memory_space=pltpu....  4.56 us
  transfers between devices with their start and end apart: 3, of which 3 were waited for; matrix products, arithmetic and copies ran while one was open for 0% of the time, Pallas kernels for 3%

profile of v9, /device:TPU:1, one launch (start us, length us, event | category | flops | bytes accessed | tf_op | source)
XLA Modules:
  0.0 82.3 jit_solution(2207004225824898414)
XLA Ops:
  1.3 0.0 copy-start
  1.3 0.0 copy-start.9
  1.3 4.6 %forward.1 = f32[128,128]{1,0:T(8,128)} custom-call(s32[1]{0:T(128)S(6)} %copy.23.sc, bf16[1,512,512]{2,1,0:T(8,128)(2,1)} %volume.1, bf16[2,512,512]{2,1,0:T(8,128)(2,1)} %constant.37.clone.dft_hbm, bf16[2,512,512]{2,1,0:T(8,128)(2,1)} %constant.38.clone.dft_t_hbm.dft_t, f32[8,88,512]{2,1,0:T(8,128)} %constant.41.clone.factors_hbm, ...), custom_call_target="tpu_custom_call" | custom-call | flops 4000000000 | bytes 4000000 | tf_op jit(solution)/shard_map/forward/pallas_call | solution.py:458
  5.9 11.1 %all-to-all-start = ((f32[32,4,128]{2,1,0:T(4,128)}), f32[32,4,128]{2,1,0:T(4,128)S(1)}, u32[]{:S(2)}, u32[]{:S(2)}) async-start(f32[32,4,128]{2,1,0:T(4,128)} %bitcast.10), calls=%async_computation | async-start | bytes 131072 | tf_op jit(solution)/shard_map/all_to_all | solution.py:511
  17.6 0.0 copy-done
  17.6 0.0 copy-done.9
  17.6 0.0 copy-start.1
  17.6 1.1 %prepare.1 = (f32[4,256,256]{2,1,0:T(8,128)S(1)}, bf16[256,256]{1,0:T(8,128)(2,1)S(1)}, f32[8,2,32,128]{3,2,1,0:T(8,128)S(1)}) custom-call(s32[1,1]{1,0:T(1,128)S(6)} %copy.24.row_ref, f32[8,2,128,128]{3,2,1,0:T(8,128)S(1)} %copy-done, bf16[2,2,256,256]{3,2,1,0:T(8,128)(2,1)S(1)} %copy-done.9), custom_call_target="tpu_custom_call" | custom-call | flops 3000000000 | bytes 4000000 | tf_op jit(solution)/shard_map/prepare/pallas_call | solution.py:482
  19.4 5.7 %all-to-all-done = f32[32,4,128]{2,1,0:T(4,128)S(1)} async-done(((f32[32,4,128]{2,1,0:T(4,128)}), f32[32,4,128]{2,1,0:T(4,128)S(1)}, u32[]{:S(2)}, u32[]{:S(2)}) %all-to-all-start) | async-done | bytes 65568 | tf_op jit(solution)/shard_map/all_to_all | solution.py:511
  25.0 0.0 copy-done.1
  25.0 2.1 %window.1 = (f32[1048,128]{1,0:T(8,128)S(1)}, f32[1048,128]{1,0:T(8,128)S(1)}) custom-call(s32[1,1]{1,0:T(1,128)S(6)} %copy.24.row_ref, s32[1,1]{1,0:T(1,128)S(6)} %copy.25.col_ref, f32[128,128]{1,0:T(8,128)S(1)} %bitcast.9, f32[8,2,128,128]{3,2,1,0:T(8,128)S(1)} %copy-done, f32[1,1,128,128]{3,2,1,0:T(8,128)S(1)} %copy-done.1, ...), custom_call_target="tpu_custom_call" | custom-call | flops 3000000000 | bytes 4000000 | tf_op jit(solution)/shard_map/window/pallas_call | solution.py:482
  27.1 1.3 %collective-permute-start = (f32[1048,128]{1,0:T(8,128)S(1)}, f32[1048,128]{1,0:T(8,128)S(1)}, u32[]{:S(2)}, u32[]{:S(2)}) collective-permute-start(f32[1048,128]{1,0:T(8,128)S(1)} %get-tuple-element.13), channel_id=1, source_target_pairs={{0,1},{1,0},{2,3},{3,2},{4,5},{5,4},{6,7},{7,6},{8,9},{9,8},{10,11... | collective-permute-start | bytes 1609736 | tf_op jit(solution)/shard_map/ppermute | solution.py:515
  28.4 1.6 %collective-permute-done.other = f32[1048,128]{1,0:T(8,128)S(1)} collective-permute-done((f32[1048,128]{1,0:T(8,128)S(1)}, f32[1048,128]{1,0:T(8,128)S(1)}, u32[]{:S(2)}, u32[]{:S(2)}) %collective-permute-start) | collective-permute-done | bytes 536608 | tf_op jit(solution)/shard_map/ppermute | solution.py:515
  30.0 0.1 pack.1
  30.0 19.6 %all_to_all.20 = f32[32,41,1,128]{3,2,1,0:T(1,128)S(1)} all-to-all(f32[32,41,1,128]{3,2,1,0:T(1,128)S(1)} %bitcast.7), channel_id=1, replica_groups=mesh['y'=4,'xh'=2,'xl'=2,'zq'=4,'zp'=2,'core'=2] {'xl','xh','y','zp'}, dimensions={0} | all-to-all | bytes 1343488 | tf_op jit(solution)/shard_map/all_to_all | solution.py:511
  49.6 0.0 copy-start.2
  49.6 0.0 copy-start.3
  49.6 0.0 copy-start.4
  49.6 0.0 copy-start.5
  49.6 0.0 copy-start.6
  49.6 0.0 copy-start.7
  49.6 0.0 copy-start.8
  49.6 0.0 copy-start.10
  49.6 0.0 copy-start.11
  49.7 0.3 relay.1
  49.9 10.4 %all_to_all.21.received = f32[8,64,128]{2,1,0:T(8,128)S(1)} all-to-all(f32[8,64,128]{2,1,0:T(8,128)S(1)} %relay.1), channel_id=1, replica_groups=mesh['y'=4,'xh'=2,'xl'=2,'zq'=4,'zp'=2,'core'=2] {'zp','zq'}, dimensions={0} | all-to-all | bytes 524288 | tf_op jit(solution)/shard_map/all_to_all | solution.py:511
  60.4 0.0 copy-done.2
  60.4 0.0 copy-done.3
  60.4 0.0 copy-done.4
  60.4 0.0 copy-done.5
  60.4 0.0 copy-done.6
  60.4 0.0 copy-done.7
  60.4 0.0 copy-done.8
  60.4 0.0 copy-done.10
  60.4 0.0 copy-done.11
  60.5 1.6 %adjoint.1 = f32[16,96,128]{2,1,0:T(8,128)S(1)} custom-call(f32[8,64,128]{2,1,0:T(8,128)S(1)} %all_to_all.21.received, bf16[2,512,512]{2,1,0:T(8,128)(2,1)S(1)} %copy-done.2, bf16[2,512,512]{2,1,0:T(8,128)(2,1)S(1)} %copy-done.3, f32[4,2,72,256]{3,2,1,0:T(8,128)S(1)} %copy-done.4, f32[4,8,256]{2,1,0:T(8,128)S(1)} %copy-done.10, f32[16,256]{1,0:T(8,128)S(1)} %copy-done.11, ...), custom_call_target="tpu_custom_call" | custom-call | flops 3000000000 | bytes 4000000 | tf_op jit(solution)/shard_map/adjoint/pallas_call | solution.py:482
  62.1 13.1 %all_to_all.22.received = f32[16,96,128]{2,1,0:T(8,128)S(1)} all-to-all(f32[16,96,128]{2,1,0:T(8,128)S(1)} %adjoint.1), channel_id=1, replica_groups=mesh['y'=4,'xh'=2,'xl'=2,'zq'=4,'zp'=2,'core'=2] {'xl','xh','y'}, dimensions={0} | all-to-all | bytes 1572864 | tf_op jit(solution)/shard_map/all_to_all | solution.py:511
  75.2 4.8 %collective-permute-start.1 = (f32[16,64,128]{2,1,0:T(8,128)S(1)}, f32[16,64,128]{2,1,0:T(8,128)S(1)}, u32[]{:S(2)}, u32[]{:S(2)}) collective-permute-start(f32[16,64,128]{2,1,0:T(8,128)S(1)} %slice.4), channel_id=1, source_target_pairs={{0,1},{1,0},{2,3},{3,2},{4,5},{5,4},{6,7},{7,6},{8,9},{9,8},{10,11... | collective-permute-start | bytes 1572872 | tf_op jit(solution)/shard_map/ppermute | solution.py:515
  80.0 1.5 %assemble.1 = (f32[1,64,512]{2,1,0:T(8,128)}, f32[2,16,64,128]{3,2,1,0:T(8,128)}) custom-call(f32[16,96,128]{2,1,0:T(8,128)S(1)} %all_to_all.22.received), custom_call_target="tpu_custom_call" | custom-call | flops 3000000000 | bytes 4000000 | tf_op jit(solution)/shard_map/assemble/pallas_call | solution.py:482
  81.4 0.1 collective-permute-done.1
  81.5 0.8 %bitcast_dynamic-update-slice_fusion = f32[2,16,64,128]{3,2,1,0:T(8,128)} fusion(f32[2,16,64,128]{3,2,1,0:T(8,128)} %get-tuple-element.15, s32[]{:T(128)S(6)} %select_n.3, f32[16,64,128]{2,1,0:T(8,128)S(1)} %collective-permute-done.1), kind=kLoop, calls=%fused_computation | loop fusion | bytes 1048580 | tf_op jit(solution)/shard_map/dynamic_update_slice | solution.py:579
  (1 shorter events, 0.0 us)
Async XLA Ops:
  1.3 16.3 %copy-start = (f32[8,2,128,128]{3,2,1,0:T(8,128)S(1)}, f32[8,2,128,128]{3,2,1,0:T(8,128)}, u32[]{:S(2)}) copy-start(f32[8,2,128,128]{3,2,1,0:T(8,128)} %probe.3) | copy-start | bytes 3145732
  1.3 16.3 %copy-start.9 = (bf16[2,2,256,256]{3,2,1,0:T(8,128)(2,1)S(1)}, bf16[2,2,256,256]{3,2,1,0:T(8,128)(2,1)}, u32[]{:S(2)}) copy-start(bf16[2,2,256,256]{3,2,1,0:T(8,128)(2,1)} %constant.40.clone.dfts) | copy-start | bytes 1572868
  5.9 19.1 %all-to-all-start = ((f32[32,4,128]{2,1,0:T(4,128)}), f32[32,4,128]{2,1,0:T(4,128)S(1)}, u32[]{:S(2)}, u32[]{:S(2)}) async-start(f32[32,4,128]{2,1,0:T(4,128)} %bitcast.10), calls=%async_computation | async-start | bytes 131072 | tf_op jit(solution)/shard_map/all_to_all | solution.py:511
  17.6 7.4 %copy-start.1 = (f32[1,1,128,128]{3,2,1,0:T(8,128)S(1)}, f32[1,1,128,128]{3,2,1,0:T(8,128)}, u32[]{:S(2)}) copy-start(f32[1,1,128,128]{3,2,1,0:T(8,128)} %measured.1) | copy-start | bytes 196612
  27.1 2.8 %collective-permute-start = (f32[1048,128]{1,0:T(8,128)S(1)}, f32[1048,128]{1,0:T(8,128)S(1)}, u32[]{:S(2)}, u32[]{:S(2)}) collective-permute-start(f32[1048,128]{1,0:T(8,128)S(1)} %get-tuple-element.13), channel_id=1, source_target_pairs={{0,1},{1,0},{2,3},{3,2},{4,5},{5,4},{6,7},{7,6},{8,9},{9,8},{10,11... | collective-permute-start | bytes 1609736 | tf_op jit(solution)/shard_map/ppermute | solution.py:515
  49.6 10.8 %copy-start.2 = (bf16[2,512,512]{2,1,0:T(8,128)(2,1)S(1)}, bf16[2,512,512]{2,1,0:T(8,128)(2,1)}, u32[]{:S(2)}) copy-start(bf16[2,512,512]{2,1,0:T(8,128)(2,1)} %constant.38.clone.dft_t_hbm.dft_t) | copy-start | bytes 3145732
  49.6 10.8 %copy-start.3 = (bf16[2,512,512]{2,1,0:T(8,128)(2,1)S(1)}, bf16[2,512,512]{2,1,0:T(8,128)(2,1)}, u32[]{:S(2)}) copy-start(bf16[2,512,512]{2,1,0:T(8,128)(2,1)} %constant.39.clone.leaving) | copy-start | bytes 3145732
  49.6 10.8 %copy-start.4 = (f32[4,2,72,256]{3,2,1,0:T(8,128)S(1)}, f32[4,2,72,256]{3,2,1,0:T(8,128)}, u32[]{:S(2)}) copy-start(f32[4,2,72,256]{3,2,1,0:T(8,128)} %constant.42.clone.rows_tables) | copy-start | bytes 1769476
  49.6 10.8 %copy-start.5 = (bf16[2,512,256]{2,1,0:T(8,128)(2,1)S(1)}, bf16[2,512,256]{2,1,0:T(8,128)(2,1)}, u32[]{:S(2)}) copy-start(bf16[2,512,256]{2,1,0:T(8,128)(2,1)} %constant.49.clone.refs_3_) | copy-start | bytes 1572868
  49.6 10.8 %copy-start.6 = (bf16[2,512,256]{2,1,0:T(8,128)(2,1)S(1)}, bf16[2,512,256]{2,1,0:T(8,128)(2,1)}, u32[]{:S(2)}) copy-start(bf16[2,512,256]{2,1,0:T(8,128)(2,1)} %constant.48.clone.refs_2_) | copy-start | bytes 1572868
  49.6 10.8 %copy-start.7 = (bf16[2,512,256]{2,1,0:T(8,128)(2,1)S(1)}, bf16[2,512,256]{2,1,0:T(8,128)(2,1)}, u32[]{:S(2)}) copy-start(bf16[2,512,256]{2,1,0:T(8,128)(2,1)} %constant.47.clone.refs_1_) | copy-start | bytes 1572868
  49.6 10.8 %copy-start.8 = (bf16[2,512,256]{2,1,0:T(8,128)(2,1)S(1)}, bf16[2,512,256]{2,1,0:T(8,128)(2,1)}, u32[]{:S(2)}) copy-start(bf16[2,512,256]{2,1,0:T(8,128)(2,1)} %constant.46.clone.refs_0_) | copy-start | bytes 1572868
  49.6 10.8 %copy-start.10 = (f32[4,8,256]{2,1,0:T(8,128)S(1)}, f32[4,8,256]{2,1,0:T(8,128)}, u32[]{:S(2)}) copy-start(f32[4,8,256]{2,1,0:T(8,128)} %constant.44.clone.edges_hbm.edges) | copy-start | bytes 98308
  49.6 10.8 %copy-start.11 = (f32[16,256]{1,0:T(8,128)S(1)}, f32[16,256]{1,0:T(8,128)}, u32[]{:S(2)}) copy-start(f32[16,256]{1,0:T(8,128)} %constant.45.clone.middles) | copy-start | bytes 49156
  75.2 6.3 %collective-permute-start.1 = (f32[16,64,128]{2,1,0:T(8,128)S(1)}, f32[16,64,128]{2,1,0:T(8,128)S(1)}, u32[]{:S(2)}, u32[]{:S(2)}) collective-permute-start(f32[16,64,128]{2,1,0:T(8,128)S(1)} %slice.4), channel_id=1, source_target_pairs={{0,1},{1,0},{2,3},{3,2},{4,5},{5,4},{6,7},{7,6},{8,9},{9,8},{10,11... | collective-permute-start | bytes 1572872 | tf_op jit(solution)/shard_map/ppermute | solution.py:515

commit v10 on v9

--- a/solution.py
+++ b/solution.py
@@ -321,10 +321,11 @@
     first, second = keep[HALF + 16 : HALF + 17, :], other[HALF + 16 : HALF + 17, :]
     numbers = jnp.where(lane < 32, sc[0].astype(F32), jnp.where(lane < 64, first, second))
     for peer in range(32):
-        rows = slice(PART * peer, PART * (peer + 1))
+        place, zp = peer % 16, peer // 16
+        rows = slice(PART * (2 * place + zp), PART * (2 * place + zp + 1))
         at = MESSAGE * peer
         out[at : at + PART, :] = keep[rows, :] + other[rows, :]
-        rows = pl.ds(HALF + 8 * BLOCKS[peer // 2][1] + peer % 2, 4, stride=2)
+        rows = pl.ds(HALF + 8 * BLOCKS[place][1] + zp, 4, stride=2)
         out[at + PART : at + PART + 4, :] = keep[rows, :]
         out[at + PART + 4 : at + PART + 8, :] = other[rows, :]
         out[at + PART + 8 : at + MESSAGE, :] = numbers
@@ -342,7 +343,7 @@
         for shift in (1, 2, 3):
             value = jnp.where(quarter == (i + shift) % 4, rolls[shift], value)
         numbers[i] = value
-    order = [2 * rank(a, xl) + zp for a in range(ANGLES) for xl in range(2) for zp in range(2)]
+    order = [16 * zp + rank(a, xl) for a in range(ANGLES) for xl in range(2) for zp in range(2)]
     rows = jnp.concatenate([received[MESSAGE * p + PART : MESSAGE * p + PART + 8, :] for p in order], 0)
     first, second = (
         jnp.concatenate([jnp.broadcast_to(numbers[1 + i, p : p + 1, :], (8, W)) for p in order], 0)
@@ -548,7 +549,7 @@
         band_probe,
     )
     packed = vmem_call(pack_kernel, [(32 * MESSAGE, W)], [], "pack", angle_index, keep, swap(send))
-    shared = exchange(packed.reshape(32, MESSAGE, 1, W), PLANE + ("zp",)).reshape(32 * MESSAGE, W)
+    shared = exchange(packed.reshape(32, MESSAGE, 1, W), ("zp",) + PLANE).reshape(32 * MESSAGE, W)
     scratch = [pltpu.VMEM((256, W), F32), pltpu.VMEM((3, 32, W), F32)]
     relay = vmem_call(relay_kernel, [(8, PART + 32, W)], scratch, "relay", shared)
     rows = exchange(relay, Z)

time: 82.6 us -> 82.3 us (level)
  no operation moved by 1% of the time
where the time goes in v10:
time: 82.3 us; the launch traced here: 82 us
  blocking collectives  42.6 us (52%)
  starting transfers between devices  17.2 us (21%)
  Pallas kernels  11.2 us (14%)
  waiting for transfers between devices  7.28 us (9%)
  between operations  2.77 us (3%)
  local copies, waits for them, and re-layouts  0.94 us (1%)
    all_to_all x3, blocking collectives, exchange(): return lax.all_to_all(blocks, axes, split_axis=0, concat_axis=0, tiled=True)  42.6 us
    all_to_all x1, starting transfers between devices, exchange(): return lax.all_to_all(blocks, axes, split_axis=0, concat_axis=0, tiled=True)  11.1 us
    pallas_call x6, Pallas kernels, vmem_call(): pl.pallas_call(kernel, in_specs=[pl.BlockSpec(memory_space=pltpu.SMEM if...  6.61 us
    ppermute x2, starting transfers between devices, swap(): return lax.ppermute(rows, 'core', [(0, 1), (1, 0)])  6.16 us
    all_to_all x1, waiting for transfers between devices, exchange(): return lax.all_to_all(blocks, axes, split_axis=0, concat_axis=0, tiled=True)  5.65 us
    pallas_call x1, Pallas kernels, forward_call(): pl.pallas_call(forward_kernel, in_specs=[pl.BlockSpec(memory_space=pltpu....  4.56 us
  transfers between devices with their start and end apart: 3, of which 3 were waited for; matrix products, arithmetic and copies ran while one was open for 0% of the time, Pallas kernels for 3%

profile of v10, /device:TPU:1, one launch (start us, length us, event | category | flops | bytes accessed | tf_op | source)
XLA Modules:
  0.0 82.0 jit_solution(7830262993884523542)
XLA Ops:
  1.3 0.0 copy-start
  1.3 0.0 copy-start.9
  1.3 4.6 %forward.1 = f32[128,128]{1,0:T(8,128)} custom-call(s32[1]{0:T(128)S(6)} %copy.23.sc, bf16[1,512,512]{2,1,0:T(8,128)(2,1)} %volume.1, bf16[2,512,512]{2,1,0:T(8,128)(2,1)} %constant.37.clone.dft_hbm, bf16[2,512,512]{2,1,0:T(8,128)(2,1)} %constant.38.clone.dft_t_hbm.dft_t, f32[8,88,512]{2,1,0:T(8,128)} %constant.41.clone.factors_hbm, ...), custom_call_target="tpu_custom_call" | custom-call | flops 4000000000 | bytes 4000000 | tf_op jit(solution)/shard_map/forward/pallas_call | solution.py:459
  5.9 11.1 %all-to-all-start = ((f32[32,4,128]{2,1,0:T(4,128)}), f32[32,4,128]{2,1,0:T(4,128)S(1)}, u32[]{:S(2)}, u32[]{:S(2)}) async-start(f32[32,4,128]{2,1,0:T(4,128)} %bitcast.10), calls=%async_computation | async-start | bytes 131072 | tf_op jit(solution)/shard_map/all_to_all | solution.py:512
  17.6 0.0 copy-done
  17.6 0.0 copy-done.9
  17.6 0.0 copy-start.1
  17.6 1.1 %prepare.1 = (f32[4,256,256]{2,1,0:T(8,128)S(1)}, bf16[256,256]{1,0:T(8,128)(2,1)S(1)}, f32[8,2,32,128]{3,2,1,0:T(8,128)S(1)}) custom-call(s32[1,1]{1,0:T(1,128)S(6)} %copy.24.row_ref, f32[8,2,128,128]{3,2,1,0:T(8,128)S(1)} %copy-done, bf16[2,2,256,256]{3,2,1,0:T(8,128)(2,1)S(1)} %copy-done.9), custom_call_target="tpu_custom_call" | custom-call | flops 3000000000 | bytes 4000000 | tf_op jit(solution)/shard_map/prepare/pallas_call | solution.py:483
  19.4 5.7 %all-to-all-done = f32[32,4,128]{2,1,0:T(4,128)S(1)} async-done(((f32[32,4,128]{2,1,0:T(4,128)}), f32[32,4,128]{2,1,0:T(4,128)S(1)}, u32[]{:S(2)}, u32[]{:S(2)}) %all-to-all-start) | async-done | bytes 65568 | tf_op jit(solution)/shard_map/all_to_all | solution.py:512
  25.0 0.0 copy-done.1
  25.0 2.1 %window.1 = (f32[1048,128]{1,0:T(8,128)S(1)}, f32[1048,128]{1,0:T(8,128)S(1)}) custom-call(s32[1,1]{1,0:T(1,128)S(6)} %copy.24.row_ref, s32[1,1]{1,0:T(1,128)S(6)} %copy.25.col_ref, f32[128,128]{1,0:T(8,128)S(1)} %bitcast.9, f32[8,2,128,128]{3,2,1,0:T(8,128)S(1)} %copy-done, f32[1,1,128,128]{3,2,1,0:T(8,128)S(1)} %copy-done.1, ...), custom_call_target="tpu_custom_call" | custom-call | flops 3000000000 | bytes 4000000 | tf_op jit(solution)/shard_map/window/pallas_call | solution.py:483
  27.1 1.3 %collective-permute-start = (f32[1048,128]{1,0:T(8,128)S(1)}, f32[1048,128]{1,0:T(8,128)S(1)}, u32[]{:S(2)}, u32[]{:S(2)}) collective-permute-start(f32[1048,128]{1,0:T(8,128)S(1)} %get-tuple-element.13), channel_id=1, source_target_pairs={{0,1},{1,0},{2,3},{3,2},{4,5},{5,4},{6,7},{7,6},{8,9},{9,8},{10,11... | collective-permute-start | bytes 1609736 | tf_op jit(solution)/shard_map/ppermute | solution.py:516
  28.4 1.6 %collective-permute-done.other = f32[1048,128]{1,0:T(8,128)S(1)} collective-permute-done((f32[1048,128]{1,0:T(8,128)S(1)}, f32[1048,128]{1,0:T(8,128)S(1)}, u32[]{:S(2)}, u32[]{:S(2)}) %collective-permute-start) | collective-permute-done | bytes 536608 | tf_op jit(solution)/shard_map/ppermute | solution.py:516
  30.0 0.1 pack.1
  30.0 17.9 %all_to_all.20 = f32[32,41,1,128]{3,2,1,0:T(1,128)S(1)} all-to-all(f32[32,41,1,128]{3,2,1,0:T(1,128)S(1)} %bitcast.7), channel_id=1, replica_groups=mesh['y'=4,'xh'=2,'xl'=2,'zq'=4,'zp'=2,'core'=2] {'zp','xl','xh','y'}, dimensions={0} | all-to-all | bytes 1343488 | tf_op jit(solution)/shard_map/all_to_all | solution.py:512
  47.9 0.0 copy-start.2
  47.9 0.0 copy-start.3
  47.9 0.0 copy-start.4
  47.9 0.0 copy-start.5
  47.9 0.0 copy-start.6
  47.9 0.0 copy-start.7
  47.9 0.0 copy-start.8
  48.0 0.0 copy-start.10
  48.0 0.0 copy-start.11
  48.0 0.3 relay.1
  48.3 10.8 %all_to_all.21.received = f32[8,64,128]{2,1,0:T(8,128)S(1)} all-to-all(f32[8,64,128]{2,1,0:T(8,128)S(1)} %relay.1), channel_id=1, replica_groups=mesh['y'=4,'xh'=2,'xl'=2,'zq'=4,'zp'=2,'core'=2] {'zp','zq'}, dimensions={0} | all-to-all | bytes 524288 | tf_op jit(solution)/shard_map/all_to_all | solution.py:512
  59.0 0.0 copy-done.2
  59.0 0.0 copy-done.3
  59.0 0.0 copy-done.4
  59.0 0.0 copy-done.5
  59.0 0.0 copy-done.6
  59.1 0.0 copy-done.7
  59.1 0.0 copy-done.8
  59.1 0.0 copy-done.10
  59.1 0.0 copy-done.11
  59.1 1.6 %adjoint.1 = f32[16,96,128]{2,1,0:T(8,128)S(1)} custom-call(f32[8,64,128]{2,1,0:T(8,128)S(1)} %all_to_all.21.received, bf16[2,512,512]{2,1,0:T(8,128)(2,1)S(1)} %copy-done.2, bf16[2,512,512]{2,1,0:T(8,128)(2,1)S(1)} %copy-done.3, f32[4,2,72,256]{3,2,1,0:T(8,128)S(1)} %copy-done.4, f32[4,8,256]{2,1,0:T(8,128)S(1)} %copy-done.10, f32[16,256]{1,0:T(8,128)S(1)} %copy-done.11, ...), custom_call_target="tpu_custom_call" | custom-call | flops 3000000000 | bytes 4000000 | tf_op jit(solution)/shard_map/adjoint/pallas_call | solution.py:483
  60.7 14.0 %all_to_all.22.received = f32[16,96,128]{2,1,0:T(8,128)S(1)} all-to-all(f32[16,96,128]{2,1,0:T(8,128)S(1)} %adjoint.1), channel_id=1, replica_groups=mesh['y'=4,'xh'=2,'xl'=2,'zq'=4,'zp'=2,'core'=2] {'xl','xh','y'}, dimensions={0} | all-to-all | bytes 1572864 | tf_op jit(solution)/shard_map/all_to_all | solution.py:512
  74.8 4.9 %collective-permute-start.1 = (f32[16,64,128]{2,1,0:T(8,128)S(1)}, f32[16,64,128]{2,1,0:T(8,128)S(1)}, u32[]{:S(2)}, u32[]{:S(2)}) collective-permute-start(f32[16,64,128]{2,1,0:T(8,128)S(1)} %slice.4), channel_id=1, source_target_pairs={{0,1},{1,0},{2,3},{3,2},{4,5},{5,4},{6,7},{7,6},{8,9},{9,8},{10,11... | collective-permute-start | bytes 1572872 | tf_op jit(solution)/shard_map/ppermute | solution.py:516
  79.6 1.5 %assemble.1 = (f32[1,64,512]{2,1,0:T(8,128)}, f32[2,16,64,128]{3,2,1,0:T(8,128)}) custom-call(f32[16,96,128]{2,1,0:T(8,128)S(1)} %all_to_all.22.received), custom_call_target="tpu_custom_call" | custom-call | flops 3000000000 | bytes 4000000 | tf_op jit(solution)/shard_map/assemble/pallas_call | solution.py:483
  81.1 0.1 collective-permute-done.1
  81.2 0.8 %bitcast_dynamic-update-slice_fusion = f32[2,16,64,128]{3,2,1,0:T(8,128)} fusion(f32[2,16,64,128]{3,2,1,0:T(8,128)} %get-tuple-element.15, s32[]{:T(128)S(6)} %select_n.3, f32[16,64,128]{2,1,0:T(8,128)S(1)} %collective-permute-done.1), kind=kLoop, calls=%fused_computation | loop fusion | bytes 1048580 | tf_op jit(solution)/shard_map/dynamic_update_slice | solution.py:580
  (1 shorter events, 0.0 us)
Async XLA Ops:
  1.3 16.3 %copy-start = (f32[8,2,128,128]{3,2,1,0:T(8,128)S(1)}, f32[8,2,128,128]{3,2,1,0:T(8,128)}, u32[]{:S(2)}) copy-start(f32[8,2,128,128]{3,2,1,0:T(8,128)} %probe.3) | copy-start | bytes 3145732
  1.3 16.3 %copy-start.9 = (bf16[2,2,256,256]{3,2,1,0:T(8,128)(2,1)S(1)}, bf16[2,2,256,256]{3,2,1,0:T(8,128)(2,1)}, u32[]{:S(2)}) copy-start(bf16[2,2,256,256]{3,2,1,0:T(8,128)(2,1)} %constant.40.clone.dfts) | copy-start | bytes 1572868
  5.9 19.1 %all-to-all-start = ((f32[32,4,128]{2,1,0:T(4,128)}), f32[32,4,128]{2,1,0:T(4,128)S(1)}, u32[]{:S(2)}, u32[]{:S(2)}) async-start(f32[32,4,128]{2,1,0:T(4,128)} %bitcast.10), calls=%async_computation | async-start | bytes 131072 | tf_op jit(solution)/shard_map/all_to_all | solution.py:512
  17.6 7.4 %copy-start.1 = (f32[1,1,128,128]{3,2,1,0:T(8,128)S(1)}, f32[1,1,128,128]{3,2,1,0:T(8,128)}, u32[]{:S(2)}) copy-start(f32[1,1,128,128]{3,2,1,0:T(8,128)} %measured.1) | copy-start | bytes 196612
  27.1 2.8 %collective-permute-start = (f32[1048,128]{1,0:T(8,128)S(1)}, f32[1048,128]{1,0:T(8,128)S(1)}, u32[]{:S(2)}, u32[]{:S(2)}) collective-permute-start(f32[1048,128]{1,0:T(8,128)S(1)} %get-tuple-element.13), channel_id=1, source_target_pairs={{0,1},{1,0},{2,3},{3,2},{4,5},{5,4},{6,7},{7,6},{8,9},{9,8},{10,11... | collective-permute-start | bytes 1609736 | tf_op jit(solution)/shard_map/ppermute | solution.py:516
  47.9 11.1 %copy-start.2 = (bf16[2,512,512]{2,1,0:T(8,128)(2,1)S(1)}, bf16[2,512,512]{2,1,0:T(8,128)(2,1)}, u32[]{:S(2)}) copy-start(bf16[2,512,512]{2,1,0:T(8,128)(2,1)} %constant.38.clone.dft_t_hbm.dft_t) | copy-start | bytes 3145732
  47.9 11.1 %copy-start.3 = (bf16[2,512,512]{2,1,0:T(8,128)(2,1)S(1)}, bf16[2,512,512]{2,1,0:T(8,128)(2,1)}, u32[]{:S(2)}) copy-start(bf16[2,512,512]{2,1,0:T(8,128)(2,1)} %constant.39.clone.leaving) | copy-start | bytes 3145732
  47.9 11.1 %copy-start.4 = (f32[4,2,72,256]{3,2,1,0:T(8,128)S(1)}, f32[4,2,72,256]{3,2,1,0:T(8,128)}, u32[]{:S(2)}) copy-start(f32[4,2,72,256]{3,2,1,0:T(8,128)} %constant.42.clone.rows_tables) | copy-start | bytes 1769476
  47.9 11.1 %copy-start.5 = (bf16[2,512,256]{2,1,0:T(8,128)(2,1)S(1)}, bf16[2,512,256]{2,1,0:T(8,128)(2,1)}, u32[]{:S(2)}) copy-start(bf16[2,512,256]{2,1,0:T(8,128)(2,1)} %constant.49.clone.refs_3_) | copy-start | bytes 1572868
  47.9 11.1 %copy-start.6 = (bf16[2,512,256]{2,1,0:T(8,128)(2,1)S(1)}, bf16[2,512,256]{2,1,0:T(8,128)(2,1)}, u32[]{:S(2)}) copy-start(bf16[2,512,256]{2,1,0:T(8,128)(2,1)} %constant.48.clone.refs_2_) | copy-start | bytes 1572868
  47.9 11.1 %copy-start.7 = (bf16[2,512,256]{2,1,0:T(8,128)(2,1)S(1)}, bf16[2,512,256]{2,1,0:T(8,128)(2,1)}, u32[]{:S(2)}) copy-start(bf16[2,512,256]{2,1,0:T(8,128)(2,1)} %constant.47.clone.refs_1_) | copy-start | bytes 1572868
  47.9 11.1 %copy-start.8 = (bf16[2,512,256]{2,1,0:T(8,128)(2,1)S(1)}, bf16[2,512,256]{2,1,0:T(8,128)(2,1)}, u32[]{:S(2)}) copy-start(bf16[2,512,256]{2,1,0:T(8,128)(2,1)} %constant.46.clone.refs_0_) | copy-start | bytes 1572868
  48.0 11.1 %copy-start.10 = (f32[4,8,256]{2,1,0:T(8,128)S(1)}, f32[4,8,256]{2,1,0:T(8,128)}, u32[]{:S(2)}) copy-start(f32[4,8,256]{2,1,0:T(8,128)} %constant.44.clone.edges_hbm.edges) | copy-start | bytes 98308
  48.0 11.1 %copy-start.11 = (f32[16,256]{1,0:T(8,128)S(1)}, f32[16,256]{1,0:T(8,128)}, u32[]{:S(2)}) copy-start(f32[16,256]{1,0:T(8,128)} %constant.45.clone.middles) | copy-start | bytes 49156
  74.8 6.4 %collective-permute-start.1 = (f32[16,64,128]{2,1,0:T(8,128)S(1)}, f32[16,64,128]{2,1,0:T(8,128)S(1)}, u32[]{:S(2)}, u32[]{:S(2)}) collective-permute-start(f32[16,64,128]{2,1,0:T(8,128)S(1)} %slice.4), channel_id=1, source_target_pairs={{0,1},{1,0},{2,3},{3,2},{4,5},{5,4},{6,7},{7,6},{8,9},{9,8},{10,11... | collective-permute-start | bytes 1572872 | tf_op jit(solution)/shard_map/ppermute | solution.py:516
